TPU v7x, 128 devices: a whole 4x4x4 slice. The times are simulated.
128 devices in a mesh: dp: 16 (over z, x), table: 8 (over y, core).
Axes of the slice: x: 4, y: 4, z: 4, core: 2. Of those that a mesh axis runs over, the one named last changes fastest.
Arguments:
- table: bfloat16 [524288, 512], P(('dp', 'table')), may hold values from -6 to 6
- w_in: bfloat16 [512, 2048], replicated, may hold values from -0.25 to 0.25
- w_out: bfloat16 [512, 512], replicated, may hold values from -0.25 to 0.25
- item_owner: int32 [3, 32768, 1], P(None, ('dp', 'table')), may hold values from 0 to 127; in each aligned block of 256 rows (0 to 255, 256 to 511, ..., all dimensions but the last counted through in order) at most 4 rows name the same one
- item_slot: int32 [3, 32768], P(None, ('dp', 'table')), may hold values from 0 to 4095
- seq_lengths: int32 [3, 128, 4], P(None, ('dp', 'table')), may hold values from 1 to 128, 256 in all within a row
- cotangent: bfloat16 [3, 32768, 512], P(None, ('dp', 'table')), may hold values from -6 to 6
Outputs:
- layer_out: bfloat16 [3, 32768, 512], P(None, ('dp', 'table'))
- table_grad: float32 [524288, 512], P(('dp', 'table'))
- w_in_grad: float32 [512, 2048], replicated
- w_out_grad: float32 [512, 512], replicated
Inputs may be any that keep to these rules, and one draw needn't show every extreme that they name: `item_owner`: in every micro-batch, no owner is named by more than 4 of one device's 256 positions; some owner is named exactly 4 times. `seq_lengths`: each device's 4 lengths in a micro-batch sum to 256; the longest is 128.
All inputs are finite; a program needn't handle non-finite values.
Results may differ from a plain program's by a relative error of at most 0.019.
Values may be sent and summed in bfloat16 or wider, within the bound.
No kernel may reach another device: no remote copies, remote signals or barrier semaphores. Data moves between devices by JAX's collectives and lax.ppermute only.
A program may use at most 128 MiB of HBM per device.

v0:
```python
import functools

import jax
import jax.numpy as jnp
from jax import lax
from jax.experimental import pallas as pl
from jax.experimental.pallas import tpu as pltpu
from jax.sharding import PartitionSpec as P

HEADS = 8
MB = 3
CAP = 4
AXES = ("dp", "table")
F32 = jnp.float32
BF16 = jnp.bfloat16
I32 = jnp.int32
VMEM = pl.BlockSpec(memory_space=pltpu.VMEM)
SMEM = pl.BlockSpec(memory_space=pltpu.SMEM)


def iota(shape, dim):
    return lax.broadcasted_iota(I32, shape, dim)


def mm(a, b):
    return jnp.dot(a, b, preferred_element_type=F32)


def mm_nt(a, b):
    return lax.dot_general(a, b, (((1,), (1,)), ((), ())), preferred_element_type=F32)


def mm_tn(a, b):
    return lax.dot_general(a, b, (((0,), (0,)), ((), ())), preferred_element_type=F32)


def params(**more):
    return pltpu.CompilerParams(vmem_limit_bytes=48 * 1024 * 1024, **more)


def cost(flops, bytes_accessed):
    return pl.CostEstimate(flops=flops, bytes_accessed=bytes_accessed, transcendentals=0)


def request_kernel(owner_ref, slot_ref, wanted_ref, flat_ref):
    length = owner_ref.shape[1]
    owners_n = wanted_ref.shape[0]
    upto = (iota((length, length), 0) <= iota((length, length), 1)).astype(BF16)
    lane_row = iota((128, length), 0)
    high = jnp.zeros((owners_n, 128), F32)
    low = jnp.zeros((owners_n, 128), F32)
    live = jnp.zeros((owners_n, 128), F32)
    flat_ref[...] = jnp.zeros(flat_ref.shape, I32)
    for micro in range(MB):
        owner = owner_ref[micro : micro + 1, :]
        slot = slot_ref[micro : micro + 1, :]
        hot = (iota((owners_n, length), 0) == owner).astype(F32)
        hot_bf = hot.astype(BF16)
        counts = mm(hot_bf, upto)
        rank = (jnp.sum(counts * hot, axis=0, keepdims=True) - 1.0).astype(I32)
        flat_ref[micro : micro + 1, :] = owner * 8 + rank
        here = lane_row == rank + CAP * micro
        high = high + mm_nt(hot_bf, jnp.where(here, (slot >> 6).astype(F32), 0.0).astype(BF16))
        low = low + mm_nt(hot_bf, jnp.where(here, (slot & 63).astype(F32), 0.0).astype(BF16))
        live = live + mm_nt(hot_bf, jnp.where(here, 1.0, 0.0).astype(BF16))
    wanted_ref[...] = jnp.where(live > 0.5, high * 64.0 + low, -1.0).astype(I32)


def requests(owner, slot, owners_n):
    return pl.pallas_call(
        request_kernel,
        out_shape=(
            jax.ShapeDtypeStruct((owners_n, 128), I32),
            jax.ShapeDtypeStruct((8, owner.shape[1]), I32),
        ),
        in_specs=[VMEM, VMEM],
        out_specs=(VMEM, VMEM),
        compiler_params=params(),
        name="requests",
    )(owner, slot)


def gather_kernel(asked_ref, table_ref, out_ref, column_ref, sum_ref, *, first, width, steps):
    step = pl.program_id(0)
    rows = sum_ref.shape[0]
    block = table_ref.shape[0]

    @pl.when(step == 0)
    def _():
        asked = asked_ref[...]
        devices = asked.shape[0]
        spread = (iota((rows, devices), 0) // width == iota((rows, devices), 1)).astype(BF16)
        high = mm(spread, (asked >> 6).astype(F32).astype(BF16))
        low = mm(spread, (asked & 63).astype(F32).astype(BF16))
        mine = iota((rows, 128), 1) == iota((rows, 128), 0) % width + first
        column = jnp.sum(jnp.where(mine, high * 64.0 + low, 0.0), axis=1, keepdims=True)
        column_ref[...] = jnp.broadcast_to(column.astype(I32), column_ref.shape)

    column = column_ref[...][:, :1] - step * block
    hot = jnp.where(column == iota((rows, block), 1), 1.0, 0.0).astype(BF16)
    part = mm(hot, table_ref[...])

    @pl.when(step == 0)
    def _():
        sum_ref[...] = part

    @pl.when(step > 0)
    def _():
        sum_ref[...] += part

    @pl.when(step == steps - 1)
    def _():
        if width == 8:
            out_ref[...] = sum_ref[...].astype(BF16)
        else:
            whole = sum_ref[...].reshape(rows // 8, 8, sum_ref.shape[1])
            half = whole.shape[2] // 2
            left, right = whole[:, :, :half], whole[:, :, half:]
            top = iota(left.shape, 1) < 4
            even = jnp.where(top, left, pltpu.roll(right, 4, 1))
            odd = jnp.where(top, pltpu.roll(left, 4, 1), right)
            both = jnp.concatenate([even, odd], axis=1)
            out_ref[...] = both.reshape(out_ref.shape).astype(BF16)


def gather(asked, table, first, width):
    own_rows, columns = table.shape
    devices = asked.shape[0]
    steps = 4
    rows = devices * width
    out = (devices * 8, columns if width == 8 else columns // 2)
    return pl.pallas_call(
        functools.partial(gather_kernel, first=first, width=width, steps=steps),
        out_shape=jax.ShapeDtypeStruct(out, BF16),
        grid=(steps,),
        in_specs=[
            pl.BlockSpec((devices, 128), lambda i: (0, 0)),
            pl.BlockSpec((own_rows // steps, columns), lambda i: (i, 0)),
        ],
        out_specs=pl.BlockSpec(out, lambda i: (0, 0)),
        scratch_shapes=[pltpu.VMEM((rows, 128), I32), pltpu.VMEM((rows, columns), F32)],
        compiler_params=params(),
        cost_estimate=cost(2 * rows * own_rows * columns, 6 * 1024 * 1024),
        name=f"gather{width}",
    )(asked, table)


def column_of(row, copies=128):
    return jnp.transpose(jnp.broadcast_to(row.astype(F32), (copies, row.shape[1])))


def layer_kernel(
    lengths_ref,
    flat_ref,
    rows_ref,
    w_in_ref,
    w_out_ref,
    cot_ref,
    *rest,
    micro,
):
    out_ref, grad_ref, emb_t_ref, dpre_ref, gated_t_ref, hidden_ref, slope_ref, weight_ref, dsilu_ref, att_ref, datt_ref = (
        rest[-11:]
    )
    length, width = grad_ref.shape
    slots = rows_ref.shape[0]
    column = column_of(flat_ref[micro : micro + 1, :])

    def placing(shift):
        lanes = iota((length, 128), 1).astype(F32)
        parts = [
            jnp.where(column == lanes + float(first - shift), 1.0, 0.0).astype(BF16)
            for first in range(0, slots, 128)
        ]
        return jnp.concatenate(parts, axis=1)

    if micro == 0:
        rows = rows_ref[...]
        embedded = jnp.concatenate([mm(placing(0), rows), mm(placing(4), rows)], axis=1)
    else:
        embedded = mm(placing(4 * (micro - 1)), rows_ref[...])
    emb_t_ref[...] = jnp.transpose(embedded).astype(BF16)
    emb = embedded.astype(BF16)

    chunk = 512
    for first in range(0, 4 * width, chunk):
        at = slice(first, first + chunk)
        half = mm(emb, w_in_ref[:, at]) * 0.5
        tanh = jnp.tanh(half)
        act = half + half * tanh
        hidden_ref[:, at] = act.astype(BF16)
        slope_ref[:, at] = (0.5 * ((1.0 + tanh) + act * (1.0 - tanh))).astype(BF16)

    ends = []
    total = 0
    for which in range(3):
        total = total + lengths_ref[micro, 0, which]
        ends.append(total)

    def segment(places):
        return sum((places >= end).astype(I32) for end in ends)

    query_at = iota((length, length), 0)
    key_at = iota((length, length), 1)
    allowed = (segment(query_at) == segment(key_at)) & (key_at <= query_at)

    lane = iota((1, 128), 1)
    first_head = (lane < 64).astype(F32)
    second_head = 1.0 - first_head
    masks = (first_head.astype(BF16), second_head.astype(BF16))
    score_masks = ((first_head * 0.0625).astype(BF16), (second_head * 0.0625).astype(BF16))
    pairs = HEADS // 2
    for pair in range(pairs):
        lanes = slice(128 * pair, 128 * pair + 128)
        value = hidden_ref[:, width + 128 * pair : width + 128 * pair + 128]
        query = hidden_ref[:, 2 * width + 128 * pair : 2 * width + 128 * pair + 128]
        key = hidden_ref[:, 3 * width + 128 * pair : 3 * width + 128 * pair + 128]
        for head in range(2):
            half = mm_nt(query * score_masks[head], key)
            tanh = jnp.tanh(half)
            act = half + half * tanh
            at = slice(length * head, length * head + length)
            weight_ref[pair, :, at] = jnp.where(allowed, act, 0.0).astype(BF16)
            dsilu_ref[pair, :, at] = jnp.where(
                allowed, (1.0 + tanh) + act * (1.0 - tanh), 0.0
            ).astype(BF16)
        both = jnp.concatenate([value * masks[0], value * masks[1]], axis=0)
        att_ref[:, lanes] = mm(weight_ref[pair], both)

    attended = att_ref[...]
    centred = attended - jnp.mean(attended, axis=1, keepdims=True)
    inverse = lax.rsqrt(jnp.mean(centred * centred, axis=1, keepdims=True) + 1e-05)
    normed = centred * inverse
    gate = hidden_ref[:, :width].astype(F32)
    gated = normed * gate
    gated_t_ref[...] = jnp.transpose(gated).astype(BF16)
    cot = cot_ref[0]
    out_ref[0] = (embedded + mm(gated.astype(BF16), w_out_ref[...])).astype(BF16)

    dgated = mm_nt(cot, w_out_ref[...])
    dgate = dgated * normed
    dnormed = dgated * gate
    dpre_ref[:, :width] = (dgate * slope_ref[:, :width].astype(F32)).astype(BF16)
    shared = jnp.mean(dnormed * normed, axis=1, keepdims=True)
    dcentred = inverse * (dnormed - normed * shared)
    datt = dcentred - jnp.mean(dcentred, axis=1, keepdims=True)
    datt_ref[...] = datt.astype(BF16)

    for pair in range(pairs):
        at_value = slice(width + 128 * pair, width + 128 * pair + 128)
        at_query = slice(2 * width + 128 * pair, 2 * width + 128 * pair + 128)
        at_key = slice(3 * width + 128 * pair, 3 * width + 128 * pair + 128)
        value = hidden_ref[:, at_value]
        query = hidden_ref[:, at_query]
        key = hidden_ref[:, at_key]
        dhead = datt_ref[:, 128 * pair : 128 * pair + 128]
        parts = []
        for head in range(2):
            at = slice(length * head, length * head + length)
            dweight = mm_nt(dhead * masks[head], value)
            parts.append((dweight * dsilu_ref[pair, :, at].astype(F32)).astype(BF16))
        dscore = jnp.concatenate(parts, axis=1)
        both_keys = jnp.concatenate([key * score_masks[0], key * score_masks[1]], axis=0)
        dquery = mm(dscore, both_keys)
        dkeys = mm_tn(dscore, query * jnp.asarray(0.0625, BF16))
        dkey = jnp.where(lane < 64, dkeys[:length], dkeys[length:])
        dvalues = mm_tn(weight_ref[pair], dhead)
        dvalue = jnp.where(lane < 64, dvalues[:length], dvalues[length:])
        for at, grad in ((at_value, dvalue), (at_query, dquery), (at_key, dkey)):
            dpre_ref[:, at] = (grad * slope_ref[:, at].astype(F32)).astype(BF16)

    grad_ref[...] = (cot.astype(F32) + mm_nt(dpre_ref[...], w_in_ref[...])).astype(BF16)


def layer(lengths, flat, rows, w_in, w_out, cotangent, outputs, micro):
    width = w_in.shape[0]
    length = cotangent.shape[1]
    pairs = HEADS // 2
    block = pl.BlockSpec((1, length, width), lambda i: (micro, 0, 0))

    def whole(shape):
        return pl.BlockSpec(shape, lambda i: (0,) * len(shape))

    operands = [lengths, flat, rows, w_in, w_out, cotangent]
    in_specs = [SMEM, whole(flat.shape), whole(rows.shape), whole(w_in.shape), whole(w_out.shape), block]
    alias = {}
    if outputs is not None:
        alias = {len(operands): 0}
        operands.append(outputs)
        in_specs.append(pl.BlockSpec(memory_space=pl.ANY))
    return pl.pallas_call(
        functools.partial(layer_kernel, micro=micro),
        out_shape=(
            jax.ShapeDtypeStruct(cotangent.shape, BF16),
            jax.ShapeDtypeStruct((length, width), BF16),
            jax.ShapeDtypeStruct((width, length), BF16),
            jax.ShapeDtypeStruct((length, 4 * width), BF16),
            jax.ShapeDtypeStruct((width, length), BF16),
        ),
        grid=(1,),
        in_specs=in_specs,
        out_specs=(
            block,
            whole((length, width)),
            whole((width, length)),
            whole((length, 4 * width)),
            whole((width, length)),
        ),
        scratch_shapes=[
            pltpu.VMEM((length, 4 * width), BF16),
            pltpu.VMEM((length, 4 * width), BF16),
            pltpu.VMEM((pairs, length, 2 * length), BF16),
            pltpu.VMEM((pairs, length, 2 * length), BF16),
            pltpu.VMEM((length, width), F32),
            pltpu.VMEM((length, width), BF16),
        ],
        input_output_aliases=alias,
        compiler_params=params(),
        cost_estimate=cost(8_000_000_000, 6 * 1024 * 1024),
        name=f"layer{micro}",
    )(*operands)


def send_pair_kernel(flat_ref, first_ref, second_ref, out_ref):
    slots = out_ref.shape[0]
    length = first_ref.shape[0]
    places = iota((slots, length), 0)
    one = jnp.where(places == flat_ref[0:1, :], 1.0, 0.0).astype(BF16)
    two = jnp.where(places == flat_ref[1:2, :] + 4, 1.0, 0.0).astype(BF16)
    placing = jnp.concatenate([one, two], axis=1)
    grads = jnp.concatenate([first_ref[...], second_ref[...]], axis=0)
    out_ref[...] = mm(placing, grads).astype(BF16)


def send_pair(flat, first, second, slots):
    return pl.pallas_call(
        send_pair_kernel,
        out_shape=jax.ShapeDtypeStruct((slots, first.shape[1]), BF16),
        in_specs=[VMEM] * 3,
        out_specs=VMEM,
        compiler_params=params(),
        cost_estimate=cost(1_000_000_000, 2 * 1024 * 1024),
        name="send_pair",
    )(flat, first, second)


def weights_kernel(core_ref, *refs):
    embs, dpres, gateds, cots, out_ref = refs[0:3], refs[3:6], refs[6:9], refs[9], refs[10]
    width4 = dpres[0].shape[1]
    left = jnp.concatenate([ref[...] for ref in embs], axis=1)
    groups, _, columns = out_ref.shape[1:]
    right_out = jnp.concatenate([cots[m] for m in range(MB)], axis=0)
    left_out = jnp.concatenate([ref[...] for ref in gateds], axis=1)
    tail = mm(left_out, right_out).astype(BF16)
    for group in range(groups):
        first = group * columns
        last = min(first + columns, width4)
        right = jnp.concatenate([ref[:, first:last] for ref in dpres], axis=0)
        out_ref[0, group, :, : last - first] = mm(left, right).astype(BF16)
    kept = width4 - (groups - 1) * columns
    out_ref[0, groups - 1, :, kept:] = tail


def weight_grads(core, embs, dpres, gateds, cotangent):
    width, length = embs[0].shape
    width4 = dpres[0].shape[1]
    half = width // 2
    columns = (width4 + width) // 4
    split = pl.BlockSpec((half, length), lambda i, core: ((core[0] + i) % 2, 0))

    def whole(shape):
        return pl.BlockSpec(shape, lambda i, core: (0,) * len(shape))

    return pl.pallas_call(
        weights_kernel,
        out_shape=jax.ShapeDtypeStruct((2, 4, half, columns), BF16),
        grid_spec=pltpu.PrefetchScalarGridSpec(
            num_scalar_prefetch=1,
            grid=(2,),
            in_specs=[split] * 3 + [whole((length, width4))] * 3 + [split] * 3 + [whole(cotangent.shape)],
            out_specs=pl.BlockSpec((1, 4, half, columns), lambda i, core: (i, 0, 0, 0)),
        ),
        compiler_params=params(),
        cost_estimate=cost(2 * 768 * 512 * 2560, 8 * 1024 * 1024),
        name="weight_grads",
    )(core, *embs, *dpres, *gateds, cotangent)


def message_kernel(flat_ref, grad_ref, mine_ref, other_ref, out_ref):
    slots = out_ref.shape[0]
    length, width = grad_ref.shape
    half = width // 2
    places = iota((slots, length), 0)
    one = jnp.where(places == flat_ref[2:3, :], 1.0, 0.0).astype(BF16)
    two = jnp.where(places == flat_ref[2:3, :] + 4, 1.0, 0.0).astype(BF16)
    placing = jnp.concatenate([one, two], axis=1)
    grads = jnp.concatenate([grad_ref[:, :half], grad_ref[:, half:]], axis=0)
    out_ref[:, :half] = mm(placing, grads).astype(BF16)
    out_ref[:, half:] = (mine_ref[0].astype(F32) + other_ref[...].astype(F32)).astype(BF16)


def message(flat, grad, mine, other):
    slots, columns = other.shape
    width = grad.shape[1] // 2 + columns
    return pl.pallas_call(
        message_kernel,
        out_shape=jax.ShapeDtypeStruct((slots, width), BF16),
        grid=(1,),
        in_specs=[
            pl.BlockSpec(flat.shape, lambda i: (0, 0)),
            pl.BlockSpec(grad.shape, lambda i: (0, 0)),
            pl.BlockSpec((1, slots, columns), lambda i: (0, 0, 0)),
            pl.BlockSpec((slots, columns), lambda i: (0, 0)),
        ],
        out_specs=pl.BlockSpec((slots, width), lambda i: (0, 0)),
        compiler_params=params(),
        cost_estimate=cost(500_000_000, 6 * 1024 * 1024),
        name="message",
    )(flat, grad, mine, other)


def shard_sum_kernel(in_ref, out_ref, *, skip, factor):
    slots = in_ref.shape[0]
    parts = in_ref[:, skip:].astype(F32).reshape(slots // 16, 16, in_ref.shape[1] - skip)
    summed = (jnp.sum(parts, axis=0) * factor).astype(BF16)
    out_ref[...] = jnp.broadcast_to(summed[None], (slots // 16, *summed.shape)).reshape(out_ref.shape)


def shard_sum(arrived, skip, factor):
    slots = arrived.shape[0]
    return pl.pallas_call(
        functools.partial(shard_sum_kernel, skip=skip, factor=factor),
        out_shape=jax.ShapeDtypeStruct((slots, arrived.shape[1] - skip), BF16),
        in_specs=[VMEM],
        out_specs=VMEM,
        compiler_params=params(),
        cost_estimate=cost(1_000_000, 4 * 1024 * 1024),
        name="shard_sum",
    )(arrived)


def table_grad_kernel(pair_row_ref, last_row_ref, pair_ref, last_ref, out_ref, last_rows_ref, *, fold):
    step = pl.program_id(0)
    block = out_ref.shape[0]

    @pl.when(step == 0)
    def _():
        slots = last_ref.shape[0]
        folded = last_ref[:, :fold].astype(F32).reshape(slots // 16, 16, fold)
        even, odd = folded[:, :8], folded[:, 8:]
        top = iota(even.shape, 1) < 4
        left = jnp.where(top, even, pltpu.roll(odd, 4, 1))
        right = jnp.where(top, pltpu.roll(even, 4, 1), odd)
        last_rows_ref[...] = jnp.concatenate([left, right], axis=2).reshape(last_rows_ref.shape).astype(BF16)

    def hot(row):
        places = iota((block, row.shape[1]), 0)
        return jnp.where(places == row - step * block, 1.0, 0.0).astype(BF16)

    out_ref[...] = mm(hot(pair_row_ref[...]), pair_ref[...]) + mm(hot(last_row_ref[...]), last_rows_ref[...])


def table_gradient(pair_row, last_row, pair, last, own_rows):
    width = pair.shape[1]
    steps = 8
    block = own_rows // steps

    def whole(shape):
        return pl.BlockSpec(shape, lambda i: (0,) * len(shape))

    return pl.pallas_call(
        functools.partial(table_grad_kernel, fold=width // 2),
        out_shape=jax.ShapeDtypeStruct((own_rows, width), F32),
        grid=(steps,),
        in_specs=[whole(pair_row.shape), whole(last_row.shape), whole(pair.shape), whole(last.shape)],
        out_specs=pl.BlockSpec((block, width), lambda i: (i, 0)),
        scratch_shapes=[pltpu.VMEM((last_row.shape[1], width), BF16)],
        compiler_params=params(),
        cost_estimate=cost(2 * own_rows * 1536 * width, 12 * 1024 * 1024),
        name="table_grad",
    )(pair_row, last_row, pair, last)


def finish_kernel(core_ref, mine_ref, other_ref, win_ref, wout_ref):
    own = core_ref[0] == pl.program_id(0)
    groups, _, columns = mine_ref.shape
    width4 = win_ref.shape[1]

    def put(ref):
        for group in range(groups):
            first = group * columns
            last = min(first + columns, width4)
            win_ref[:, first:last] = ref[group, :, : last - first].astype(F32)
        wout_ref[...] = ref[groups - 1, :, width4 - (groups - 1) * columns :].astype(F32)

    @pl.when(own)
    def _():
        put(mine_ref)

    @pl.when(jnp.logical_not(own))
    def _():
        put(other_ref)


def finish(core, mine, other, width, width4):
    half = width // 2
    shape = mine.shape
    return pl.pallas_call(
        finish_kernel,
        out_shape=(jax.ShapeDtypeStruct((width, width4), F32), jax.ShapeDtypeStruct((width, width), F32)),
        grid_spec=pltpu.PrefetchScalarGridSpec(
            num_scalar_prefetch=1,
            grid=(2,),
            in_specs=[pl.BlockSpec(shape, lambda i, core: (0, 0, 0))] * 2,
            out_specs=(
                pl.BlockSpec((half, width4), lambda i, core: (i, 0)),
                pl.BlockSpec((half, width), lambda i, core: (i, 0)),
            ),
        ),
        compiler_params=params(),
        cost_estimate=cost(1_000_000, 8 * 1024 * 1024),
        name="finish",
    )(core, mine, other)


def trade(payload):
    return lax.all_to_all(payload, AXES, split_axis=0, concat_axis=0, tiled=True)


def shards(table, w_in, w_out, item_owner, item_slot, seq_lengths, cotangent):
    table_axis = lax.axis_size("table")
    owners_n = lax.axis_size("dp") * table_axis
    length = item_slot.shape[1]
    own_rows, width = table.shape
    slots = owners_n * 8
    core = (lax.axis_index("table") % 2).astype(I32).reshape(1)
    swap = [(i, i ^ 1) for i in range(table_axis)]

    wanted, flat = requests(item_owner.reshape(MB, length), item_slot, owners_n)
    asked = trade(wanted)
    rows_first = trade(gather(asked, table, 0, 4))
    rows_later = trade(gather(asked, table, 4, 8))
    pair_row = asked[:, :8].reshape(1, slots)
    last_row = asked[:, 8:12].reshape(1, slots // 2)

    out, grad0, emb0, dpre0, gated0 = layer(seq_lengths, flat, rows_first, w_in, w_out, cotangent, None, 0)
    out, grad1, emb1, dpre1, gated1 = layer(seq_lengths, flat, rows_later, w_in, w_out, cotangent, out, 1)
    incoming_pair = trade(send_pair(flat, grad0, grad1, slots))
    out, grad2, emb2, dpre2, gated2 = layer(seq_lengths, flat, rows_later, w_in, w_out, cotangent, out, 2)

    halves = weight_grads(core, (emb0, emb1, emb2), (dpre0, dpre1, dpre2), (gated0, gated1, gated2), cotangent)
    columns = halves.shape[3]
    halves = halves.reshape(2, slots, columns)
    other = lax.ppermute(halves[1], "table", swap)
    arrived = trade(message(flat, grad2, halves, other))
    factor = (MB * length * owners_n) ** (-0.5)
    mine_full = trade(shard_sum(arrived, width // 2, factor))
    other_full = lax.ppermute(mine_full, "table", swap)
    table_grad = table_gradient(pair_row, last_row, incoming_pair, arrived, own_rows)
    shape = (4, width // 2, columns)
    win_grad, wout_grad = finish(core, mine_full.reshape(shape), other_full.reshape(shape), width, w_in.shape[1])
    return out, table_grad, win_grad, wout_grad


def solution(mesh):
    in_specs = (
        P(AXES, None),
        P(),
        P(),
        P(None, AXES, None),
        P(None, AXES),
        P(None, AXES, None),
        P(None, AXES, None),
    )
    out_specs = (P(None, AXES, None), P(AXES, None), P(), P())
    return jax.shard_map(shards, mesh=mesh, in_specs=in_specs, out_specs=out_specs, check_vma=False)
```

profile of v0, /device:TPU:1, one launch (start us, length us, event | category | flops | bytes accessed | tf_op | source)
XLA Modules:
  0.0 198.4 jit_solution(17040795015244513973)
XLA Ops:
  0.6 0.7 copy.16
  1.3 0.7 copy-done.6
  2.0 0.7 requests.1
  2.7 20.9 %all_to_all.67 = s32[128,1,128]{2,1,0:T(1,128)S(1)} all-to-all(s32[128,1,128]{2,1,0:T(1,128)S(1)} %bitcast.38), channel_id=1, replica_groups=mesh['dp'=16,'table'=8] {'dp','table'}, dimensions={0} | all-to-all | bytes 131072 | tf_op jit(solution)/shard_map/all_to_all | solution.py:527
  23.7 2.2 %copy-done.7 = bf16[4096,512]{1,0:T(8,128)(2,1)S(1)} copy-done((bf16[4096,512]{1,0:T(8,128)(2,1)S(1)}, bf16[4096,512]{1,0:T(8,128)(2,1)}, u32[]{:S(2)}) %copy-start.7) | copy-done | bytes 4194328
  25.9 4.6 %gather4.1 = bf16[1024,256]{1,0:T(8,128)(2,1)} custom-call(s32[128,128]{1,0:T(8,128)S(1)} %bitcast.33, bf16[4096,512]{1,0:T(8,128)(2,1)S(1)} %copy-done.7), custom_call_target="tpu_custom_call" | custom-call | flops 2147483648 | bytes 6291456 | tf_op jit(solution)/shard_map/gather4/pallas_call | solution.py:132
  30.4 4.4 %all-to-all-start.2 = ((bf16[128,8,256]{2,1,0:T(8,128)(2,1)}), bf16[128,8,256]{2,1,0:T(8,128)(2,1)S(1)}, u32[]{:S(2)}, u32[]{:S(2)}) async-start(bf16[128,8,256]{2,1,0:T(8,128)(2,1)} %bitcast.5), calls=%async_computation.2 | async-start | bytes 1048576 | tf_op jit(solution)/shard_map/all_to_all | solution.py:527
  34.8 0.0 copy-start.8
  34.8 2.2 %copy-done.8 = bf16[4096,512]{1,0:T(8,128)(2,1)S(1)} copy-done((bf16[4096,512]{1,0:T(8,128)(2,1)S(1)}, bf16[4096,512]{1,0:T(8,128)(2,1)}, u32[]{:S(2)}) %copy-start.8) | copy-done | bytes 4194328
  37.0 7.3 %gather8.1 = bf16[1024,512]{1,0:T(8,128)(2,1)} custom-call(s32[128,128]{1,0:T(8,128)S(1)} %bitcast.34, bf16[4096,512]{1,0:T(8,128)(2,1)S(1)} %copy-done.8), custom_call_target="tpu_custom_call" | custom-call | flops 4294967296 | bytes 6291456 | tf_op jit(solution)/shard_map/gather8/pallas_call | solution.py:132
  44.3 4.0 %all-to-all-done.2 = bf16[128,8,256]{2,1,0:T(8,128)(2,1)S(1)} async-done(((bf16[128,8,256]{2,1,0:T(8,128)(2,1)}), bf16[128,8,256]{2,1,0:T(8,128)(2,1)S(1)}, u32[]{:S(2)}, u32[]{:S(2)}) %all-to-all-start.2) | async-done | bytes 524320 | tf_op jit(solution)/shard_map/all_to_all | solution.py:527
  48.3 5.9 %all-to-all-start.1 = ((bf16[128,8,512]{2,1,0:T(8,128)(2,1)}), bf16[128,8,512]{2,1,0:T(8,128)(2,1)S(1)}, u32[]{:S(2)}, u32[]{:S(2)}) async-start(bf16[128,8,512]{2,1,0:T(8,128)(2,1)} %bitcast.3), calls=%async_computation.1 | async-start | bytes 2097152 | tf_op jit(solution)/shard_map/all_to_all | solution.py:527
  54.3 0.0 copy-start.5
  54.3 1.0 copy-done.5
  55.4 1.6 copy-done.9
  57.0 1.0 copy-done.10
  58.0 6.8 %layer0.1 = (bf16[3,256,512]{2,1,0:T(8,128)(2,1)}, bf16[256,512]{1,0:T(8,128)(2,1)S(1)}, bf16[512,256]{1,0:T(8,128)(2,1)S(1)}, bf16[256,2048]{1,0:T(8,128)(2,1)S(1)}, bf16[512,256]{1,0:T(8,128)(2,1)S(1)}) custom-call(s32[3,1,4]{2,1,0:T(1,128)S(1)} %copy-done.12, s32[8,256]{1,0:T(8,128)S(1)} %get-tuple-element.23.flat_ref, bf16[1024,256]{1,0:T(8,128)(2,1)S(1)} %bitcast.37, ...), custom_call_target="tpu_custom_call" | custom-call | flops 8000000000 | bytes 6291456 | tf_op jit(solution)/shard_map/layer0/pallas_call | solution.py:291
  64.8 0.7 copy-done.13
  65.5 7.5 %all-to-all-done.1 = bf16[128,8,512]{2,1,0:T(8,128)(2,1)S(1)} async-done(((bf16[128,8,512]{2,1,0:T(8,128)(2,1)}), bf16[128,8,512]{2,1,0:T(8,128)(2,1)S(1)}, u32[]{:S(2)}, u32[]{:S(2)}) %all-to-all-start.1) | async-done | bytes 1048608 | tf_op jit(solution)/shard_map/all_to_all | solution.py:527
  73.0 1.0 copy-done.11
  74.1 7.8 %layer1.1 = (bf16[3,256,512]{2,1,0:T(8,128)(2,1)}, bf16[256,512]{1,0:T(8,128)(2,1)S(1)}, bf16[512,256]{1,0:T(8,128)(2,1)S(1)}, bf16[256,2048]{1,0:T(8,128)(2,1)S(1)}, bf16[512,256]{1,0:T(8,128)(2,1)S(1)}) custom-call(s32[3,1,4]{2,1,0:T(1,128)S(1)} %copy-done.12, s32[8,256]{1,0:T(8,128)S(1)} %get-tuple-element.23.flat_ref, ...), custom_call_target="tpu_custom_call", output_to_operand_aliasing={{0}: (6, {})} | custom-call | flops 8000000000 | bytes 6291456 | tf_op jit(solution)/shard_map/layer1/pallas_call | solution.py:291
  81.9 0.7 copy-done.15
  82.6 8.0 %layer2.1 = (bf16[3,256,512]{2,1,0:T(8,128)(2,1)}, bf16[256,512]{1,0:T(8,128)(2,1)S(1)}, bf16[512,256]{1,0:T(8,128)(2,1)S(1)}, bf16[256,2048]{1,0:T(8,128)(2,1)S(1)}, bf16[512,256]{1,0:T(8,128)(2,1)S(1)}) custom-call(s32[3,1,4]{2,1,0:T(1,128)S(1)} %copy-done.12, s32[8,256]{1,0:T(8,128)S(1)} %get-tuple-element.23.flat_ref, ...), custom_call_target="tpu_custom_call", output_to_operand_aliasing={{0}: (6, {})} | custom-call | flops 8000000000 | bytes 6291456 | tf_op jit(solution)/shard_map/layer2/pallas_call | solution.py:291
  90.6 3.9 %weight_grads.1 = bf16[2,4,256,640]{3,2,1,0:T(8,128)(2,1)} custom-call(s32[1]{0:T(128)} %bitcast.9.core_ref, bf16[512,256]{1,0:T(8,128)(2,1)S(1)} %get-tuple-element.31.refs_0_, bf16[512,256]{1,0:T(8,128)(2,1)S(1)} %get-tuple-element.32.refs_1_, bf16[512,256]{1,0:T(8,128)(2,1)S(1)} %get-tuple-element.33.refs_2_, ...), custom_call_target="tpu_custom_call" | custom-call | flops 2013265920 | bytes 8388608 | tf_op jit(solution)/shard_map/weight_grads/pallas_call | solution.py:374
  94.5 1.6 slice.15
  96.1 1.3 collective-permute-start
  97.4 2.7 %collective-permute-done.other_ref = bf16[1024,640]{1,0:T(8,128)(2,1)S(1)} collective-permute-done((bf16[1024,640]{1,0:T(8,128)(2,1)S(1)}, bf16[1024,640]{1,0:T(8,128)(2,1)S(1)}, u32[]{:S(2)}, u32[]{:S(2)}) %collective-permute-start) | collective-permute-done | bytes 1310752 | tf_op jit(solution)/shard_map/ppermute | solution.py:554
  100.1 0.9 message.1
  101.0 31.2 %all_to_all.68 = bf16[128,8,896]{2,1,0:T(8,128)(2,1)S(1)} all-to-all(bf16[128,8,896]{2,1,0:T(8,128)(2,1)S(1)} %bitcast.26), channel_id=1, replica_groups=mesh['dp'=16,'table'=8] {'dp','table'}, dimensions={0} | all-to-all | bytes 3670016 | tf_op jit(solution)/shard_map/all_to_all | solution.py:527
  132.3 0.3 shard_sum.1
  132.5 0.0 copy-start.1
  132.5 1.0 copy-done.1
  133.6 4.5 %all-to-all-start.5 = ((bf16[128,8,640]{2,1,0:T(8,128)(2,1)}), bf16[128,8,640]{2,1,0:T(8,128)(2,1)S(1)}, u32[]{:S(2)}, u32[]{:S(2)}) async-start(bf16[128,8,640]{2,1,0:T(8,128)(2,1)} %bitcast.29), calls=%async_computation.5 | async-start | bytes 2621440 | tf_op jit(solution)/shard_map/all_to_all | solution.py:527
  138.1 0.0 copy-start.16
  138.1 0.9 copy-done.16
  139.0 0.7 send_pair.1
  139.7 0.0 copy-start.2
  139.7 1.0 copy-done.2
  140.7 19.2 %all-to-all-done.5 = bf16[128,8,640]{2,1,0:T(8,128)(2,1)S(1)} async-done(((bf16[128,8,640]{2,1,0:T(8,128)(2,1)}), bf16[128,8,640]{2,1,0:T(8,128)(2,1)S(1)}, u32[]{:S(2)}, u32[]{:S(2)}) %all-to-all-start.5) | async-done | bytes 1310752 | tf_op jit(solution)/shard_map/all_to_all | solution.py:527
  159.9 5.8 %all-to-all-start.3 = ((bf16[128,8,512]{2,1,0:T(8,128)(2,1)}), bf16[128,8,512]{2,1,0:T(8,128)(2,1)}, u32[]{:S(2)}, u32[]{:S(2)}) async-start(bf16[128,8,512]{2,1,0:T(8,128)(2,1)} %bitcast.32), calls=%async_computation.3 | async-start | bytes 2097152 | tf_op jit(solution)/shard_map/all_to_all | solution.py:527
  165.7 1.4 collective-permute-start.1
  167.0 0.1 slice.14
  167.1 0.1 reshape.45.pair_row_ref
  167.2 0.1 reshape.46.last_row_ref
  167.3 17.0 %all-to-all-done.3 = bf16[128,8,512]{2,1,0:T(8,128)(2,1)} async-done(((bf16[128,8,512]{2,1,0:T(8,128)(2,1)}), bf16[128,8,512]{2,1,0:T(8,128)(2,1)}, u32[]{:S(2)}, u32[]{:S(2)}) %all-to-all-start.3) | async-done | bytes 1048608 | tf_op jit(solution)/shard_map/all_to_all | solution.py:527
  184.4 10.2 %table_grad.1 = f32[4096,512]{1,0:T(8,128)} custom-call(s32[1,1024]{1,0:T(1,128)S(1)} %reshape.45.pair_row_ref, s32[1,512]{1,0:T(1,128)S(1)} %reshape.46.last_row_ref, bf16[1024,512]{1,0:T(8,128)(2,1)} %bitcast.8.pair_ref, bf16[1024,896]{1,0:T(8,128)(2,1)S(1)} %bitcast.25), custom_call_target="tpu_custom_call" | custom-call | flops 6442450944 | bytes 12582912 | tf_op jit(solution)/shard_map/table_grad/pallas_call | solution.py:471
  194.6 0.0 collective-permute-done.1
  194.6 3.8 %finish.1 = (f32[512,2048]{1,0:T(8,128)}, f32[512,512]{1,0:T(8,128)}) custom-call(s32[1]{0:T(128)} %bitcast.9.core_ref, bf16[4,256,640]{2,1,0:T(8,128)(2,1)S(1)} %bitcast.28, bf16[4,256,640]{2,1,0:T(8,128)(2,1)} %bitcast.17.other_ref), custom_call_target="tpu_custom_call" | custom-call | flops 1000000 | bytes 8388608 | tf_op jit(solution)/shard_map/finish/pallas_call | solution.py:508
  (17 shorter events, 0.0 us)
Async XLA Ops:
  1.3 0.7 copy-start.6
  23.7 2.2 %copy-start.7 = (bf16[4096,512]{1,0:T(8,128)(2,1)S(1)}, bf16[4096,512]{1,0:T(8,128)(2,1)}, u32[]{:S(2)}) copy-start(bf16[4096,512]{1,0:T(8,128)(2,1)} %table_ref.3) | copy-start | bytes 12582916
  30.4 17.9 %all-to-all-start.2 = ((bf16[128,8,256]{2,1,0:T(8,128)(2,1)}), bf16[128,8,256]{2,1,0:T(8,128)(2,1)S(1)}, u32[]{:S(2)}, u32[]{:S(2)}) async-start(bf16[128,8,256]{2,1,0:T(8,128)(2,1)} %bitcast.5), calls=%async_computation.2 | async-start | bytes 1048576 | tf_op jit(solution)/shard_map/all_to_all | solution.py:527
  34.8 2.2 %copy-start.8 = (bf16[4096,512]{1,0:T(8,128)(2,1)S(1)}, bf16[4096,512]{1,0:T(8,128)(2,1)}, u32[]{:S(2)}) copy-start(bf16[4096,512]{1,0:T(8,128)(2,1)} %table_ref.3) | copy-start | bytes 12582916
  44.3 10.0 %copy-start.3 = (bf16[3,256,512]{2,1,0:T(8,128)(2,1)S(1)}, bf16[3,256,512]{2,1,0:T(8,128)(2,1)}, u32[]{:S(2)}) copy-start(bf16[3,256,512]{2,1,0:T(8,128)(2,1)} %refs_9_.1) | copy-start | bytes 2359300
  44.3 10.0 %copy-start.12 = (s32[3,1,4]{2,1,0:T(1,128)S(1)}, s32[3,1,4]{2,1,0:T(1,128)}, u32[]{:S(2)}) copy-start(s32[3,1,4]{2,1,0:T(1,128)} %lengths_ref.5) | copy-start | bytes 148
  48.3 6.0 %copy-start.4 = (bf16[128,8,256]{2,1,0:T(8,128)(2,1)}, bf16[128,8,256]{2,1,0:T(8,128)(2,1)S(1)}, u32[]{:S(2)}) copy-start(bf16[128,8,256]{2,1,0:T(8,128)(2,1)S(1)} %all-to-all-done.2) | copy-start | bytes 1572868
  48.3 24.7 %all-to-all-start.1 = ((bf16[128,8,512]{2,1,0:T(8,128)(2,1)}), bf16[128,8,512]{2,1,0:T(8,128)(2,1)S(1)}, u32[]{:S(2)}, u32[]{:S(2)}) async-start(bf16[128,8,512]{2,1,0:T(8,128)(2,1)} %bitcast.3), calls=%async_computation.1 | async-start | bytes 2097152 | tf_op jit(solution)/shard_map/all_to_all | solution.py:527
  54.3 1.0 copy-start.5
  55.4 1.6 copy-start.9
  57.0 1.0 copy-start.10
  64.8 0.7 copy-start.13
  73.0 1.0 copy-start.11
  81.9 0.7 copy-start.15
  94.5 5.6 %copy-start = (bf16[2,4,256,640]{3,2,1,0:T(8,128)(2,1)S(1)}, bf16[2,4,256,640]{3,2,1,0:T(8,128)(2,1)}, u32[]{:S(2)}) copy-start(bf16[2,4,256,640]{3,2,1,0:T(8,128)(2,1)} %weight_grads.1) | copy-start | bytes 7864324
  96.1 4.0 %collective-permute-start = (bf16[1024,640]{1,0:T(8,128)(2,1)S(1)}, bf16[1024,640]{1,0:T(8,128)(2,1)S(1)}, u32[]{:S(2)}, u32[]{:S(2)}) collective-permute-start(bf16[1024,640]{1,0:T(8,128)(2,1)S(1)} %bitcast.40), channel_id=1, source_target_pairs={{0,1},{1,0},{2,3},{3,2},{4,5},{5,4},{6,7},{7,6},{8,9},{9,8},{10,11... | collective-permute-start | bytes 3932168 | tf_op jit(solution)/shard_map/ppermute | solution.py:554
  132.5 1.1 copy-start.1
  133.6 4.5 %copy-start.14 = (bf16[256,512]{1,0:T(8,128)(2,1)S(1)}, bf16[256,512]{1,0:T(8,128)(2,1)}, u32[]{:S(2)}) copy-start(bf16[256,512]{1,0:T(8,128)(2,1)} %copy-done.13) | copy-start | bytes 786436
  133.6 26.3 %all-to-all-start.5 = ((bf16[128,8,640]{2,1,0:T(8,128)(2,1)}), bf16[128,8,640]{2,1,0:T(8,128)(2,1)S(1)}, u32[]{:S(2)}, u32[]{:S(2)}) async-start(bf16[128,8,640]{2,1,0:T(8,128)(2,1)} %bitcast.29), calls=%async_computation.5 | async-start | bytes 2621440 | tf_op jit(solution)/shard_map/all_to_all | solution.py:527
  138.1 1.0 copy-start.16
  139.7 1.0 copy-start.2
  159.9 24.5 %all-to-all-start.3 = ((bf16[128,8,512]{2,1,0:T(8,128)(2,1)}), bf16[128,8,512]{2,1,0:T(8,128)(2,1)}, u32[]{:S(2)}, u32[]{:S(2)}) async-start(bf16[128,8,512]{2,1,0:T(8,128)(2,1)} %bitcast.32), calls=%async_computation.3 | async-start | bytes 2097152 | tf_op jit(solution)/shard_map/all_to_all | solution.py:527
  165.7 28.9 %collective-permute-start.1 = (bf16[1024,640]{1,0:T(8,128)(2,1)S(1)}, bf16[1024,640]{1,0:T(8,128)(2,1)}, u32[]{:S(2)}, u32[]{:S(2)}) collective-permute-start(bf16[1024,640]{1,0:T(8,128)(2,1)S(1)} %bitcast.27), channel_id=1, source_target_pairs={{0,1},{1,0},{2,3},{3,2},{4,5},{5,4},{6,7},{7,6},{8,9},{9,8},{10,11... | collective-permute-start | bytes 3932168 | tf_op jit(solution)/shard_map/ppermute | solution.py:558
where the time goes:
time: 199 us; the launch traced here: 198 us
  Pallas kernels  55.1 us (28%)
  blocking collectives  52.2 us (26%)
  waiting for transfers between devices  50.4 us (25%)
  starting transfers between devices  23.3 us (12%)
  local copies, waits for them, and re-layouts  16.7 us (8%)
    all_to_all x2, blocking collectives, trade(): lax.all_to_all(payload, AXES, split_axis=0, concat_axis=0, tiled=True)  52.2 us
    all_to_all x4, waiting for transfers between devices, trade(): lax.all_to_all(payload, AXES, split_axis=0, concat_axis=0, tiled=True)  47.7 us
    pallas_call x3, Pallas kernels, layer(): pl.pallas_call(functools.partial(layer_kernel, micro=micro), out_shape=(j...  22.6 us
    all_to_all x4, starting transfers between devices, trade(): lax.all_to_all(payload, AXES, split_axis=0, concat_axis=0, tiled=True)  20.6 us
    unnamed x35, local copies, waits for them, and re-layouts  14.8 us
    pallas_call x2, Pallas kernels, gather(): pl.pallas_call(functools.partial(gather_kernel, first=first, width=width,...  11.9 us
    pallas_call x1, Pallas kernels, table_gradient(): pl.pallas_call(functools.partial(table_grad_kernel, fold=width // 2), out...  10.2 us
  transfers between devices with their start and end apart: 6, of which 5 were waited for; matrix products, arithmetic and copies ran while one was open for 0% of the time, Pallas kernels for 13%

commit v1 on v0

v1 whole, which is shorter than its diff:
```python
import functools

import jax
import jax.numpy as jnp
from jax import lax
from jax.experimental import pallas as pl
from jax.experimental.pallas import tpu as pltpu
from jax.sharding import PartitionSpec as P

HEADS = 8
MB = 3
CAP = 4
AXES = ("dp", "table")
F32 = jnp.float32
BF16 = jnp.bfloat16
I32 = jnp.int32
VMEM = pl.BlockSpec(memory_space=pltpu.VMEM)
HBM = pl.BlockSpec(memory_space=pltpu.HBM)
SMEM = pl.BlockSpec(memory_space=pltpu.SMEM)


def iota(shape, dim):
    return lax.broadcasted_iota(I32, shape, dim)


def mm(a, b):
    return jnp.dot(a, b, preferred_element_type=F32)


def mm_nt(a, b):
    return lax.dot_general(a, b, (((1,), (1,)), ((), ())), preferred_element_type=F32)


def mm_tn(a, b):
    return lax.dot_general(a, b, (((0,), (0,)), ((), ())), preferred_element_type=F32)


def params(mib):
    return pltpu.CompilerParams(vmem_limit_bytes=mib * 1024 * 1024)


def cost(flops, bytes_accessed):
    return pl.CostEstimate(flops=flops, bytes_accessed=bytes_accessed, transcendentals=0)


def request_kernel(owner_ref, slot_ref, wanted_ref, flat_ref):
    length = slot_ref.shape[1]
    owners_n = wanted_ref.shape[0]
    upto = (iota((length, length), 0) <= iota((length, length), 1)).astype(BF16)
    lane_row = iota((128, length), 0)
    high = jnp.zeros((owners_n, 128), F32)
    low = jnp.zeros((owners_n, 128), F32)
    live = jnp.zeros((owners_n, 128), F32)
    flat_ref[...] = jnp.zeros(flat_ref.shape, I32)
    for micro in range(MB):
        owner = owner_ref[micro]
        slot = slot_ref[micro : micro + 1, :]
        hot = (iota((owners_n, length), 0) == owner).astype(F32)
        hot_bf = hot.astype(BF16)
        counts = mm(hot_bf, upto)
        rank = (jnp.sum(counts * hot, axis=0, keepdims=True) - 1.0).astype(I32)
        flat_ref[micro : micro + 1, :] = owner * 8 + rank
        here = lane_row == rank + CAP * micro
        high = high + mm_nt(hot_bf, jnp.where(here, (slot >> 6).astype(F32), 0.0).astype(BF16))
        low = low + mm_nt(hot_bf, jnp.where(here, (slot & 63).astype(F32), 0.0).astype(BF16))
        live = live + mm_nt(hot_bf, jnp.where(here, 1.0, 0.0).astype(BF16))
    wanted_ref[...] = jnp.where(live > 0.5, high * 64.0 + low, -1.0).astype(I32)


def requests(owner, slot, owners_n):
    return pl.pallas_call(
        request_kernel,
        out_shape=(
            jax.ShapeDtypeStruct((owners_n, 128), I32),
            jax.ShapeDtypeStruct((8, slot.shape[1]), I32),
        ),
        grid=(1,),
        in_specs=[
            pl.BlockSpec(owner.shape, lambda i: (0, 0, 0)),
            pl.BlockSpec(slot.shape, lambda i: (0, 0)),
        ],
        out_specs=(
            pl.BlockSpec((owners_n, 128), lambda i: (0, 0)),
            pl.BlockSpec((8, slot.shape[1]), lambda i: (0, 0)),
        ),
        compiler_params=params(8),
        name="requests",
    )(owner, slot)


def gather_kernel(asked_ref, table_ref, out_ref, block_ref, sem, *, first, width, steps):
    devices = asked_ref.shape[0]
    rows = devices * width
    block = table_ref.shape[0] // steps
    copies = [
        pltpu.make_async_copy(table_ref.at[pl.ds(step * block, block)], block_ref.at[step], sem.at[step])
        for step in range(steps)
    ]
    for copy in copies:
        copy.start()
    asked = asked_ref[...]
    spread = (iota((rows, devices), 0) // width == iota((rows, devices), 1)).astype(BF16)
    high = mm(spread, (asked >> 6).astype(F32).astype(BF16))
    low = mm(spread, (asked & 63).astype(F32).astype(BF16))
    mine = iota((rows, 128), 1) == iota((rows, 128), 0) % width + first
    column = jnp.sum(jnp.where(mine, high * 64.0 + low, 0.0), axis=1, keepdims=True).astype(I32)
    found = None
    for step in range(steps):
        copies[step].wait()
        hot = jnp.where(column - step * block == iota((rows, block), 1), 1.0, 0.0).astype(BF16)
        part = mm(hot, block_ref[step])
        found = part if found is None else found + part
    if width == 8:
        out_ref[...] = found.astype(BF16)
    else:
        whole = found.reshape(rows // 8, 8, found.shape[1])
        half = whole.shape[2] // 2
        left, right = whole[:, :, :half], whole[:, :, half:]
        top = iota(left.shape, 1) < 4
        even = jnp.where(top, left, pltpu.roll(right, 4, 1))
        odd = jnp.where(top, pltpu.roll(left, 4, 1), right)
        both = jnp.concatenate([even, odd], axis=1)
        out_ref[...] = both.reshape(out_ref.shape).astype(BF16)


def gather(asked, table, first, width):
    own_rows, columns = table.shape
    devices = asked.shape[0]
    steps = 8
    rows = devices * width
    out = (devices * 8, columns if width == 8 else columns // 2)
    return pl.pallas_call(
        functools.partial(gather_kernel, first=first, width=width, steps=steps),
        out_shape=jax.ShapeDtypeStruct(out, BF16),
        grid=(1,),
        in_specs=[
            pl.BlockSpec((devices, 128), lambda i: (0, 0)),
            pl.BlockSpec(memory_space=pltpu.HBM),
        ],
        out_specs=pl.BlockSpec(out, lambda i: (0, 0)),
        scratch_shapes=[
            pltpu.VMEM((steps, own_rows // steps, columns), BF16),
            pltpu.SemaphoreType.DMA((steps,)),
        ],
        compiler_params=params(60),
        cost_estimate=cost(2 * rows * own_rows * columns, 6 * 1024 * 1024),
        name=f"gather{width}",
    )(asked, table)


def column_of(row, copies=128):
    return jnp.transpose(jnp.broadcast_to(row.astype(F32), (copies, row.shape[1])))


def layer_kernel(lengths_ref, flat_ref, rows_hbm, w_in_hbm, w_out_hbm, cot_hbm, *rest, micro):
    out_hbm, grad_hbm, emb_t_hbm, dpre_hbm, gated_t_hbm = rest[-23:-18]
    (
        rows_ref,
        w_in_ref,
        w_out_ref,
        cot_ref,
        out_ref,
        grad_ref,
        emb_t_ref,
        dpre_ref,
        gated_t_ref,
        hidden_ref,
        slope_ref,
        weight_ref,
        dsilu_ref,
        att_ref,
        datt_ref,
        in_sem,
        w_sem,
        out_sem,
    ) = rest[-18:]
    length, width = grad_ref.shape
    slots = rows_ref.shape[0]
    chunk = 512

    rows_copy = pltpu.make_async_copy(rows_hbm, rows_ref, in_sem.at[0])
    rows_copy.start()
    w_copies = []
    for which, first in enumerate(range(0, 4 * width, chunk)):
        at = pl.ds(first, chunk)
        w_copies.append(pltpu.make_async_copy(w_in_hbm.at[:, at], w_in_ref.at[:, at], w_sem.at[which]))
        w_copies[-1].start()
    w_out_copy = pltpu.make_async_copy(w_out_hbm, w_out_ref, in_sem.at[1])
    w_out_copy.start()
    cot_copy = pltpu.make_async_copy(cot_hbm.at[micro], cot_ref, in_sem.at[2])
    cot_copy.start()
    column = column_of(flat_ref[micro : micro + 1, :])

    def placing(shift):
        lanes = iota((length, 128), 1).astype(F32)
        parts = [
            jnp.where(column == lanes + float(first - shift), 1.0, 0.0).astype(BF16)
            for first in range(0, slots, 128)
        ]
        return jnp.concatenate(parts, axis=1)

    if micro == 2:
        places = (placing(0), placing(4))
        rows_copy.wait()
        rows = rows_ref[...]
        embedded = jnp.concatenate([mm(places[0], rows), mm(places[1], rows)], axis=1)
    else:
        places = placing(4 * micro)
        rows_copy.wait()
        embedded = mm(places, rows_ref[...])
    emb_t_ref[...] = jnp.transpose(embedded).astype(BF16)
    outgoing = [pltpu.make_async_copy(emb_t_ref, emb_t_hbm, out_sem.at[0])]
    outgoing[-1].start()
    emb = embedded.astype(BF16)

    for which, first in enumerate(range(0, 4 * width, chunk)):
        w_copies[which].wait()
        at = slice(first, first + chunk)
        half = mm(emb, w_in_ref[:, at]) * 0.5
        tanh = jnp.tanh(half)
        act = half + half * tanh
        hidden_ref[:, at] = act.astype(BF16)
        slope_ref[:, at] = (0.5 * ((1.0 + tanh) + act * (1.0 - tanh))).astype(BF16)

    ends = []
    total = 0
    for which in range(3):
        total = total + lengths_ref[micro, 0, which]
        ends.append(total)

    def segment(places):
        return sum((places >= end).astype(I32) for end in ends)

    query_at = iota((length, length), 0)
    key_at = iota((length, length), 1)
    allowed = (segment(query_at) == segment(key_at)) & (key_at <= query_at)

    lane = iota((1, 128), 1)
    first_head = (lane < 64).astype(F32)
    second_head = 1.0 - first_head
    masks = (first_head.astype(BF16), second_head.astype(BF16))
    score_masks = ((first_head * 0.0625).astype(BF16), (second_head * 0.0625).astype(BF16))
    pairs = HEADS // 2
    for pair in range(pairs):
        lanes = slice(128 * pair, 128 * pair + 128)
        value = hidden_ref[:, width + 128 * pair : width + 128 * pair + 128]
        query = hidden_ref[:, 2 * width + 128 * pair : 2 * width + 128 * pair + 128]
        key = hidden_ref[:, 3 * width + 128 * pair : 3 * width + 128 * pair + 128]
        for head in range(2):
            half = mm_nt(query * score_masks[head], key)
            tanh = jnp.tanh(half)
            act = half + half * tanh
            at = slice(length * head, length * head + length)
            weight_ref[pair, :, at] = jnp.where(allowed, act, 0.0).astype(BF16)
            dsilu_ref[pair, :, at] = jnp.where(
                allowed, (1.0 + tanh) + act * (1.0 - tanh), 0.0
            ).astype(BF16)
        both = jnp.concatenate([value * masks[0], value * masks[1]], axis=0)
        att_ref[:, lanes] = mm(weight_ref[pair], both)

    attended = att_ref[...]
    centred = attended - jnp.mean(attended, axis=1, keepdims=True)
    inverse = lax.rsqrt(jnp.mean(centred * centred, axis=1, keepdims=True) + 1e-05)
    normed = centred * inverse
    gate = hidden_ref[:, :width].astype(F32)
    gated = normed * gate
    gated_t_ref[...] = jnp.transpose(gated).astype(BF16)
    outgoing.append(pltpu.make_async_copy(gated_t_ref, gated_t_hbm, out_sem.at[1]))
    outgoing[-1].start()
    w_out_copy.wait()
    cot_copy.wait()
    cot = cot_ref[...]
    out_ref[...] = (embedded + mm(gated.astype(BF16), w_out_ref[...])).astype(BF16)
    outgoing.append(pltpu.make_async_copy(out_ref, out_hbm.at[micro], out_sem.at[2]))
    outgoing[-1].start()

    dgated = mm_nt(cot, w_out_ref[...])
    dgate = dgated * normed
    dnormed = dgated * gate
    dpre_ref[:, :width] = (dgate * slope_ref[:, :width].astype(F32)).astype(BF16)
    shared = jnp.mean(dnormed * normed, axis=1, keepdims=True)
    dcentred = inverse * (dnormed - normed * shared)
    datt = dcentred - jnp.mean(dcentred, axis=1, keepdims=True)
    datt_ref[...] = datt.astype(BF16)

    for pair in range(pairs):
        at_value = slice(width + 128 * pair, width + 128 * pair + 128)
        at_query = slice(2 * width + 128 * pair, 2 * width + 128 * pair + 128)
        at_key = slice(3 * width + 128 * pair, 3 * width + 128 * pair + 128)
        value = hidden_ref[:, at_value]
        query = hidden_ref[:, at_query]
        key = hidden_ref[:, at_key]
        dhead = datt_ref[:, 128 * pair : 128 * pair + 128]
        parts = []
        for head in range(2):
            at = slice(length * head, length * head + length)
            dweight = mm_nt(dhead * masks[head], value)
            parts.append((dweight * dsilu_ref[pair, :, at].astype(F32)).astype(BF16))
        dscore = jnp.concatenate(parts, axis=1)
        both_keys = jnp.concatenate([key * score_masks[0], key * score_masks[1]], axis=0)
        dquery = mm(dscore, both_keys)
        dkeys = mm_tn(dscore, query * jnp.asarray(0.0625, BF16))
        dkey = jnp.where(lane < 64, dkeys[:length], dkeys[length:])
        dvalues = mm_tn(weight_ref[pair], dhead)
        dvalue = jnp.where(lane < 64, dvalues[:length], dvalues[length:])
        for at, grad in ((at_value, dvalue), (at_query, dquery), (at_key, dkey)):
            dpre_ref[:, at] = (grad * slope_ref[:, at].astype(F32)).astype(BF16)

    outgoing.append(pltpu.make_async_copy(dpre_ref, dpre_hbm, out_sem.at[3]))
    outgoing[-1].start()
    grad_ref[...] = (cot.astype(F32) + mm_nt(dpre_ref[...], w_in_ref[...])).astype(BF16)
    outgoing.append(pltpu.make_async_copy(grad_ref, grad_hbm, out_sem.at[4]))
    outgoing[-1].start()
    for copy in outgoing:
        copy.wait()


def layer(lengths, flat, rows, w_in, w_out, cotangent, outputs, after, micro):
    width = w_in.shape[0]
    length = cotangent.shape[1]
    pairs = HEADS // 2
    operands = [lengths, flat, rows, w_in, w_out, cotangent, *outputs, *after]
    shapes = [(length, width), (width, length), (length, 4 * width), (width, length)]
    return pl.pallas_call(
        functools.partial(layer_kernel, micro=micro),
        out_shape=[jax.ShapeDtypeStruct(cotangent.shape, BF16)] + [jax.ShapeDtypeStruct(shape, BF16) for shape in shapes],
        in_specs=[SMEM, VMEM] + [HBM] * (len(operands) - 2),
        out_specs=[HBM] * 5,
        scratch_shapes=[
            pltpu.VMEM(rows.shape, BF16),
            pltpu.VMEM(w_in.shape, BF16),
            pltpu.VMEM(w_out.shape, BF16),
            pltpu.VMEM((length, width), BF16),
            pltpu.VMEM((length, width), BF16),
        ]
        + [pltpu.VMEM(shape, BF16) for shape in shapes]
        + [
            pltpu.VMEM((length, 4 * width), BF16),
            pltpu.VMEM((length, 4 * width), BF16),
            pltpu.VMEM((pairs, length, 2 * length), BF16),
            pltpu.VMEM((pairs, length, 2 * length), BF16),
            pltpu.VMEM((length, width), F32),
            pltpu.VMEM((length, width), BF16),
            pltpu.SemaphoreType.DMA((3,)),
            pltpu.SemaphoreType.DMA((4,)),
            pltpu.SemaphoreType.DMA((5,)),
        ],
        input_output_aliases={6: 0} if outputs else {},
        compiler_params=params(60),
        cost_estimate=cost(8_000_000_000, 6 * 1024 * 1024),
        name=f"layer{micro}",
    )(*operands)


def send_pair_kernel(flat_ref, first_ref, second_ref, out_ref):
    slots = out_ref.shape[0]
    length = first_ref.shape[0]
    places = iota((slots, length), 0)
    one = jnp.where(places == flat_ref[0:1, :], 1.0, 0.0).astype(BF16)
    two = jnp.where(places == flat_ref[1:2, :] + 4, 1.0, 0.0).astype(BF16)
    placing = jnp.concatenate([one, two], axis=1)
    grads = jnp.concatenate([first_ref[...], second_ref[...]], axis=0)
    out_ref[...] = mm(placing, grads).astype(BF16)


def send_pair(flat, first, second, slots):
    return pl.pallas_call(
        send_pair_kernel,
        out_shape=jax.ShapeDtypeStruct((slots, first.shape[1]), BF16),
        grid=(1,),
        in_specs=[pl.BlockSpec(part.shape, lambda i: (0, 0)) for part in (flat, first, second)],
        out_specs=pl.BlockSpec((slots, first.shape[1]), lambda i: (0, 0)),
        compiler_params=params(16),
        cost_estimate=cost(1_000_000_000, 2 * 1024 * 1024),
        name="send_pair",
    )(flat, first, second)


def weights_kernel(half_ref, *refs):
    embs, dpres, gateds, cot_hbm, out_hbm = refs[0:3], refs[3:6], refs[6:9], refs[9], refs[10]
    emb_ref, dpre_ref, gated_ref, cot_ref, out_ref, sem, out_sem = refs[-7:]
    length = cot_hbm.shape[1]
    half = emb_ref.shape[0]
    groups, _, columns = out_ref.shape
    width4 = dpre_ref.shape[1]
    at = pl.ds(pl.multiple_of(half_ref[0] * half, half), half)
    copies = []

    def bring(source, target):
        copy = pltpu.make_async_copy(source, target, sem.at[len(copies)])
        copies.append(copy)
        copy.start()

    for m in range(MB):
        bring(embs[m].at[at], emb_ref.at[:, pl.ds(m * length, length)])
    for group in range(groups):
        first = group * columns
        across = pl.ds(first, min(columns, width4 - first))
        for m in range(MB):
            bring(dpres[m].at[:, across], dpre_ref.at[pl.ds(m * length, length), across])
    for m in range(MB):
        bring(gateds[m].at[at], gated_ref.at[:, pl.ds(m * length, length)])
        bring(cot_hbm.at[m], cot_ref.at[pl.ds(m * length, length)])
    for copy in copies[:MB]:
        copy.wait()
    sends = []
    for group in range(groups):
        first = group * columns
        last = min(first + columns, width4)
        for copy in copies[MB * (group + 1) : MB * (group + 2)]:
            copy.wait()
        out_ref[group, :, : last - first] = mm(emb_ref[...], dpre_ref[:, first:last]).astype(BF16)
        if group == groups - 1:
            for copy in copies[MB * (groups + 1) :]:
                copy.wait()
            out_ref[group, :, last - first :] = mm(gated_ref[...], cot_ref[...]).astype(BF16)
        send = pltpu.make_async_copy(out_ref.at[group], out_hbm.at[group], out_sem.at[group])
        sends.append(send)
        send.start()
    for send in sends:
        send.wait()


def weight_grads(half_index, embs, dpres, gateds, cotangent):
    width, length = embs[0].shape
    width4 = dpres[0].shape[1]
    half = width // 2
    shape = (4, half, (width4 + width) // 4)
    return pl.pallas_call(
        weights_kernel,
        out_shape=jax.ShapeDtypeStruct(shape, BF16),
        in_specs=[SMEM] + [HBM] * 10,
        out_specs=HBM,
        scratch_shapes=[
            pltpu.VMEM((half, MB * length), BF16),
            pltpu.VMEM((MB * length, width4), BF16),
            pltpu.VMEM((half, MB * length), BF16),
            pltpu.VMEM((MB * length, width), BF16),
            pltpu.VMEM(shape, BF16),
            pltpu.SemaphoreType.DMA((7 * MB,)),
            pltpu.SemaphoreType.DMA((4,)),
        ],
        compiler_params=params(60),
        cost_estimate=cost(768 * 512 * 2560, 6 * 1024 * 1024),
        name="weight_grads",
    )(half_index, *embs, *dpres, *gateds, cotangent)


def message_kernel(flat_ref, grad_ref, mine_ref, other_ref, after_ref, out_ref):
    del after_ref
    slots = out_ref.shape[0]
    length, width = grad_ref.shape
    half = width // 2
    places = iota((slots, length), 0)
    one = jnp.where(places == flat_ref[2:3, :], 1.0, 0.0).astype(BF16)
    two = jnp.where(places == flat_ref[2:3, :] + 4, 1.0, 0.0).astype(BF16)
    placing = jnp.concatenate([one, two], axis=1)
    grads = jnp.concatenate([grad_ref[:, :half], grad_ref[:, half:]], axis=0)
    out_ref[:, :half] = mm(placing, grads).astype(BF16)
    out_ref[:, half:] = (mine_ref[...].astype(F32) + other_ref[...].astype(F32)).astype(BF16)


def message(flat, grad, mine, other, after):
    slots, columns = other.shape
    width = grad.shape[1] // 2 + columns
    return pl.pallas_call(
        message_kernel,
        out_shape=jax.ShapeDtypeStruct((slots, width), BF16),
        grid=(1,),
        in_specs=[
            pl.BlockSpec(flat.shape, lambda i: (0, 0)),
            pl.BlockSpec(grad.shape, lambda i: (0, 0)),
            pl.BlockSpec((slots, columns), lambda i: (0, 0)),
            pl.BlockSpec((slots, columns), lambda i: (0, 0)),
            pl.BlockSpec(memory_space=pl.ANY),
        ],
        out_specs=pl.BlockSpec((slots, width), lambda i: (0, 0)),
        compiler_params=params(20),
        cost_estimate=cost(500_000_000, 6 * 1024 * 1024),
        name="message",
    )(flat, grad, mine, other, after)


def shard_sum_kernel(in_ref, out_hbm, copy_ref, sem, *, skip, factor):
    slots = in_ref.shape[0]
    parts = in_ref[:, skip:].astype(F32).reshape(slots // 16, 16, in_ref.shape[1] - skip)
    summed = (jnp.sum(parts, axis=0) * factor).astype(BF16)
    rows = copy_ref.shape[0]
    copy_ref[...] = jnp.broadcast_to(summed[None], (rows // 16, *summed.shape)).reshape(copy_ref.shape)
    copies = [
        pltpu.make_async_copy(copy_ref, out_hbm.at[pl.ds(part * rows, rows)], sem.at[part])
        for part in range(slots // rows)
    ]
    for copy in copies:
        copy.start()
    for copy in copies:
        copy.wait()


def shard_sum(arrived, skip, factor):
    slots = arrived.shape[0]
    columns = arrived.shape[1] - skip
    return pl.pallas_call(
        functools.partial(shard_sum_kernel, skip=skip, factor=factor),
        out_shape=jax.ShapeDtypeStruct((slots, columns), BF16),
        in_specs=[VMEM],
        out_specs=HBM,
        scratch_shapes=[pltpu.VMEM((slots // 4, columns), BF16), pltpu.SemaphoreType.DMA((4,))],
        compiler_params=params(60),
        cost_estimate=cost(1_000_000, 4 * 1024 * 1024),
        name="shard_sum",
    )(arrived)


def table_grad_kernel(pair_row_ref, last_row_ref, pair_ref, last_ref, out_ref, last_rows_ref, *, fold):
    step = pl.program_id(0)
    block = out_ref.shape[0]

    @pl.when(step == 0)
    def _():
        slots = last_ref.shape[0]
        folded = last_ref[:, :fold].astype(F32).reshape(slots // 16, 16, fold)
        even, odd = folded[:, :8], folded[:, 8:]
        top = iota(even.shape, 1) < 4
        left = jnp.where(top, even, pltpu.roll(odd, 4, 1))
        right = jnp.where(top, pltpu.roll(even, 4, 1), odd)
        last_rows_ref[...] = jnp.concatenate([left, right], axis=2).reshape(last_rows_ref.shape).astype(BF16)

    def hot(row):
        places = iota((block, row.shape[1]), 0)
        return jnp.where(places == row - step * block, 1.0, 0.0).astype(BF16)

    out_ref[...] = mm(hot(pair_row_ref[...]), pair_ref[...]) + mm(hot(last_row_ref[...]), last_rows_ref[...])


def table_gradient(pair_row, last_row, pair, last, own_rows):
    width = pair.shape[1]
    steps = 8
    block = own_rows // steps

    def whole(shape):
        return pl.BlockSpec(shape, lambda i: (0,) * len(shape))

    return pl.pallas_call(
        functools.partial(table_grad_kernel, fold=width // 2),
        out_shape=jax.ShapeDtypeStruct((own_rows, width), F32),
        grid=(steps,),
        in_specs=[whole(pair_row.shape), whole(last_row.shape), whole(pair.shape), whole(last.shape)],
        out_specs=pl.BlockSpec((block, width), lambda i: (i, 0)),
        scratch_shapes=[pltpu.VMEM((last_row.shape[1], width), BF16)],
        compiler_params=params(24),
        cost_estimate=cost(2 * own_rows * 1536 * width, 12 * 1024 * 1024),
        name="table_grad",
    )(pair_row, last_row, pair, last)


def finish_kernel(half_ref, in_ref, *rest):
    del half_ref
    win_ref, wout_ref = rest[-2:]
    groups, _, columns = in_ref.shape
    width4 = win_ref.shape[1]
    for group in range(groups):
        first = group * columns
        last = min(first + columns, width4)
        win_ref[:, first:last] = in_ref[group, :, : last - first].astype(F32)
    wout_ref[...] = in_ref[groups - 1, :, width4 - (groups - 1) * columns :].astype(F32)


def finish(half_index, part, before, width, width4):
    half = width // 2
    shape = part.shape
    steps = 2
    return pl.pallas_call(
        finish_kernel,
        out_shape=(jax.ShapeDtypeStruct((width, width4), F32), jax.ShapeDtypeStruct((width, width), F32)),
        grid_spec=pltpu.PrefetchScalarGridSpec(
            num_scalar_prefetch=1,
            grid=(steps,),
            in_specs=[pl.BlockSpec((shape[0], shape[1] // steps, shape[2]), lambda i, which: (0, i, 0))]
            + [pl.BlockSpec(memory_space=pl.ANY)] * len(before),
            out_specs=(
                pl.BlockSpec((half // steps, width4), lambda i, which: (which[0] * steps + i, 0)),
                pl.BlockSpec((half // steps, width), lambda i, which: (which[0] * steps + i, 0)),
            ),
        ),
        input_output_aliases={2: 0, 3: 1} if before else {},
        compiler_params=params(16),
        cost_estimate=cost(1_000_000, 4 * 1024 * 1024),
        name=f"finish{len(before)}",
    )(half_index, part, *before)


def trade(payload):
    return lax.all_to_all(payload, AXES, split_axis=0, concat_axis=0, tiled=True)


def shards(table, w_in, w_out, item_owner, item_slot, seq_lengths, cotangent):
    table_axis = lax.axis_size("table")
    owners_n = lax.axis_size("dp") * table_axis
    length = item_slot.shape[1]
    own_rows, width = table.shape
    slots = owners_n * 8
    core = (lax.axis_index("table") % 2).astype(I32).reshape(1)
    swap = [(i, i ^ 1) for i in range(table_axis)]

    wanted, flat = requests(item_owner.reshape(MB, 1, length), item_slot, owners_n)
    asked = trade(wanted)
    rows_pair = trade(gather(asked, table, 0, 8))
    rows_last = trade(gather(asked, table, 8, 4))
    pair_row = asked[:, :8].reshape(1, slots)
    last_row = asked[:, 8:12].reshape(1, slots // 2)

    out, grad0, emb0, dpre0, gated0 = layer(seq_lengths, flat, rows_pair, w_in, w_out, cotangent, (), (), 0)
    out, grad1, emb1, dpre1, gated1 = layer(seq_lengths, flat, rows_pair, w_in, w_out, cotangent, (out,), (), 1)
    sent_pair = send_pair(flat, grad0, grad1, slots)
    incoming_pair = trade(sent_pair)
    out, grad2, emb2, dpre2, gated2 = layer(
        seq_lengths, flat, rows_last, w_in, w_out, cotangent, (out,), (sent_pair,), 2
    )

    parts = ((emb0, emb1, emb2), (dpre0, dpre1, dpre2), (gated0, gated1, gated2), cotangent)
    sent = weight_grads(1 - core, *parts)
    columns = sent.shape[2]
    sent, incoming_pair = lax.optimization_barrier((sent, incoming_pair))
    other = lax.ppermute(sent.reshape(slots, columns), "table", swap)
    kept = weight_grads(core, *parts)
    arrived = trade(message(flat, grad2, kept.reshape(slots, columns), other, incoming_pair))
    factor = (MB * length * owners_n) ** (-0.5)
    mine_full = trade(shard_sum(arrived, width // 2, factor))
    table_grad = table_gradient(pair_row, last_row, incoming_pair, arrived, own_rows)
    mine_full, table_grad = lax.optimization_barrier((mine_full, table_grad))
    other_full = lax.ppermute(mine_full, "table", swap)
    shape = (4, width // 2, columns)
    partial = finish(core, mine_full.reshape(shape), (), width, w_in.shape[1])
    win_grad, wout_grad = finish(1 - core, other_full.reshape(shape), partial, width, w_in.shape[1])
    return out, table_grad, win_grad, wout_grad


def solution(mesh):
    in_specs = (
        P(AXES, None),
        P(),
        P(),
        P(None, AXES, None),
        P(None, AXES),
        P(None, AXES, None),
        P(None, AXES, None),
    )
    out_specs = (P(None, AXES, None), P(AXES, None), P(), P())
    return jax.shard_map(shards, mesh=mesh, in_specs=in_specs, out_specs=out_specs, check_vma=False)
```

time: 199 us -> 186 us (0.935)
  waiting for transfers between devices: 50.4 us -> 30.6 us
  Pallas kernels: 55.1 us -> 70 us
  local copies, waits for them, and re-layouts: 16.7 us -> 5.17 us
  starting transfers between devices: 23.3 us -> 26.1 us
    all_to_all x4, waiting for transfers between devices: 47.7 us -> 29.6 us  [trade(): lax.all_to_all(payload, AXES, split_axis=0, concat_axis=0, tiled=True)]
    pallas_call x4 -> x5, Pallas kernels: 26.5 us -> 38.1 us  [the longest x3 29 us: layer(): pl.pallas_call(functools.partial(layer_kernel, micro=micro), out_shape=[j...]
    unnamed x35 -> x30, local copies, waits for them, and re-layouts: 14.8 us -> 4.88 us
    all_to_all x4, starting transfers between devices: 20.6 us -> 23.5 us  [trade(): lax.all_to_all(payload, AXES, split_axis=0, concat_axis=0, tiled=True)]
    ppermute x1, waiting for transfers between devices: 2.66 us -> 0.01 us  [shards(): other = lax.ppermute(sent.reshape(slots, columns), 'table', swap)]
    pallas_call x1, Pallas kernels: 0.26 us -> 2.79 us  [shard_sum(): pl.pallas_call(functools.partial(shard_sum_kernel, skip=skip, factor=fact...]
  transfers between devices with their start and end apart: 6 -> 6, of which waited for: 5 -> 4; matrix products, arithmetic and copies ran while one was open for 0% -> 0% of each run, Pallas kernels for 13% -> 30%
where the time goes in v1:
time: 186 us
  Pallas kernels  70 us (38%)
  blocking collectives  52.9 us (28%)
  waiting for transfers between devices  30.6 us (16%)
  starting transfers between devices  26.1 us (14%)
  local copies, waits for them, and re-layouts  5.17 us (3%)
    all_to_all x2, blocking collectives, trade(): lax.all_to_all(payload, AXES, split_axis=0, concat_axis=0, tiled=True)  52.9 us
    all_to_all x4, waiting for transfers between devices, trade(): lax.all_to_all(payload, AXES, split_axis=0, concat_axis=0, tiled=True)  29.6 us
    pallas_call x3, Pallas kernels, layer(): pl.pallas_call(functools.partial(layer_kernel, micro=micro), out_shape=[j...  29 us
    all_to_all x4, starting transfers between devices, trade(): lax.all_to_all(payload, AXES, split_axis=0, concat_axis=0, tiled=True)  23.5 us
    pallas_call x2, Pallas kernels, gather(): pl.pallas_call(functools.partial(gather_kernel, first=first, width=width,...  13.4 us
    pallas_call x2, Pallas kernels, weight_grads(): pl.pallas_call(weights_kernel, out_shape=jax.ShapeDtypeStruct(shape, BF16...  9.1 us
    pallas_call x1, Pallas kernels, table_gradient(): pl.pallas_call(functools.partial(table_grad_kernel, fold=width // 2), out...  8.98 us
    unnamed x30, local copies, waits for them, and re-layouts  4.88 us
  transfers between devices with their start and end apart: 6, of which 4 were waited for; matrix products, arithmetic and copies ran while one was open for 0% of the time, Pallas kernels for 30%

profile of v1, /device:TPU:1, one launch (start us, length us, event | category | flops | bytes accessed | tf_op | source)
XLA Modules:
  0.0 185.7 jit_solution(12406977708477161843)
XLA Ops:
  0.6 0.0 copy-start.8
  0.6 0.7 copy-done.8
  1.3 0.7 copy-done.9
  2.0 0.7 requests.1
  2.7 0.0 copy-start.5
  2.8 21.1 %all_to_all.68 = s32[128,1,128]{2,1,0:T(1,128)} all-to-all(s32[128,1,128]{2,1,0:T(1,128)S(1)} %bitcast.30), channel_id=1, replica_groups=mesh['dp'=16,'table'=8] {'dp','table'}, dimensions={0} | all-to-all | bytes 131072 | tf_op jit(solution)/shard_map/all_to_all | solution.py:594
  23.9 0.0 copy-done.5
  23.9 7.9 %gather8.1 = bf16[1024,512]{1,0:T(8,128)(2,1)} custom-call(s32[128,128]{1,0:T(8,128)} %bitcast.37, bf16[4096,512]{1,0:T(8,128)(2,1)} %table_ref.3), custom_call_target="tpu_custom_call" | custom-call | flops 4294967296 | bytes 6291456 | tf_op jit(solution)/shard_map/gather8/pallas_call | solution.py:132
  31.8 4.5 %all-to-all-start.2 = ((bf16[128,8,512]{2,1,0:T(8,128)(2,1)}), bf16[128,8,512]{2,1,0:T(8,128)(2,1)S(1)}, u32[]{:S(2)}, u32[]{:S(2)}) async-start(bf16[128,8,512]{2,1,0:T(8,128)(2,1)} %bitcast.36), calls=%async_computation.2 | async-start | bytes 2097152 | tf_op jit(solution)/shard_map/all_to_all | solution.py:594
  36.3 5.5 %gather4.1 = bf16[1024,256]{1,0:T(8,128)(2,1)} custom-call(s32[128,128]{1,0:T(8,128)} %bitcast.38, bf16[4096,512]{1,0:T(8,128)(2,1)} %table_ref.3), custom_call_target="tpu_custom_call" | custom-call | flops 2147483648 | bytes 6291456 | tf_op jit(solution)/shard_map/gather4/pallas_call | solution.py:132
  41.8 13.5 %all-to-all-done.2 = bf16[128,8,512]{2,1,0:T(8,128)(2,1)S(1)} async-done(((bf16[128,8,512]{2,1,0:T(8,128)(2,1)}), bf16[128,8,512]{2,1,0:T(8,128)(2,1)S(1)}, u32[]{:S(2)}, u32[]{:S(2)}) %all-to-all-start.2) | async-done | bytes 1048608 | tf_op jit(solution)/shard_map/all_to_all | solution.py:594
  55.3 4.7 %all-to-all-start.1 = ((bf16[128,8,256]{2,1,0:T(8,128)(2,1)}), bf16[128,8,256]{2,1,0:T(8,128)(2,1)S(1)}, u32[]{:S(2)}, u32[]{:S(2)}) async-start(bf16[128,8,256]{2,1,0:T(8,128)(2,1)} %bitcast.42), calls=%async_computation.1 | async-start | bytes 1048576 | tf_op jit(solution)/shard_map/all_to_all | solution.py:594
  60.0 0.0 copy-done.12
  60.0 9.7 %layer0.1 = (bf16[3,256,512]{2,1,0:T(8,128)(2,1)}, bf16[256,512]{1,0:T(8,128)(2,1)}, bf16[512,256]{1,0:T(8,128)(2,1)}, bf16[256,2048]{1,0:T(8,128)(2,1)}, bf16[512,256]{1,0:T(8,128)(2,1)}) custom-call(s32[3,1,4]{2,1,0:T(1,128)} %lengths_ref.5, s32[8,256]{1,0:T(8,128)} %copy-done.5, bf16[1024,512]{1,0:T(8,128)(2,1)} %bitcast.34, bf16[512,2048]{1,0:T(8,128)(2,1)} %w_in_hbm.5, ...), custom_call_target="tpu_custom_call" | custom-call | flops 8000000000 | bytes 6291456 | tf_op jit(solution)/shard_map/layer0/pallas_call | solution.py:324
  69.7 0.0 copy-start.6
  69.7 0.0 copy-start.10
  69.7 9.8 %layer1.1 = (bf16[3,256,512]{2,1,0:T(8,128)(2,1)}, bf16[256,512]{1,0:T(8,128)(2,1)}, bf16[512,256]{1,0:T(8,128)(2,1)}, bf16[256,2048]{1,0:T(8,128)(2,1)}, bf16[512,256]{1,0:T(8,128)(2,1)}) custom-call(s32[3,1,4]{2,1,0:T(1,128)} %lengths_ref.5, s32[8,256]{1,0:T(8,128)} %copy-done.5, bf16[1024,512]{1,0:T(8,128)(2,1)} %bitcast.35, ...), custom_call_target="tpu_custom_call", output_to_operand_aliasing={{0}: (6, {})} | custom-call | flops 8000000000 | bytes 6291456 | tf_op jit(solution)/shard_map/layer1/pallas_call | solution.py:324
  79.5 0.0 copy-done.6
  79.5 0.0 copy-done.10
  79.6 0.0 copy-start.11
  79.6 0.9 copy-done.11
  80.5 1.7 send_pair.1.rest_1_
  82.2 0.0 all-to-all-done.1
  82.2 9.9 %all-to-all-start.3 = ((bf16[128,8,512]{2,1,0:T(8,128)(2,1)}), bf16[128,8,512]{2,1,0:T(8,128)(2,1)S(1)}, u32[]{:S(2)}, u32[]{:S(2)}) async-start(bf16[128,8,512]{2,1,0:T(8,128)(2,1)} %bitcast.10), calls=%async_computation.3 | async-start | bytes 2097152 | tf_op jit(solution)/shard_map/all_to_all | solution.py:594
  92.1 0.0 copy-done.14
  92.1 9.5 %layer2.1 = (bf16[3,256,512]{2,1,0:T(8,128)(2,1)}, bf16[256,512]{1,0:T(8,128)(2,1)}, bf16[512,256]{1,0:T(8,128)(2,1)}, bf16[256,2048]{1,0:T(8,128)(2,1)}, bf16[512,256]{1,0:T(8,128)(2,1)}) custom-call(s32[3,1,4]{2,1,0:T(1,128)} %lengths_ref.5, s32[8,256]{1,0:T(8,128)} %copy-done.5, bf16[1024,256]{1,0:T(8,128)(2,1)} %bitcast.41, ...), custom_call_target="tpu_custom_call", output_to_operand_aliasing={{0}: (6, {})} | custom-call | flops 8000000000 | bytes 6291456 | tf_op jit(solution)/shard_map/layer2/pallas_call | solution.py:324
  101.6 4.6 %weight_grads.3 = bf16[4,256,640]{2,1,0:T(8,128)(2,1)} custom-call(s32[1]{0:T(128)S(6)} %sub.4.half_ref, bf16[512,256]{1,0:T(8,128)(2,1)} %get-tuple-element.37.refs_0_, bf16[512,256]{1,0:T(8,128)(2,1)} %get-tuple-element.38.refs_1_, bf16[512,256]{1,0:T(8,128)(2,1)} %get-tuple-element.39.refs_2_, bf16[256,2048]{1,0:T(8,128)(2,1)} %get-tuple-element.40.refs_3_, ...), custom_call_target="tpu_custom_call" | custom-call | flops 1006632960 | bytes 6291456 | tf_op jit(solution)/shard_map/weight_grads/pallas_call | solution.py:429
  106.2 4.8 %all-to-all-done.3 = bf16[128,8,512]{2,1,0:T(8,128)(2,1)S(1)} async-done(((bf16[128,8,512]{2,1,0:T(8,128)(2,1)}), bf16[128,8,512]{2,1,0:T(8,128)(2,1)S(1)}, u32[]{:S(2)}, u32[]{:S(2)}) %all-to-all-start.3) | async-done | bytes 1048608 | tf_op jit(solution)/shard_map/all_to_all | solution.py:594
  111.0 1.3 collective-permute-start
  112.2 4.5 %weight_grads.2 = bf16[4,256,640]{2,1,0:T(8,128)(2,1)} custom-call(s32[1]{0:T(128)} %bitcast.8.half_ref, bf16[512,256]{1,0:T(8,128)(2,1)} %get-tuple-element.37.refs_0_, bf16[512,256]{1,0:T(8,128)(2,1)} %get-tuple-element.38.refs_1_, bf16[512,256]{1,0:T(8,128)(2,1)} %get-tuple-element.39.refs_2_, bf16[256,2048]{1,0:T(8,128)(2,1)} %get-tuple-element.40.refs_3_, ...), custom_call_target="tpu_custom_call" | custom-call | flops 1006632960 | bytes 6291456 | tf_op jit(solution)/shard_map/weight_grads/pallas_call | solution.py:429
  116.8 0.0 collective-permute-done.other_ref
  116.8 0.0 copy-start.1
  116.8 1.3 copy-done.1
  118.2 0.9 message.1
  119.1 31.8 %all_to_all.69 = bf16[128,8,896]{2,1,0:T(8,128)(2,1)} all-to-all(bf16[128,8,896]{2,1,0:T(8,128)(2,1)S(1)} %bitcast.23), channel_id=1, replica_groups=mesh['dp'=16,'table'=8] {'dp','table'}, dimensions={0} | all-to-all | bytes 3670016 | tf_op jit(solution)/shard_map/all_to_all | solution.py:594
  150.9 2.8 %shard_sum.1 = bf16[1024,640]{1,0:T(8,128)(2,1)} custom-call(bf16[1024,896]{1,0:T(8,128)(2,1)} %bitcast.21), custom_call_target="tpu_custom_call" | custom-call | flops 1000000 | bytes 4194304 | tf_op jit(solution)/shard_map/shard_sum/pallas_call | solution.py:503
  153.7 4.5 %all-to-all-start.5 = ((bf16[128,8,640]{2,1,0:T(8,128)(2,1)}), bf16[128,8,640]{2,1,0:T(8,128)(2,1)S(1)}, u32[]{:S(2)}, u32[]{:S(2)}) async-start(bf16[128,8,640]{2,1,0:T(8,128)(2,1)} %bitcast.32), calls=%async_computation.5 | async-start | bytes 2621440 | tf_op jit(solution)/shard_map/all_to_all | solution.py:594
  158.2 0.1 slice.9
  158.3 0.1 reshape.48.pair_row_ref
  158.4 0.1 reshape.49.last_row_ref
  158.5 0.0 copy-start.3
  158.5 1.2 copy-done.3
  159.7 9.0 %table_grad.1 = f32[4096,512]{1,0:T(8,128)} custom-call(s32[1,1024]{1,0:T(1,128)S(1)} %reshape.48.pair_row_ref, s32[1,512]{1,0:T(1,128)S(1)} %reshape.49.last_row_ref, bf16[1024,512]{1,0:T(8,128)(2,1)S(1)} %bitcast.28, bf16[1024,896]{1,0:T(8,128)(2,1)S(1)} %bitcast.22), custom_call_target="tpu_custom_call" | custom-call | flops 6442450944 | bytes 12582912 | tf_op jit(solution)/shard_map/table_grad/pallas_call | solution.py:544
  168.7 11.3 %all-to-all-done.5 = bf16[128,8,640]{2,1,0:T(8,128)(2,1)S(1)} async-done(((bf16[128,8,640]{2,1,0:T(8,128)(2,1)}), bf16[128,8,640]{2,1,0:T(8,128)(2,1)S(1)}, u32[]{:S(2)}, u32[]{:S(2)}) %all-to-all-start.5) | async-done | bytes 1310752 | tf_op jit(solution)/shard_map/all_to_all | solution.py:594
  180.0 1.3 collective-permute-start.1
  181.3 1.7 finish0.1
  183.0 1.0 collective-permute-done.1
  184.0 1.7 finish2.1
  (13 shorter events, 0.0 us)
Async XLA Ops:
  0.6 0.7 copy-start.8
  1.3 0.7 copy-start.9
  2.7 21.1 %copy-start.5 = (s32[8,256]{1,0:T(8,128)}, s32[8,256]{1,0:T(8,128)S(1)}, u32[]{:S(2)}) copy-start(s32[8,256]{1,0:T(8,128)S(1)} %get-tuple-element.29.flat_ref) | copy-start | bytes 24580
  31.8 23.5 %all-to-all-start.2 = ((bf16[128,8,512]{2,1,0:T(8,128)(2,1)}), bf16[128,8,512]{2,1,0:T(8,128)(2,1)S(1)}, u32[]{:S(2)}, u32[]{:S(2)}) async-start(bf16[128,8,512]{2,1,0:T(8,128)(2,1)} %bitcast.36), calls=%async_computation.2 | async-start | bytes 2097152 | tf_op jit(solution)/shard_map/all_to_all | solution.py:594
  55.3 4.7 %copy-start.12 = (bf16[128,8,512]{2,1,0:T(8,128)(2,1)}, bf16[128,8,512]{2,1,0:T(8,128)(2,1)S(1)}, u32[]{:S(2)}) copy-start(bf16[128,8,512]{2,1,0:T(8,128)(2,1)S(1)} %all-to-all-done.2) | copy-start | bytes 3145732
  55.3 26.9 %all-to-all-start.1 = ((bf16[128,8,256]{2,1,0:T(8,128)(2,1)}), bf16[128,8,256]{2,1,0:T(8,128)(2,1)S(1)}, u32[]{:S(2)}, u32[]{:S(2)}) async-start(bf16[128,8,256]{2,1,0:T(8,128)(2,1)} %bitcast.42), calls=%async_computation.1 | async-start | bytes 1048576 | tf_op jit(solution)/shard_map/all_to_all | solution.py:594
  69.7 9.8 %copy-start.6 = (s32[8,256]{1,0:T(8,128)S(1)}, s32[8,256]{1,0:T(8,128)}, u32[]{:S(2)}) copy-start(s32[8,256]{1,0:T(8,128)} %copy-done.5) | copy-start | bytes 24580
  69.7 9.8 %copy-start.10 = (bf16[256,512]{1,0:T(8,128)(2,1)S(1)}, bf16[256,512]{1,0:T(8,128)(2,1)}, u32[]{:S(2)}) copy-start(bf16[256,512]{1,0:T(8,128)(2,1)} %get-tuple-element.33.first_ref) | copy-start | bytes 786436
  79.6 1.0 copy-start.11
  82.2 9.9 %copy-start.14 = (bf16[128,8,256]{2,1,0:T(8,128)(2,1)}, bf16[128,8,256]{2,1,0:T(8,128)(2,1)S(1)}, u32[]{:S(2)}) copy-start(bf16[128,8,256]{2,1,0:T(8,128)(2,1)S(1)} %all-to-all-done.1) | copy-start | bytes 1572868
  82.2 28.8 %all-to-all-start.3 = ((bf16[128,8,512]{2,1,0:T(8,128)(2,1)}), bf16[128,8,512]{2,1,0:T(8,128)(2,1)S(1)}, u32[]{:S(2)}, u32[]{:S(2)}) async-start(bf16[128,8,512]{2,1,0:T(8,128)(2,1)} %bitcast.10), calls=%async_computation.3 | async-start | bytes 2097152 | tf_op jit(solution)/shard_map/all_to_all | solution.py:594
  111.0 5.8 %copy-start.2 = (bf16[128,8,512]{2,1,0:T(8,128)(2,1)}, bf16[128,8,512]{2,1,0:T(8,128)(2,1)S(1)}, u32[]{:S(2)}) copy-start(bf16[128,8,512]{2,1,0:T(8,128)(2,1)S(1)} %all-to-all-done.3) | copy-start | bytes 3145732
  111.0 5.8 %copy-start.4 = (bf16[256,512]{1,0:T(8,128)(2,1)S(1)}, bf16[256,512]{1,0:T(8,128)(2,1)}, u32[]{:S(2)}) copy-start(bf16[256,512]{1,0:T(8,128)(2,1)} %get-tuple-element.36.grad_ref) | copy-start | bytes 786436
  111.0 5.8 %copy-start.7 = (s32[8,256]{1,0:T(8,128)S(1)}, s32[8,256]{1,0:T(8,128)}, u32[]{:S(2)}) copy-start(s32[8,256]{1,0:T(8,128)} %copy-done.5) | copy-start | bytes 24580
  111.0 5.8 %collective-permute-start = (bf16[1024,640]{1,0:T(8,128)(2,1)}, bf16[1024,640]{1,0:T(8,128)(2,1)S(1)}, u32[]{:S(2)}, u32[]{:S(2)}) collective-permute-start(bf16[1024,640]{1,0:T(8,128)(2,1)} %bitcast.33), channel_id=1, source_target_pairs={{0,1},{1,0},{2,3},{3,2},{4,5},{5,4},{6,7},{7,6},{8,9},{9,8},{10,11... | collective-permute-start | bytes 3932168 | tf_op jit(solution)/shard_map/ppermute | solution.py:625
  116.8 1.3 copy-start.1
  153.7 4.5 %copy-start.13 = (s32[128,1,128]{2,1,0:T(1,128)S(1)}, s32[128,1,128]{2,1,0:T(1,128)}, u32[]{:S(2)}) copy-start(s32[128,1,128]{2,1,0:T(1,128)} %all_to_all.68) | copy-start | bytes 196612
  153.7 4.8 %copy-start = (bf16[128,8,896]{2,1,0:T(8,128)(2,1)S(1)}, bf16[128,8,896]{2,1,0:T(8,128)(2,1)}, u32[]{:S(2)}) copy-start(bf16[128,8,896]{2,1,0:T(8,128)(2,1)} %all_to_all.69) | copy-start | bytes 5505028
  153.7 26.3 %all-to-all-start.5 = ((bf16[128,8,640]{2,1,0:T(8,128)(2,1)}), bf16[128,8,640]{2,1,0:T(8,128)(2,1)S(1)}, u32[]{:S(2)}, u32[]{:S(2)}) async-start(bf16[128,8,640]{2,1,0:T(8,128)(2,1)} %bitcast.32), calls=%async_computation.5 | async-start | bytes 2621440 | tf_op jit(solution)/shard_map/all_to_all | solution.py:594
  158.5 1.2 copy-start.3
  180.0 4.0 %collective-permute-start.1 = (bf16[1024,640]{1,0:T(8,128)(2,1)S(1)}, bf16[1024,640]{1,0:T(8,128)(2,1)S(1)}, u32[]{:S(2)}, u32[]{:S(2)}) collective-permute-start(bf16[1024,640]{1,0:T(8,128)(2,1)S(1)} %bitcast.24), channel_id=1, source_target_pairs={{0,1},{1,0},{2,3},{3,2},{4,5},{5,4},{6,7},{7,6},{8,9},{9,8},{10,11... | collective-permute-start | bytes 3932168 | tf_op jit(solution)/shard_map/ppermute | solution.py:632

commit v2 on v1

v2 whole, which is shorter than its diff:
```python
import functools

import jax
import jax.numpy as jnp
from jax import lax
from jax.experimental import pallas as pl
from jax.experimental.pallas import tpu as pltpu
from jax.sharding import PartitionSpec as P

HEADS = 8
MB = 3
CAP = 4
AXES = ("dp", "table")
F32 = jnp.float32
BF16 = jnp.bfloat16
I32 = jnp.int32
VMEM = pl.BlockSpec(memory_space=pltpu.VMEM)
HBM = pl.BlockSpec(memory_space=pltpu.HBM)
SMEM = pl.BlockSpec(memory_space=pltpu.SMEM)


def iota(shape, dim):
    return lax.broadcasted_iota(I32, shape, dim)


def mm(a, b):
    return jnp.dot(a, b, preferred_element_type=F32)


def mm_nt(a, b):
    return lax.dot_general(a, b, (((1,), (1,)), ((), ())), preferred_element_type=F32)


def mm_tn(a, b):
    return lax.dot_general(a, b, (((0,), (0,)), ((), ())), preferred_element_type=F32)


def params(mib):
    return pltpu.CompilerParams(vmem_limit_bytes=mib * 1024 * 1024)


def cost(flops, bytes_accessed):
    return pl.CostEstimate(flops=flops, bytes_accessed=bytes_accessed, transcendentals=0)


def request_kernel(owner_ref, slot_ref, wanted_ref, flat_ref):
    length = slot_ref.shape[1]
    owners_n = wanted_ref.shape[0]
    upto = (iota((length, length), 0) <= iota((length, length), 1)).astype(BF16)
    lane_row = iota((128, length), 0)
    high = jnp.zeros((owners_n, 128), F32)
    low = jnp.zeros((owners_n, 128), F32)
    live = jnp.zeros((owners_n, 128), F32)
    flat_ref[...] = jnp.zeros(flat_ref.shape, I32)
    for micro in range(MB):
        owner = owner_ref[micro]
        slot = slot_ref[micro : micro + 1, :]
        hot = (iota((owners_n, length), 0) == owner).astype(F32)
        hot_bf = hot.astype(BF16)
        counts = mm(hot_bf, upto)
        rank = (jnp.sum(counts * hot, axis=0, keepdims=True) - 1.0).astype(I32)
        flat_ref[micro : micro + 1, :] = owner * 8 + rank
        here = lane_row == rank + CAP * micro
        high = high + mm_nt(hot_bf, jnp.where(here, (slot >> 6).astype(F32), 0.0).astype(BF16))
        low = low + mm_nt(hot_bf, jnp.where(here, (slot & 63).astype(F32), 0.0).astype(BF16))
        live = live + mm_nt(hot_bf, jnp.where(here, 1.0, 0.0).astype(BF16))
    wanted_ref[...] = jnp.where(live > 0.5, high * 64.0 + low, -1.0).astype(I32)


def requests(owner, slot, owners_n):
    return pl.pallas_call(
        request_kernel,
        out_shape=(
            jax.ShapeDtypeStruct((owners_n, 128), I32),
            jax.ShapeDtypeStruct((8, slot.shape[1]), I32),
        ),
        grid=(1,),
        in_specs=[
            pl.BlockSpec(owner.shape, lambda i: (0, 0, 0)),
            pl.BlockSpec(slot.shape, lambda i: (0, 0)),
        ],
        out_specs=(
            pl.BlockSpec((owners_n, 128), lambda i: (0, 0)),
            pl.BlockSpec((8, slot.shape[1]), lambda i: (0, 0)),
        ),
        compiler_params=params(8),
        name="requests",
    )(owner, slot)


def unfold(folded):
    half = folded.shape[1]
    whole = folded.reshape(folded.shape[0] // 16, 16, half)
    even, odd = whole[:, :8], whole[:, 8:]
    top = iota(even.shape, 1) < 4
    left = jnp.where(top, even, pltpu.roll(odd, 4, 1))
    right = jnp.where(top, pltpu.roll(even, 4, 1), odd)
    return jnp.concatenate([left, right], axis=2).reshape(folded.shape[0] // 2, 2 * half)


def gather_kernel(asked_hbm, table_hbm, out_ref, asked_ref, block_ref, wide_ref, sem):
    steps, block, columns = block_ref.shape
    devices = asked_ref.shape[0]
    copies = [pltpu.make_async_copy(asked_hbm, asked_ref, sem.at[steps])]
    for step in range(steps):
        source = table_hbm.at[pl.ds(step * block, block)]
        copies.append(pltpu.make_async_copy(source, block_ref.at[step], sem.at[step]))
    for copy in copies:
        copy.start()
    for step in range(steps):
        copies[1 + step].wait()
        wide_ref[step * block : (step + 1) * block, :] = block_ref[step].astype(F32)
    copies[0].wait()
    half = columns // 2
    below = iota((8, columns), 0)
    below_half = iota((8, half), 0)

    def two_devices(turn, carry):
        pairs = []
        lasts = []
        for which in range(2):
            names = [jnp.maximum(asked_ref[2 * turn + which, place], 0) for place in range(12)]
            rows = [wide_ref[pl.ds(name, 1), :] for name in names]
            tile = jnp.broadcast_to(rows[0], (8, columns))
            for place in range(1, 8):
                tile = jnp.where(below == place, rows[place], tile)
            pairs.append(tile)
            parts = [row[:, :half] for row in rows[8:]] + [row[:, half:] for row in rows[8:]]
            tile = jnp.broadcast_to(parts[0], (8, half))
            for place in range(1, 8):
                tile = jnp.where(below_half == place, parts[place], tile)
            lasts.append(tile)
        at = pl.ds(pl.multiple_of(16 * turn, 16), 16)
        out_ref[at, :columns] = jnp.concatenate(pairs, axis=0).astype(BF16)
        out_ref[at, columns:] = jnp.concatenate(lasts, axis=0).astype(BF16)
        return carry

    lax.fori_loop(0, devices // 2, two_devices, 0)


def gather(asked, table):
    own_rows, columns = table.shape
    devices = asked.shape[0]
    steps = 8
    return pl.pallas_call(
        gather_kernel,
        out_shape=jax.ShapeDtypeStruct((devices * 8, columns + columns // 2), BF16),
        in_specs=[HBM, HBM],
        out_specs=VMEM,
        scratch_shapes=[
            pltpu.SMEM(asked.shape, I32),
            pltpu.VMEM((steps, own_rows // steps, columns), BF16),
            pltpu.VMEM((own_rows, columns), F32),
            pltpu.SemaphoreType.DMA((steps + 1,)),
        ],
        compiler_params=params(59),
        cost_estimate=cost(6_000_000_000, 6 * 1024 * 1024),
        name="gather",
    )(asked, table)


def column_of(row, copies=128):
    return jnp.transpose(jnp.broadcast_to(row.astype(F32), (copies, row.shape[1])))


def layer_body(micro, lengths_ref, column, rows_ref, weights, cot, stores, scratch, folded):
    w_in_ref, w_out_ref, wait_in, wait_out = weights
    out_ref, grad_ref, emb_t_ref, gated_t_ref, dpre_ref, stored = stores
    hidden_ref, slope_ref, weight_ref, dsilu_ref, att_ref, datt_ref = scratch
    width = w_out_ref.shape[0]
    length = hidden_ref.shape[0]
    slots = rows_ref.shape[0]
    chunk = 512

    def placing(shift):
        lanes = iota((length, 128), 1).astype(F32)
        parts = [
            jnp.where(column == lanes + float(first - shift), 1.0, 0.0).astype(BF16)
            for first in range(0, slots, 128)
        ]
        return jnp.concatenate(parts, axis=1)

    if folded:
        places = (placing(0), placing(4))
        rows = rows_ref[:, width:]
        embedded = jnp.concatenate([mm(places[0], rows), mm(places[1], rows)], axis=1)
    else:
        places = placing(4 * micro)
        embedded = mm(places, rows_ref[:, :width])
    emb_t_ref[...] = jnp.transpose(embedded).astype(BF16)
    stored("emb_t")
    emb = embedded.astype(BF16)

    for which, first in enumerate(range(0, 4 * width, chunk)):
        wait_in(which)
        at = slice(first, first + chunk)
        half = mm(emb, w_in_ref[:, at]) * 0.5
        tanh = jnp.tanh(half)
        act = half + half * tanh
        hidden_ref[:, at] = act.astype(BF16)
        slope_ref[:, at] = (0.5 * ((1.0 + tanh) + act * (1.0 - tanh))).astype(BF16)

    ends = []
    total = 0
    for which in range(3):
        total = total + lengths_ref[micro, 0, which]
        ends.append(total)

    def segment(places):
        return sum((places >= end).astype(I32) for end in ends)

    query_at = iota((length, length), 0)
    key_at = iota((length, length), 1)
    allowed = (segment(query_at) == segment(key_at)) & (key_at <= query_at)

    lane = iota((1, 128), 1)
    first_head = (lane < 64).astype(F32)
    second_head = 1.0 - first_head
    masks = (first_head.astype(BF16), second_head.astype(BF16))
    score_masks = ((first_head * 0.0625).astype(BF16), (second_head * 0.0625).astype(BF16))
    pairs = HEADS // 2
    for pair in range(pairs):
        lanes = slice(128 * pair, 128 * pair + 128)
        value = hidden_ref[:, width + 128 * pair : width + 128 * pair + 128]
        query = hidden_ref[:, 2 * width + 128 * pair : 2 * width + 128 * pair + 128]
        key = hidden_ref[:, 3 * width + 128 * pair : 3 * width + 128 * pair + 128]
        for head in range(2):
            half = mm_nt(query * score_masks[head], key)
            tanh = jnp.tanh(half)
            act = half + half * tanh
            at = slice(length * head, length * head + length)
            weight_ref[pair, :, at] = jnp.where(allowed, act, 0.0).astype(BF16)
            dsilu_ref[pair, :, at] = jnp.where(
                allowed, (1.0 + tanh) + act * (1.0 - tanh), 0.0
            ).astype(BF16)
        both = jnp.concatenate([value * masks[0], value * masks[1]], axis=0)
        att_ref[:, lanes] = mm(weight_ref[pair], both)

    attended = att_ref[...]
    centred = attended - jnp.mean(attended, axis=1, keepdims=True)
    inverse = lax.rsqrt(jnp.mean(centred * centred, axis=1, keepdims=True) + 1e-05)
    normed = centred * inverse
    gate = hidden_ref[:, :width].astype(F32)
    gated = normed * gate
    gated_t_ref[...] = jnp.transpose(gated).astype(BF16)
    stored("gated_t")
    wait_out()
    cot = cot()
    out_ref[...] = (embedded + mm(gated.astype(BF16), w_out_ref[...])).astype(BF16)
    stored("out")

    dgated = mm_nt(cot, w_out_ref[...])
    dgate = dgated * normed
    dnormed = dgated * gate
    dpre_ref[:, :width] = (dgate * slope_ref[:, :width].astype(F32)).astype(BF16)
    shared = jnp.mean(dnormed * normed, axis=1, keepdims=True)
    dcentred = inverse * (dnormed - normed * shared)
    datt = dcentred - jnp.mean(dcentred, axis=1, keepdims=True)
    datt_ref[...] = datt.astype(BF16)

    for pair in range(pairs):
        at_value = slice(width + 128 * pair, width + 128 * pair + 128)
        at_query = slice(2 * width + 128 * pair, 2 * width + 128 * pair + 128)
        at_key = slice(3 * width + 128 * pair, 3 * width + 128 * pair + 128)
        value = hidden_ref[:, at_value]
        query = hidden_ref[:, at_query]
        key = hidden_ref[:, at_key]
        dhead = datt_ref[:, 128 * pair : 128 * pair + 128]
        parts = []
        for head in range(2):
            at = slice(length * head, length * head + length)
            dweight = mm_nt(dhead * masks[head], value)
            parts.append((dweight * dsilu_ref[pair, :, at].astype(F32)).astype(BF16))
        dscore = jnp.concatenate(parts, axis=1)
        both_keys = jnp.concatenate([key * score_masks[0], key * score_masks[1]], axis=0)
        dquery = mm(dscore, both_keys)
        dkeys = mm_tn(dscore, query * jnp.asarray(0.0625, BF16))
        dkey = jnp.where(lane < 64, dkeys[:length], dkeys[length:])
        dvalues = mm_tn(weight_ref[pair], dhead)
        dvalue = jnp.where(lane < 64, dvalues[:length], dvalues[length:])
        for at, grad in ((at_value, dvalue), (at_query, dquery), (at_key, dkey)):
            dpre_ref[:, at] = (grad * slope_ref[:, at].astype(F32)).astype(BF16)

    stored("dpre")
    grad_ref[...] = (cot.astype(F32) + mm_nt(dpre_ref[...], w_in_ref[...])).astype(BF16)


def start_all(pairs, sem):
    copies = [pltpu.make_async_copy(source, target, sem.at[k]) for k, (source, target) in enumerate(pairs)]
    for copy in copies:
        copy.start()
    return copies


def waiting(copies):
    pending = list(copies)

    def wait():
        while pending:
            pending.pop().wait()

    return wait


def column_chunks(source, target, chunk):
    at = [pl.ds(first, chunk) for first in range(0, source.shape[1], chunk)]
    return [(source.at[:, here], target.at[:, here]) for here in at]


def layer_scratch(length, width):
    pairs = HEADS // 2
    return [
        pltpu.VMEM((length, 4 * width), BF16),
        pltpu.VMEM((length, 4 * width), BF16),
        pltpu.VMEM((pairs, length, 2 * length), BF16),
        pltpu.VMEM((pairs, length, 2 * length), BF16),
        pltpu.VMEM((length, width), F32),
        pltpu.VMEM((length, width), BF16),
    ]


def layers_kernel(half_ref, lengths_ref, flat_ref, rows_ref, w_in_hbm, w_out_hbm, cot_hbm, *rest):
    out_hbm, sent_hbm, back_hbm, kept_ref = rest[:4]
    w_in_ref, w_out_ref, cot_ref, out_ref, emb_t_ref, gated_t_ref, dpre_ref, grad_ref, sent_ref, back_ref = rest[4:14]
    scratch, (in_sem, out_sem) = rest[14:20], rest[20:]
    slots = rows_ref.shape[0]
    width = w_out_ref.shape[0]
    length = cot_hbm.shape[1]
    width4 = w_in_ref.shape[1]
    w_chunks = column_chunks(w_in_hbm, w_in_ref, 512)
    at = [pl.ds(m * length, length) for m in range(MB)]
    copies = start_all(
        [*w_chunks, (w_out_hbm, w_out_ref)] + [(cot_hbm.at[m], cot_ref.at[at[m]]) for m in range(MB)], in_sem
    )
    waits = [waiting([copy]) for copy in copies]
    outgoing = []

    def send(source, target):
        outgoing.append(pltpu.make_async_copy(source, target, out_sem.at[len(outgoing)]))
        outgoing[-1].start()

    for micro in range(MB):

        def stored(name, micro=micro):
            if name == "out":
                send(out_ref.at[micro], out_hbm.at[micro])

        def cot(micro=micro):
            waits[5 + micro]()
            return cot_ref[micro * length : (micro + 1) * length]

        layer_body(
            micro,
            lengths_ref,
            column_of(flat_ref[micro : micro + 1, :]),
            rows_ref,
            (w_in_ref, w_out_ref, lambda which: waits[which](), waits[4]),
            cot,
            (
                out_ref.at[micro],
                grad_ref.at[at[micro]],
                emb_t_ref.at[:, at[micro]],
                gated_t_ref.at[:, at[micro]],
                dpre_ref.at[at[micro]],
                stored,
            ),
            scratch,
            micro == 2,
        )
    groups, half, columns = sent_ref.shape

    def weights(mine, put):
        rows = pl.ds(pl.multiple_of(mine * half, half), half)
        for group in range(groups):
            first = group * columns
            last = min(first + columns, width4)
            part = mm(emb_t_ref[rows, :], dpre_ref[:, first:last]).astype(BF16)
            if group == groups - 1:
                part = jnp.concatenate([part, mm(gated_t_ref[rows, :], cot_ref[...]).astype(BF16)], axis=1)
            put(group, part)

    def put_sent(group, part):
        sent_ref[group] = part
        send(sent_ref.at[group], sent_hbm.at[group])

    def put_kept(group, part):
        kept_ref[group * half : (group + 1) * half, :] = part

    weights(1 - half_ref[0], put_sent)
    places = iota((slots, length), 0)

    def placing(micro, shift):
        return jnp.where(places == flat_ref[micro : micro + 1, :] + shift, 1.0, 0.0).astype(BF16)

    pair = jnp.concatenate([placing(0, 0), placing(1, 4)], axis=1)
    back_ref[:, :width] = mm(pair, grad_ref[: 2 * length]).astype(BF16)
    last = jnp.concatenate([placing(2, 0), placing(2, 4)], axis=1)
    halves = [grad_ref[2 * length :, : width // 2], grad_ref[2 * length :, width // 2 :]]
    back_ref[:, width:] = mm(last, jnp.concatenate(halves, axis=0)).astype(BF16)
    send(back_ref, back_hbm)
    weights(half_ref[0], put_kept)
    for copy in outgoing:
        copy.wait()


def layers(core, lengths, flat, rows, w_in, w_out, cotangent):
    width = w_in.shape[0]
    length = cotangent.shape[1]
    slots = rows.shape[0]
    columns = 5 * width // 4
    sent = (4, width // 2, columns)
    return pl.pallas_call(
        layers_kernel,
        out_shape=[
            jax.ShapeDtypeStruct(shape, BF16) for shape in [cotangent.shape, sent, rows.shape, (slots, columns)]
        ],
        in_specs=[SMEM, SMEM, VMEM, VMEM] + [HBM] * 3,
        out_specs=[HBM, HBM, HBM, VMEM],
        scratch_shapes=[
            pltpu.VMEM(shape, BF16)
            for shape in [
                w_in.shape,
                w_out.shape,
                (MB * length, width),
                cotangent.shape,
                (width, MB * length),
                (width, MB * length),
                (MB * length, 4 * width),
                (MB * length, width),
                sent,
                rows.shape,
            ]
        ]
        + layer_scratch(length, width)
        + [pltpu.SemaphoreType.DMA((8,)), pltpu.SemaphoreType.DMA((8,))],
        compiler_params=params(46),
        cost_estimate=cost(28_000_000_000, 10 * 1024 * 1024),
        name="layers",
    )(core, lengths, flat, rows, w_in, w_out, cotangent)


def message_kernel(back_hbm, kept_ref, other_ref, out_ref, sem):
    skip = back_hbm.shape[1]
    copy = pltpu.make_async_copy(back_hbm, out_ref.at[:, pl.ds(0, skip)], sem)
    copy.start()
    out_ref[:, skip:] = (kept_ref[...].astype(F32) + other_ref[...].astype(F32)).astype(BF16)
    copy.wait()


def message(back, kept, other):
    return pl.pallas_call(
        message_kernel,
        out_shape=jax.ShapeDtypeStruct((back.shape[0], back.shape[1] + kept.shape[1]), BF16),
        in_specs=[HBM, VMEM, VMEM],
        out_specs=VMEM,
        scratch_shapes=[pltpu.SemaphoreType.DMA],
        compiler_params=params(16),
        cost_estimate=cost(1_000_000, 4 * 1024 * 1024),
        name="message",
    )(back, kept, other)


def shard_sum_kernel(in_ref, out_ref, *, skip, factor):
    slots = in_ref.shape[0]
    parts = in_ref[:, skip:].astype(F32).reshape(slots // 16, 16, in_ref.shape[1] - skip)
    summed = (jnp.sum(parts, axis=0) * factor).astype(BF16)
    out_ref[...] = jnp.broadcast_to(summed[None], (slots // 16, *summed.shape)).reshape(out_ref.shape)


def shard_sum(arrived, skip, factor):
    slots = arrived.shape[0]
    return pl.pallas_call(
        functools.partial(shard_sum_kernel, skip=skip, factor=factor),
        out_shape=jax.ShapeDtypeStruct((slots, arrived.shape[1] - skip), BF16),
        in_specs=[VMEM],
        out_specs=VMEM,
        compiler_params=params(16),
        cost_estimate=cost(1_000_000, 4 * 1024 * 1024),
        name="shard_sum",
    )(arrived)


def table_grad_kernel(pair_row_ref, last_row_ref, arrived_ref, out_ref, last_rows_ref):
    step = pl.program_id(0)
    block, width = out_ref.shape

    @pl.when(step == 0)
    def _():
        last_rows_ref[...] = unfold(arrived_ref[:, width : width + width // 2].astype(F32)).astype(BF16)

    def hot(row):
        places = iota((block, row.shape[1]), 0)
        return jnp.where(places == row - step * block, 1.0, 0.0).astype(BF16)

    out_ref[...] = mm(hot(pair_row_ref[...]), arrived_ref[:, :width]) + mm(
        hot(last_row_ref[...]), last_rows_ref[...]
    )


def table_gradient(pair_row, last_row, arrived, own_rows, width):
    steps = 8
    block = own_rows // steps

    def whole(shape):
        return pl.BlockSpec(shape, lambda i: (0,) * len(shape))

    return pl.pallas_call(
        table_grad_kernel,
        out_shape=jax.ShapeDtypeStruct((own_rows, width), F32),
        grid=(steps,),
        in_specs=[whole(pair_row.shape), whole(last_row.shape), whole(arrived.shape)],
        out_specs=pl.BlockSpec((block, width), lambda i: (i, 0)),
        scratch_shapes=[pltpu.VMEM((last_row.shape[1], width), BF16)],
        compiler_params=params(24),
        cost_estimate=cost(2 * own_rows * 1536 * width, 12 * 1024 * 1024),
        name="table_grad",
    )(pair_row, last_row, arrived)


def finish_kernel(half_ref, in_ref, *rest):
    del half_ref
    win_ref, wout_ref = rest[-2:]
    groups, _, columns = in_ref.shape
    width4 = win_ref.shape[1]
    for group in range(groups):
        first = group * columns
        last = min(first + columns, width4)
        win_ref[:, first:last] = in_ref[group, :, : last - first].astype(F32)
    wout_ref[...] = in_ref[groups - 1, :, width4 - (groups - 1) * columns :].astype(F32)


def finish(half_index, part, before, width, width4):
    half = width // 2
    shape = part.shape
    steps = 2
    return pl.pallas_call(
        finish_kernel,
        out_shape=(jax.ShapeDtypeStruct((width, width4), F32), jax.ShapeDtypeStruct((width, width), F32)),
        grid_spec=pltpu.PrefetchScalarGridSpec(
            num_scalar_prefetch=1,
            grid=(steps,),
            in_specs=[pl.BlockSpec((shape[0], shape[1] // steps, shape[2]), lambda i, which: (0, i, 0))]
            + [pl.BlockSpec(memory_space=pl.ANY)] * len(before),
            out_specs=(
                pl.BlockSpec((half // steps, width4), lambda i, which: (which[0] * steps + i, 0)),
                pl.BlockSpec((half // steps, width), lambda i, which: (which[0] * steps + i, 0)),
            ),
        ),
        input_output_aliases={2: 0, 3: 1} if before else {},
        compiler_params=params(16),
        cost_estimate=cost(1_000_000, 4 * 1024 * 1024),
        name=f"finish{len(before)}",
    )(half_index, part, *before)


def trade(payload):
    return lax.all_to_all(payload, AXES, split_axis=0, concat_axis=0, tiled=True)


def shards(table, w_in, w_out, item_owner, item_slot, seq_lengths, cotangent):
    table_axis = lax.axis_size("table")
    owners_n = lax.axis_size("dp") * table_axis
    length = item_slot.shape[1]
    own_rows, width = table.shape
    slots = owners_n * 8
    core = (lax.axis_index("table") % 2).astype(I32).reshape(1)
    swap = [(i, i ^ 1) for i in range(table_axis)]

    wanted, flat = requests(item_owner.reshape(MB, 1, length), item_slot, owners_n)
    asked = trade(wanted)
    rows = trade(gather(asked, table))
    pair_row = asked[:, :8].reshape(1, slots)
    last_row = asked[:, 8:12].reshape(1, slots // 2)
    out, sent, back, kept = layers(core, seq_lengths, flat, rows, w_in, w_out, cotangent)
    columns = sent.shape[2]
    other = lax.ppermute(sent.reshape(slots, columns), "table", swap)
    arrived = trade(message(back, kept, other))
    factor = (MB * length * owners_n) ** (-0.5)
    mine_full = trade(shard_sum(arrived, rows.shape[1], factor))
    table_grad = table_gradient(pair_row, last_row, arrived, own_rows, width)
    mine_full, table_grad = lax.optimization_barrier((mine_full, table_grad))
    other_full = lax.ppermute(mine_full, "table", swap)
    shape = (4, width // 2, columns)
    partial = finish(core, mine_full.reshape(shape), (), width, w_in.shape[1])
    win_grad, wout_grad = finish(1 - core, other_full.reshape(shape), partial, width, w_in.shape[1])
    return out, table_grad, win_grad, wout_grad


def solution(mesh):
    in_specs = (
        P(AXES, None),
        P(),
        P(),
        P(None, AXES, None),
        P(None, AXES),
        P(None, AXES, None),
        P(None, AXES, None),
    )
    out_specs = (P(None, AXES, None), P(AXES, None), P(), P())
    return jax.shard_map(shards, mesh=mesh, in_specs=in_specs, out_specs=out_specs, check_vma=False)
```

time: 186 us -> 167 us (0.90)
  Pallas kernels: 70 us -> 47.4 us
  starting transfers between devices: 26.1 us -> 12.7 us
  blocking collectives: 52.9 us -> 63.5 us
  waiting for transfers between devices: 30.6 us -> 39.8 us
  local copies, waits for them, and re-layouts: 5.17 us -> 2.72 us
    pallas_call x10 -> x4, Pallas kernels: 63.1 us -> 42.1 us  [the longest x1 25.1 us: layers(): pl.pallas_call(layers_kernel, out_shape=[jax.ShapeDtypeStruct(shape, BF16...]
    all_to_all x4 -> x2, starting transfers between devices: 23.5 us -> 10.1 us  [trade(): lax.all_to_all(payload, AXES, split_axis=0, concat_axis=0, tiled=True)]
    all_to_all x2, blocking collectives: 52.9 us -> 63.5 us  [trade(): lax.all_to_all(payload, AXES, split_axis=0, concat_axis=0, tiled=True)]
    all_to_all x4 -> x2, waiting for transfers between devices: 29.6 us -> 36.9 us  [trade(): lax.all_to_all(payload, AXES, split_axis=0, concat_axis=0, tiled=True)]
    ppermute x1, waiting for transfers between devices: 0.01 us -> 2.66 us  [shards(): other = lax.ppermute(sent.reshape(slots, columns), 'table', swap)]
    pallas_call x1, Pallas kernels: 2.79 us -> 0.26 us  [shard_sum(): pl.pallas_call(functools.partial(shard_sum_kernel, skip=skip, factor=fact...]
    unnamed x30 -> x14, local copies, waits for them, and re-layouts: 4.88 us -> 2.44 us
  transfers between devices with their start and end apart: 6 -> 4, of which waited for: 4 -> 4; matrix products, arithmetic and copies ran while one was open for 0% -> 0% of each run, Pallas kernels for 30% -> 7%
where the time goes in v2:
time: 167 us
  blocking collectives  63.5 us (38%)
  Pallas kernels  47.4 us (28%)
  waiting for transfers between devices  39.8 us (24%)
  starting transfers between devices  12.7 us (8%)
  local copies, waits for them, and re-layouts  2.72 us (2%)
    all_to_all x2, blocking collectives, trade(): lax.all_to_all(payload, AXES, split_axis=0, concat_axis=0, tiled=True)  63.5 us
    all_to_all x2, waiting for transfers between devices, trade(): lax.all_to_all(payload, AXES, split_axis=0, concat_axis=0, tiled=True)  36.9 us
    pallas_call x1, Pallas kernels, layers(): pl.pallas_call(layers_kernel, out_shape=[jax.ShapeDtypeStruct(shape, BF16...  25.1 us
    all_to_all x2, starting transfers between devices, trade(): lax.all_to_all(payload, AXES, split_axis=0, concat_axis=0, tiled=True)  10.1 us
    pallas_call x1, Pallas kernels, table_gradient(): pl.pallas_call(table_grad_kernel, out_shape=jax.ShapeDtypeStruct((own_row...  9 us
    pallas_call x1, Pallas kernels, gather(): pl.pallas_call(gather_kernel, out_shape=jax.ShapeDtypeStruct((devices * 8...  7.59 us
    pallas_call x2, Pallas kernels, finish(): pl.pallas_call(finish_kernel, out_shape=(jax.ShapeDtypeStruct((width, wid...  4.33 us
  transfers between devices with their start and end apart: 4, of which 4 were waited for; matrix products, arithmetic and copies ran while one was open for 0% of the time, Pallas kernels for 7%

profile of v2, /device:TPU:1, one launch (start us, length us, event | category | flops | bytes accessed | tf_op | source)
XLA Modules:
  0.0 166.9 jit_solution(9298884874449255224)
XLA Ops:
  0.6 0.0 copy-start.1
  0.6 0.7 copy-done.1
  1.3 0.0 copy-start.2
  1.3 0.7 copy-done.2
  2.0 0.7 requests.1
  2.7 21.1 %all_to_all.45 = s32[128,1,128]{2,1,0:T(1,128)} all-to-all(s32[128,1,128]{2,1,0:T(1,128)S(1)} %bitcast.22), channel_id=1, replica_groups=mesh['dp'=16,'table'=8] {'dp','table'}, dimensions={0} | all-to-all | bytes 131072 | tf_op jit(solution)/shard_map/all_to_all | solution.py:557
  23.9 7.6 %gather.1 = bf16[1024,768]{1,0:T(8,128)(2,1)} custom-call(s32[128,128]{1,0:T(8,128)} %bitcast.26, bf16[4096,512]{1,0:T(8,128)(2,1)} %table_hbm.1), custom_call_target="tpu_custom_call" | custom-call | flops 6000000000 | bytes 6291456 | tf_op jit(solution)/shard_map/gather/pallas_call | solution.py:145
  31.5 0.0 copy-start.3
  31.5 0.0 copy-start.4
  31.5 0.0 copy-start.5
  31.5 4.6 %all-to-all-start.1 = ((bf16[128,8,768]{2,1,0:T(8,128)(2,1)}), bf16[128,8,768]{2,1,0:T(8,128)(2,1)S(1)}, u32[]{:S(2)}, u32[]{:S(2)}) async-start(bf16[128,8,768]{2,1,0:T(8,128)(2,1)} %bitcast.25), calls=%async_computation.1 | async-start | bytes 3145728 | tf_op jit(solution)/shard_map/all_to_all | solution.py:557
  36.2 24.7 %all-to-all-done.1 = bf16[128,8,768]{2,1,0:T(8,128)(2,1)S(1)} async-done(((bf16[128,8,768]{2,1,0:T(8,128)(2,1)}), bf16[128,8,768]{2,1,0:T(8,128)(2,1)S(1)}, u32[]{:S(2)}, u32[]{:S(2)}) %all-to-all-start.1) | async-done | bytes 1572896 | tf_op jit(solution)/shard_map/all_to_all | solution.py:557
  60.9 0.0 copy-done.3
  60.9 0.0 copy-done.4
  60.9 0.0 copy-done.5
  60.9 25.1 %layers.1 = (bf16[3,256,512]{2,1,0:T(8,128)(2,1)}, bf16[4,256,640]{2,1,0:T(8,128)(2,1)S(1)}, bf16[1024,768]{1,0:T(8,128)(2,1)S(1)}, bf16[1024,640]{1,0:T(8,128)(2,1)S(1)}) custom-call(s32[1]{0:T(128)} %bitcast.half_ref, s32[3,1,4]{2,1,0:T(1,128)S(1)} %copy-done.5, s32[8,256]{1,0:T(8,128)S(1)} %get-tuple-element.16.flat_ref, bf16[1024,768]{1,0:T(8,128)(2,1)S(1)} %bitcast.20, ...), custom_call_target="tpu_custom_call" | custom-call | flops 28000000000 | bytes 10485760 | tf_op jit(solution)/shard_map/layers/pallas_call | solution.py:412
  85.9 1.3 collective-permute-start
  87.3 2.7 %collective-permute-done.other_ref = bf16[1024,640]{1,0:T(8,128)(2,1)S(1)} collective-permute-done((bf16[1024,640]{1,0:T(8,128)(2,1)S(1)}, bf16[1024,640]{1,0:T(8,128)(2,1)S(1)}, u32[]{:S(2)}, u32[]{:S(2)}) %collective-permute-start) | collective-permute-done | bytes 1310752 | tf_op jit(solution)/shard_map/ppermute | solution.py:576
  89.9 0.4 message.1
  90.4 42.3 %all_to_all.46 = bf16[128,8,1408]{2,1,0:T(8,128)(2,1)S(1)} all-to-all(bf16[128,8,1408]{2,1,0:T(8,128)(2,1)S(1)} %bitcast.16), channel_id=1, replica_groups=mesh['dp'=16,'table'=8] {'dp','table'}, dimensions={0} | all-to-all | bytes 5767168 | tf_op jit(solution)/shard_map/all_to_all | solution.py:557
  132.7 0.3 shard_sum.1
  133.0 0.0 copy-start
  133.0 1.0 copy-done
  134.0 0.0 copy-start.6
  134.0 5.5 %all-to-all-start.3 = ((bf16[128,8,640]{2,1,0:T(8,128)(2,1)}), bf16[128,8,640]{2,1,0:T(8,128)(2,1)}, u32[]{:S(2)}, u32[]{:S(2)}) async-start(bf16[128,8,640]{2,1,0:T(8,128)(2,1)} %bitcast.19), calls=%async_computation.3 | async-start | bytes 2621440 | tf_op jit(solution)/shard_map/all_to_all | solution.py:557
  139.5 0.0 copy-done.6
  139.5 0.1 slice.9
  139.6 0.1 reshape.40.pair_row_ref
  139.7 0.1 reshape.41.last_row_ref
  139.8 9.0 %table_grad.1 = f32[4096,512]{1,0:T(8,128)} custom-call(s32[1,1024]{1,0:T(1,128)S(1)} %reshape.40.pair_row_ref, s32[1,512]{1,0:T(1,128)S(1)} %reshape.41.last_row_ref, bf16[1024,1408]{1,0:T(8,128)(2,1)S(1)} %bitcast.18), custom_call_target="tpu_custom_call" | custom-call | flops 6442450944 | bytes 12582912 | tf_op jit(solution)/shard_map/table_grad/pallas_call | solution.py:507
  148.8 12.2 %all-to-all-done.3 = bf16[128,8,640]{2,1,0:T(8,128)(2,1)} async-done(((bf16[128,8,640]{2,1,0:T(8,128)(2,1)}), bf16[128,8,640]{2,1,0:T(8,128)(2,1)}, u32[]{:S(2)}, u32[]{:S(2)}) %all-to-all-start.3) | async-done | bytes 1310752 | tf_op jit(solution)/shard_map/all_to_all | solution.py:557
  161.0 1.3 collective-permute-start.1
  162.3 2.6 %finish0.1 = (f32[512,2048]{1,0:T(8,128)}, f32[512,512]{1,0:T(8,128)}) custom-call(s32[1]{0:T(128)} %bitcast.half_ref, bf16[4,256,640]{2,1,0:T(8,128)(2,1)} %bitcast.13.in_ref), custom_call_target="tpu_custom_call" | custom-call | flops 1000000 | bytes 4194304 | tf_op jit(solution)/shard_map/finish0/pallas_call | solution.py:536
  165.0 0.2 collective-permute-done.1
  165.2 1.7 %finish2.1 = (f32[512,2048]{1,0:T(8,128)}, f32[512,512]{1,0:T(8,128)}) custom-call(s32[1]{0:T(128)S(6)} %sub.3.half_ref, bf16[4,256,640]{2,1,0:T(8,128)(2,1)S(1)} %bitcast.21, f32[512,2048]{1,0:T(8,128)} %get-tuple-element.24.rest_0_, f32[512,512]{1,0:T(8,128)} %get-tuple-element.25.rest_1_), custom_call_target="tpu_custom_call", output_to_operand_aliasing={{0}: (2, {}), {1}: (3, {})} | custom-call | flops 1000000 | bytes 4194304 | tf_op jit(solution)/shard_map/finish2/pallas_call | solution.py:536
Async XLA Ops:
  0.6 0.7 copy-start.1
  1.3 0.7 copy-start.2
  31.5 29.4 %copy-start.3 = (bf16[3,256,512]{2,1,0:T(8,128)(2,1)S(1)}, bf16[3,256,512]{2,1,0:T(8,128)(2,1)}, u32[]{:S(2)}) copy-start(bf16[3,256,512]{2,1,0:T(8,128)(2,1)} %cot_hbm.1) | copy-start | bytes 2359300
  31.5 29.4 %copy-start.4 = (bf16[512,512]{1,0:T(8,128)(2,1)S(1)}, bf16[512,512]{1,0:T(8,128)(2,1)}, u32[]{:S(2)}) copy-start(bf16[512,512]{1,0:T(8,128)(2,1)} %w_out_hbm.1) | copy-start | bytes 1572868
  31.5 29.4 %copy-start.5 = (s32[3,1,4]{2,1,0:T(1,128)S(1)}, s32[3,1,4]{2,1,0:T(1,128)}, u32[]{:S(2)}) copy-start(s32[3,1,4]{2,1,0:T(1,128)} %lengths_ref.1) | copy-start | bytes 148
  31.5 29.3 %all-to-all-start.1 = ((bf16[128,8,768]{2,1,0:T(8,128)(2,1)}), bf16[128,8,768]{2,1,0:T(8,128)(2,1)S(1)}, u32[]{:S(2)}, u32[]{:S(2)}) async-start(bf16[128,8,768]{2,1,0:T(8,128)(2,1)} %bitcast.25), calls=%async_computation.1 | async-start | bytes 3145728 | tf_op jit(solution)/shard_map/all_to_all | solution.py:557
  85.9 4.0 %collective-permute-start = (bf16[1024,640]{1,0:T(8,128)(2,1)S(1)}, bf16[1024,640]{1,0:T(8,128)(2,1)S(1)}, u32[]{:S(2)}, u32[]{:S(2)}) collective-permute-start(bf16[1024,640]{1,0:T(8,128)(2,1)S(1)} %bitcast.24), channel_id=1, source_target_pairs={{0,1},{1,0},{2,3},{3,2},{4,5},{5,4},{6,7},{7,6},{8,9},{9,8},{10,11... | collective-permute-start | bytes 3932168 | tf_op jit(solution)/shard_map/ppermute | solution.py:576
  133.0 1.1 copy-start
  134.0 5.5 %copy-start.6 = (s32[128,1,128]{2,1,0:T(1,128)S(1)}, s32[128,1,128]{2,1,0:T(1,128)}, u32[]{:S(2)}) copy-start(s32[128,1,128]{2,1,0:T(1,128)} %all_to_all.45) | copy-start | bytes 196612
  134.0 27.0 %all-to-all-start.3 = ((bf16[128,8,640]{2,1,0:T(8,128)(2,1)}), bf16[128,8,640]{2,1,0:T(8,128)(2,1)}, u32[]{:S(2)}, u32[]{:S(2)}) async-start(bf16[128,8,640]{2,1,0:T(8,128)(2,1)} %bitcast.19), calls=%async_computation.3 | async-start | bytes 2621440 | tf_op jit(solution)/shard_map/all_to_all | solution.py:557
  161.0 4.2 %collective-permute-start.1 = (bf16[1024,640]{1,0:T(8,128)(2,1)}, bf16[1024,640]{1,0:T(8,128)(2,1)S(1)}, u32[]{:S(2)}, u32[]{:S(2)}) collective-permute-start(bf16[1024,640]{1,0:T(8,128)(2,1)} %bitcast.11), channel_id=1, source_target_pairs={{0,1},{1,0},{2,3},{3,2},{4,5},{5,4},{6,7},{7,6},{8,9},{9,8},{10,11... | collective-permute-start | bytes 3932168 | tf_op jit(solution)/shard_map/ppermute | solution.py:582

commit v3 on v2

--- a/solution.py
+++ b/solution.py
@@ -163,55 +163,64 @@
     return jnp.transpose(jnp.broadcast_to(row.astype(F32), (copies, row.shape[1])))
 
 
-def layer_body(micro, lengths_ref, column, rows_ref, weights, cot, stores, scratch, folded):
-    w_in_ref, w_out_ref, wait_in, wait_out = weights
-    out_ref, grad_ref, emb_t_ref, gated_t_ref, dpre_ref, stored = stores
-    hidden_ref, slope_ref, weight_ref, dsilu_ref, att_ref, datt_ref = scratch
+def both_heads(pair_columns, masks):
+    return jnp.concatenate([pair_columns * masks[0], pair_columns * masks[1]], axis=0)
+
+
+def layers_kernel(half_ref, lengths_ref, flat_ref, rows_ref, w_in_hbm, w_out_hbm, cot_hbm, *rest):
+    out_hbm, sent_hbm, back_hbm, kept_ref = rest[:4]
+    w_in_ref, w_out_ref, cot_ref, out_ref, emb_t_ref, gated_t_ref, dpre_ref, grad_ref, sent_ref, back_ref = rest[4:14]
+    emb_ref, hidden_ref, slope_ref, weight_ref, dsilu_ref, att_ref, datt_ref, in_sem, out_sem = rest[14:]
+    slots = rows_ref.shape[0]
     width = w_out_ref.shape[0]
-    length = hidden_ref.shape[0]
-    slots = rows_ref.shape[0]
+    length = cot_hbm.shape[1]
+    width4 = w_in_ref.shape[1]
     chunk = 512
-
-    def placing(shift):
-        lanes = iota((length, 128), 1).astype(F32)
-        parts = [
-            jnp.where(column == lanes + float(first - shift), 1.0, 0.0).astype(BF16)
-            for first in range(0, slots, 128)
-        ]
-        return jnp.concatenate(parts, axis=1)
-
-    if folded:
-        places = (placing(0), placing(4))
-        rows = rows_ref[:, width:]
-        embedded = jnp.concatenate([mm(places[0], rows), mm(places[1], rows)], axis=1)
-    else:
-        places = placing(4 * micro)
-        embedded = mm(places, rows_ref[:, :width])
-    emb_t_ref[...] = jnp.transpose(embedded).astype(BF16)
-    stored("emb_t")
-    emb = embedded.astype(BF16)
-
-    for which, first in enumerate(range(0, 4 * width, chunk)):
-        wait_in(which)
-        at = slice(first, first + chunk)
-        half = mm(emb, w_in_ref[:, at]) * 0.5
+    chunks = [slice(first, first + chunk) for first in range(0, width4, chunk)]
+    incoming = []
+
+    def bring(source, target):
+        incoming.append(pltpu.make_async_copy(source, target, in_sem.at[len(incoming)]))
+        incoming[-1].start()
+
+    for part in chunks:
+        at = pl.ds(part.start, chunk)
+        bring(w_in_hbm.at[:, at], w_in_ref.at[:, at])
+    bring(w_out_hbm, w_out_ref)
+    bring(cot_hbm, cot_ref)
+    outgoing = []
+
+    def send(source, target):
+        outgoing.append(pltpu.make_async_copy(source, target, out_sem.at[len(outgoing)]))
+        outgoing[-1].start()
+
+    of = [slice(micro * length, (micro + 1) * length) for micro in range(MB)]
+    for micro in range(MB):
+        column = column_of(flat_ref[micro : micro + 1, :])
+
+        def placed(shift, column=column):
+            lanes = iota((length, 128), 1).astype(F32)
+            parts = [
+                jnp.where(column == lanes + float(first - shift), 1.0, 0.0).astype(BF16)
+                for first in range(0, slots, 128)
+            ]
+            return jnp.concatenate(parts, axis=1)
+
+        if micro == 2:
+            rows = rows_ref[:, width:]
+            embedded = jnp.concatenate([mm(placed(0), rows), mm(placed(4), rows)], axis=1)
+        else:
+            embedded = mm(placed(4 * micro), rows_ref[:, :width])
+        emb_ref[of[micro], :] = embedded.astype(BF16)
+        emb_t_ref[:, of[micro]] = jnp.transpose(embedded).astype(BF16)
+
+    for which, at in enumerate(chunks):
+        incoming[which].wait()
+        half = mm(emb_ref[...], w_in_ref[:, at]) * 0.5
         tanh = jnp.tanh(half)
         act = half + half * tanh
         hidden_ref[:, at] = act.astype(BF16)
         slope_ref[:, at] = (0.5 * ((1.0 + tanh) + act * (1.0 - tanh))).astype(BF16)
-
-    ends = []
-    total = 0
-    for which in range(3):
-        total = total + lengths_ref[micro, 0, which]
-        ends.append(total)
-
-    def segment(places):
-        return sum((places >= end).astype(I32) for end in ends)
-
-    query_at = iota((length, length), 0)
-    key_at = iota((length, length), 1)
-    allowed = (segment(query_at) == segment(key_at)) & (key_at <= query_at)
 
     lane = iota((1, 128), 1)
     first_head = (lane < 64).astype(F32)
@@ -219,174 +228,110 @@
     masks = (first_head.astype(BF16), second_head.astype(BF16))
     score_masks = ((first_head * 0.0625).astype(BF16), (second_head * 0.0625).astype(BF16))
     pairs = HEADS // 2
-    for pair in range(pairs):
-        lanes = slice(128 * pair, 128 * pair + 128)
-        value = hidden_ref[:, width + 128 * pair : width + 128 * pair + 128]
-        query = hidden_ref[:, 2 * width + 128 * pair : 2 * width + 128 * pair + 128]
-        key = hidden_ref[:, 3 * width + 128 * pair : 3 * width + 128 * pair + 128]
-        for head in range(2):
-            half = mm_nt(query * score_masks[head], key)
-            tanh = jnp.tanh(half)
-            act = half + half * tanh
-            at = slice(length * head, length * head + length)
-            weight_ref[pair, :, at] = jnp.where(allowed, act, 0.0).astype(BF16)
-            dsilu_ref[pair, :, at] = jnp.where(
-                allowed, (1.0 + tanh) + act * (1.0 - tanh), 0.0
-            ).astype(BF16)
-        both = jnp.concatenate([value * masks[0], value * masks[1]], axis=0)
-        att_ref[:, lanes] = mm(weight_ref[pair], both)
-
-    attended = att_ref[...]
-    centred = attended - jnp.mean(attended, axis=1, keepdims=True)
-    inverse = lax.rsqrt(jnp.mean(centred * centred, axis=1, keepdims=True) + 1e-05)
-    normed = centred * inverse
-    gate = hidden_ref[:, :width].astype(F32)
-    gated = normed * gate
-    gated_t_ref[...] = jnp.transpose(gated).astype(BF16)
-    stored("gated_t")
-    wait_out()
-    cot = cot()
-    out_ref[...] = (embedded + mm(gated.astype(BF16), w_out_ref[...])).astype(BF16)
-    stored("out")
-
-    dgated = mm_nt(cot, w_out_ref[...])
-    dgate = dgated * normed
-    dnormed = dgated * gate
-    dpre_ref[:, :width] = (dgate * slope_ref[:, :width].astype(F32)).astype(BF16)
-    shared = jnp.mean(dnormed * normed, axis=1, keepdims=True)
-    dcentred = inverse * (dnormed - normed * shared)
-    datt = dcentred - jnp.mean(dcentred, axis=1, keepdims=True)
-    datt_ref[...] = datt.astype(BF16)
-
-    for pair in range(pairs):
-        at_value = slice(width + 128 * pair, width + 128 * pair + 128)
-        at_query = slice(2 * width + 128 * pair, 2 * width + 128 * pair + 128)
-        at_key = slice(3 * width + 128 * pair, 3 * width + 128 * pair + 128)
-        value = hidden_ref[:, at_value]
-        query = hidden_ref[:, at_query]
-        key = hidden_ref[:, at_key]
-        dhead = datt_ref[:, 128 * pair : 128 * pair + 128]
-        parts = []
-        for head in range(2):
-            at = slice(length * head, length * head + length)
-            dweight = mm_nt(dhead * masks[head], value)
-            parts.append((dweight * dsilu_ref[pair, :, at].astype(F32)).astype(BF16))
-        dscore = jnp.concatenate(parts, axis=1)
-        both_keys = jnp.concatenate([key * score_masks[0], key * score_masks[1]], axis=0)
-        dquery = mm(dscore, both_keys)
-        dkeys = mm_tn(dscore, query * jnp.asarray(0.0625, BF16))
-        dkey = jnp.where(lane < 64, dkeys[:length], dkeys[length:])
-        dvalues = mm_tn(weight_ref[pair], dhead)
-        dvalue = jnp.where(lane < 64, dvalues[:length], dvalues[length:])
-        for at, grad in ((at_value, dvalue), (at_query, dquery), (at_key, dkey)):
-            dpre_ref[:, at] = (grad * slope_ref[:, at].astype(F32)).astype(BF16)
-
-    stored("dpre")
+    query_at = iota((length, length), 0)
+    key_at = iota((length, length), 1)
+    for micro in range(MB):
+        ends = []
+        total = 0
+        for which in range(3):
+            total = total + lengths_ref[micro, 0, which]
+            ends.append(total)
+
+        def segment(places, ends=ends):
+            return sum((places >= end).astype(I32) for end in ends)
+
+        allowed = (segment(query_at) == segment(key_at)) & (key_at <= query_at)
+        for pair in range(pairs):
+            first = 128 * pair
+            value = hidden_ref[of[micro], width + first : width + first + 128]
+            query = hidden_ref[of[micro], 2 * width + first : 2 * width + first + 128]
+            key = hidden_ref[of[micro], 3 * width + first : 3 * width + first + 128]
+            halves = mm_nt(both_heads(query, score_masks), key)
+            for head in range(2):
+                at = slice(length * head, length * head + length)
+                half = halves[at]
+                tanh = jnp.tanh(half)
+                act = half + half * tanh
+                weight_ref[micro * pairs + pair, :, at] = jnp.where(allowed, act, 0.0).astype(BF16)
+                dsilu_ref[micro * pairs + pair, :, at] = jnp.where(
+                    allowed, (1.0 + tanh) + act * (1.0 - tanh), 0.0
+                ).astype(BF16)
+            att_ref[of[micro], first : first + 128] = mm(
+                weight_ref[micro * pairs + pair], both_heads(value, masks)
+            )
+
+    incoming[-2].wait()
+    incoming[-1].wait()
+    cot = cot_ref[...].reshape(MB * length, width)
+    dgated_all = mm_nt(cot, w_out_ref[...])
+    gated_all = []
+    for micro in range(MB):
+        attended = att_ref[of[micro], :]
+        centred = attended - jnp.mean(attended, axis=1, keepdims=True)
+        inverse = lax.rsqrt(jnp.mean(centred * centred, axis=1, keepdims=True) + 1e-05)
+        normed = centred * inverse
+        gate = hidden_ref[of[micro], :width].astype(F32)
+        gated = normed * gate
+        gated_t_ref[:, of[micro]] = jnp.transpose(gated).astype(BF16)
+        gated_all.append(gated.astype(BF16))
+        dgated = dgated_all[of[micro]]
+        dgate = dgated * normed
+        dnormed = dgated * gate
+        dpre_ref[of[micro], :width] = (dgate * slope_ref[of[micro], :width].astype(F32)).astype(BF16)
+        shared = jnp.mean(dnormed * normed, axis=1, keepdims=True)
+        dcentred = inverse * (dnormed - normed * shared)
+        datt = dcentred - jnp.mean(dcentred, axis=1, keepdims=True)
+        datt_ref[of[micro], :] = datt.astype(BF16)
+    mixed = mm(jnp.concatenate(gated_all, axis=0), w_out_ref[...])
+    out_ref[...] = (emb_ref[...].astype(F32) + mixed).astype(BF16).reshape(out_ref.shape)
+    send(out_ref, out_hbm)
+
+    for micro in range(MB):
+        for pair in range(pairs):
+            first = 128 * pair
+            at_value = slice(width + first, width + first + 128)
+            at_query = slice(2 * width + first, 2 * width + first + 128)
+            at_key = slice(3 * width + first, 3 * width + first + 128)
+            value = hidden_ref[of[micro], at_value]
+            query = hidden_ref[of[micro], at_query]
+            key = hidden_ref[of[micro], at_key]
+            dhead = datt_ref[of[micro], first : first + 128]
+            dweights = mm_nt(both_heads(dhead, masks), value)
+            parts = []
+            for head in range(2):
+                at = slice(length * head, length * head + length)
+                parts.append((dweights[at] * dsilu_ref[micro * pairs + pair, :, at].astype(F32)).astype(BF16))
+            dscore = jnp.concatenate(parts, axis=1)
+            dquery = mm(dscore, both_heads(key, score_masks))
+            dkeys = mm_tn(dscore, query * jnp.asarray(0.0625, BF16))
+            dkey = jnp.where(lane < 64, dkeys[:length], dkeys[length:])
+            dvalues = mm_tn(weight_ref[micro * pairs + pair], dhead)
+            dvalue = jnp.where(lane < 64, dvalues[:length], dvalues[length:])
+            for at, grad in ((at_value, dvalue), (at_query, dquery), (at_key, dkey)):
+                dpre_ref[of[micro], at] = (grad * slope_ref[of[micro], at].astype(F32)).astype(BF16)
+
     grad_ref[...] = (cot.astype(F32) + mm_nt(dpre_ref[...], w_in_ref[...])).astype(BF16)
-
-
-def start_all(pairs, sem):
-    copies = [pltpu.make_async_copy(source, target, sem.at[k]) for k, (source, target) in enumerate(pairs)]
-    for copy in copies:
-        copy.start()
-    return copies
-
-
-def waiting(copies):
-    pending = list(copies)
-
-    def wait():
-        while pending:
-            pending.pop().wait()
-
-    return wait
-
-
-def column_chunks(source, target, chunk):
-    at = [pl.ds(first, chunk) for first in range(0, source.shape[1], chunk)]
-    return [(source.at[:, here], target.at[:, here]) for here in at]
-
-
-def layer_scratch(length, width):
-    pairs = HEADS // 2
-    return [
-        pltpu.VMEM((length, 4 * width), BF16),
-        pltpu.VMEM((length, 4 * width), BF16),
-        pltpu.VMEM((pairs, length, 2 * length), BF16),
-        pltpu.VMEM((pairs, length, 2 * length), BF16),
-        pltpu.VMEM((length, width), F32),
-        pltpu.VMEM((length, width), BF16),
-    ]
-
-
-def layers_kernel(half_ref, lengths_ref, flat_ref, rows_ref, w_in_hbm, w_out_hbm, cot_hbm, *rest):
-    out_hbm, sent_hbm, back_hbm, kept_ref = rest[:4]
-    w_in_ref, w_out_ref, cot_ref, out_ref, emb_t_ref, gated_t_ref, dpre_ref, grad_ref, sent_ref, back_ref = rest[4:14]
-    scratch, (in_sem, out_sem) = rest[14:20], rest[20:]
-    slots = rows_ref.shape[0]
-    width = w_out_ref.shape[0]
-    length = cot_hbm.shape[1]
-    width4 = w_in_ref.shape[1]
-    w_chunks = column_chunks(w_in_hbm, w_in_ref, 512)
-    at = [pl.ds(m * length, length) for m in range(MB)]
-    copies = start_all(
-        [*w_chunks, (w_out_hbm, w_out_ref)] + [(cot_hbm.at[m], cot_ref.at[at[m]]) for m in range(MB)], in_sem
-    )
-    waits = [waiting([copy]) for copy in copies]
-    outgoing = []
-
-    def send(source, target):
-        outgoing.append(pltpu.make_async_copy(source, target, out_sem.at[len(outgoing)]))
-        outgoing[-1].start()
-
-    for micro in range(MB):
-
-        def stored(name, micro=micro):
-            if name == "out":
-                send(out_ref.at[micro], out_hbm.at[micro])
-
-        def cot(micro=micro):
-            waits[5 + micro]()
-            return cot_ref[micro * length : (micro + 1) * length]
-
-        layer_body(
-            micro,
-            lengths_ref,
-            column_of(flat_ref[micro : micro + 1, :]),
-            rows_ref,
-            (w_in_ref, w_out_ref, lambda which: waits[which](), waits[4]),
-            cot,
-            (
-                out_ref.at[micro],
-                grad_ref.at[at[micro]],
-                emb_t_ref.at[:, at[micro]],
-                gated_t_ref.at[:, at[micro]],
-                dpre_ref.at[at[micro]],
-                stored,
-            ),
-            scratch,
-            micro == 2,
-        )
     groups, half, columns = sent_ref.shape
 
-    def weights(mine, put):
-        rows = pl.ds(pl.multiple_of(mine * half, half), half)
-        for group in range(groups):
-            first = group * columns
-            last = min(first + columns, width4)
-            part = mm(emb_t_ref[rows, :], dpre_ref[:, first:last]).astype(BF16)
-            if group == groups - 1:
-                part = jnp.concatenate([part, mm(gated_t_ref[rows, :], cot_ref[...]).astype(BF16)], axis=1)
-            put(group, part)
-
-    def put_sent(group, part):
-        sent_ref[group] = part
-        send(sent_ref.at[group], sent_hbm.at[group])
-
-    def put_kept(group, part):
-        kept_ref[group * half : (group + 1) * half, :] = part
-
-    weights(1 - half_ref[0], put_sent)
+    theirs = pl.ds(pl.multiple_of((1 - half_ref[0]) * half, half), half)
+    mine = pl.ds(pl.multiple_of(half_ref[0] * half, half), half)
+
+    def weights(left_ref, right, first):
+        left = jnp.concatenate([left_ref[theirs, :], left_ref[mine, :]], axis=0)
+        part = mm(left, right).astype(BF16)
+        start = first
+        while start < first + right.shape[1]:
+            group, inside = start // columns, start % columns
+            count = min(columns - inside, first + right.shape[1] - start)
+            here = part[:, start - first : start - first + count]
+            sent_ref[group, :, inside : inside + count] = here[:half]
+            kept_ref[group * half : (group + 1) * half, inside : inside + count] = here[half:]
+            start += count
+
+    for first in range(0, width4, 512):
+        weights(emb_t_ref, dpre_ref[:, first : first + 512], first)
+    weights(gated_t_ref, cot, width4)
+    send(sent_ref, sent_hbm)
     places = iota((slots, length), 0)
 
     def placing(micro, shift):
@@ -398,7 +343,6 @@
     halves = [grad_ref[2 * length :, : width // 2], grad_ref[2 * length :, width // 2 :]]
     back_ref[:, width:] = mm(last, jnp.concatenate(halves, axis=0)).astype(BF16)
     send(back_ref, back_hbm)
-    weights(half_ref[0], put_kept)
     for copy in outgoing:
         copy.wait()
 
@@ -421,7 +365,7 @@
             for shape in [
                 w_in.shape,
                 w_out.shape,
-                (MB * length, width),
+                cotangent.shape,
                 cotangent.shape,
                 (width, MB * length),
                 (width, MB * length),
@@ -429,10 +373,19 @@
                 (MB * length, width),
                 sent,
                 rows.shape,
+                (MB * length, width),
+                (MB * length, 4 * width),
+                (MB * length, 4 * width),
+                (MB * HEADS // 2, length, 2 * length),
+                (MB * HEADS // 2, length, 2 * length),
             ]
         ]
-        + layer_scratch(length, width)
-        + [pltpu.SemaphoreType.DMA((8,)), pltpu.SemaphoreType.DMA((8,))],
+        + [
+            pltpu.VMEM((MB * length, width), F32),
+            pltpu.VMEM((MB * length, width), BF16),
+            pltpu.SemaphoreType.DMA((10,)),
+            pltpu.SemaphoreType.DMA((3,)),
+        ],
         compiler_params=params(46),
         cost_estimate=cost(28_000_000_000, 10 * 1024 * 1024),
         name="layers",

time: 167 us -> 162 us (0.970)
  Pallas kernels: 47.4 us -> 42.6 us
    pallas_call x1, Pallas kernels: 25.1 us -> 20.2 us  [layers(): pl.pallas_call(layers_kernel, out_shape=[jax.ShapeDtypeStruct(shape, BF16...]
where the time goes in v3:
time: 162 us
  blocking collectives  63.5 us (39%)
  Pallas kernels  42.6 us (26%)
  waiting for transfers between devices  39.8 us (25%)
  starting transfers between devices  12.7 us (8%)
  local copies, waits for them, and re-layouts  2.72 us (2%)
    all_to_all x2, blocking collectives, trade(): lax.all_to_all(payload, AXES, split_axis=0, concat_axis=0, tiled=True)  63.5 us
    all_to_all x2, waiting for transfers between devices, trade(): lax.all_to_all(payload, AXES, split_axis=0, concat_axis=0, tiled=True)  36.9 us
    pallas_call x1, Pallas kernels, layers(): pl.pallas_call(layers_kernel, out_shape=[jax.ShapeDtypeStruct(shape, BF16...  20.2 us
    all_to_all x2, starting transfers between devices, trade(): lax.all_to_all(payload, AXES, split_axis=0, concat_axis=0, tiled=True)  10.1 us
    pallas_call x1, Pallas kernels, table_gradient(): pl.pallas_call(table_grad_kernel, out_shape=jax.ShapeDtypeStruct((own_row...  9 us
    pallas_call x1, Pallas kernels, gather(): pl.pallas_call(gather_kernel, out_shape=jax.ShapeDtypeStruct((devices * 8...  7.59 us
    pallas_call x2, Pallas kernels, finish(): pl.pallas_call(finish_kernel, out_shape=(jax.ShapeDtypeStruct((width, wid...  4.33 us
  transfers between devices with their start and end apart: 4, of which 4 were waited for; matrix products, arithmetic and copies ran while one was open for 0% of the time, Pallas kernels for 7%

profile of v3, /device:TPU:1, one launch (start us, length us, event | category | flops | bytes accessed | tf_op | source)
XLA Modules:
  0.0 162.0 jit_solution(14305836174312717072)
XLA Ops:
  0.6 0.0 copy-start.1
  0.6 0.7 copy-done.1
  1.3 0.0 copy-start.2
  1.3 0.7 copy-done.2
  2.0 0.7 requests.1
  2.7 21.1 %all_to_all.45 = s32[128,1,128]{2,1,0:T(1,128)} all-to-all(s32[128,1,128]{2,1,0:T(1,128)S(1)} %bitcast.22), channel_id=1, replica_groups=mesh['dp'=16,'table'=8] {'dp','table'}, dimensions={0} | all-to-all | bytes 131072 | tf_op jit(solution)/shard_map/all_to_all | solution.py:510
  23.9 7.6 %gather.1 = bf16[1024,768]{1,0:T(8,128)(2,1)} custom-call(s32[128,128]{1,0:T(8,128)} %bitcast.26, bf16[4096,512]{1,0:T(8,128)(2,1)} %table_hbm.1), custom_call_target="tpu_custom_call" | custom-call | flops 6000000000 | bytes 6291456 | tf_op jit(solution)/shard_map/gather/pallas_call | solution.py:145
  31.5 0.0 copy-start.3
  31.5 0.0 copy-start.4
  31.5 0.0 copy-start.5
  31.5 4.6 %all-to-all-start.1 = ((bf16[128,8,768]{2,1,0:T(8,128)(2,1)}), bf16[128,8,768]{2,1,0:T(8,128)(2,1)S(1)}, u32[]{:S(2)}, u32[]{:S(2)}) async-start(bf16[128,8,768]{2,1,0:T(8,128)(2,1)} %bitcast.25), calls=%async_computation.1 | async-start | bytes 3145728 | tf_op jit(solution)/shard_map/all_to_all | solution.py:510
  36.2 24.7 %all-to-all-done.1 = bf16[128,8,768]{2,1,0:T(8,128)(2,1)S(1)} async-done(((bf16[128,8,768]{2,1,0:T(8,128)(2,1)}), bf16[128,8,768]{2,1,0:T(8,128)(2,1)S(1)}, u32[]{:S(2)}, u32[]{:S(2)}) %all-to-all-start.1) | async-done | bytes 1572896 | tf_op jit(solution)/shard_map/all_to_all | solution.py:510
  60.9 0.0 copy-done.3
  60.9 0.0 copy-done.4
  60.9 0.0 copy-done.5
  60.9 20.2 %layers.1 = (bf16[3,256,512]{2,1,0:T(8,128)(2,1)}, bf16[4,256,640]{2,1,0:T(8,128)(2,1)S(1)}, bf16[1024,768]{1,0:T(8,128)(2,1)S(1)}, bf16[1024,640]{1,0:T(8,128)(2,1)S(1)}) custom-call(s32[1]{0:T(128)} %bitcast.half_ref, s32[3,1,4]{2,1,0:T(1,128)S(1)} %copy-done.5, s32[8,256]{1,0:T(8,128)S(1)} %get-tuple-element.16.flat_ref, bf16[1024,768]{1,0:T(8,128)(2,1)S(1)} %bitcast.20, ...), custom_call_target="tpu_custom_call" | custom-call | flops 28000000000 | bytes 10485760 | tf_op jit(solution)/shard_map/layers/pallas_call | solution.py:356
  81.1 1.3 collective-permute-start
  82.4 2.7 %collective-permute-done.other_ref = bf16[1024,640]{1,0:T(8,128)(2,1)S(1)} collective-permute-done((bf16[1024,640]{1,0:T(8,128)(2,1)S(1)}, bf16[1024,640]{1,0:T(8,128)(2,1)S(1)}, u32[]{:S(2)}, u32[]{:S(2)}) %collective-permute-start) | collective-permute-done | bytes 1310752 | tf_op jit(solution)/shard_map/ppermute | solution.py:529
  85.1 0.4 message.1
  85.5 42.3 %all_to_all.46 = bf16[128,8,1408]{2,1,0:T(8,128)(2,1)S(1)} all-to-all(bf16[128,8,1408]{2,1,0:T(8,128)(2,1)S(1)} %bitcast.16), channel_id=1, replica_groups=mesh['dp'=16,'table'=8] {'dp','table'}, dimensions={0} | all-to-all | bytes 5767168 | tf_op jit(solution)/shard_map/all_to_all | solution.py:510
  127.9 0.3 shard_sum.1
  128.1 0.0 copy-start
  128.1 1.0 copy-done
  129.2 0.0 copy-start.6
  129.2 5.5 %all-to-all-start.3 = ((bf16[128,8,640]{2,1,0:T(8,128)(2,1)}), bf16[128,8,640]{2,1,0:T(8,128)(2,1)}, u32[]{:S(2)}, u32[]{:S(2)}) async-start(bf16[128,8,640]{2,1,0:T(8,128)(2,1)} %bitcast.19), calls=%async_computation.3 | async-start | bytes 2621440 | tf_op jit(solution)/shard_map/all_to_all | solution.py:510
  134.6 0.0 copy-done.6
  134.6 0.1 slice.9
  134.7 0.1 reshape.40.pair_row_ref
  134.8 0.1 reshape.41.last_row_ref
  134.9 9.0 %table_grad.1 = f32[4096,512]{1,0:T(8,128)} custom-call(s32[1,1024]{1,0:T(1,128)S(1)} %reshape.40.pair_row_ref, s32[1,512]{1,0:T(1,128)S(1)} %reshape.41.last_row_ref, bf16[1024,1408]{1,0:T(8,128)(2,1)S(1)} %bitcast.18), custom_call_target="tpu_custom_call" | custom-call | flops 6442450944 | bytes 12582912 | tf_op jit(solution)/shard_map/table_grad/pallas_call | solution.py:460
  143.9 12.2 %all-to-all-done.3 = bf16[128,8,640]{2,1,0:T(8,128)(2,1)} async-done(((bf16[128,8,640]{2,1,0:T(8,128)(2,1)}), bf16[128,8,640]{2,1,0:T(8,128)(2,1)}, u32[]{:S(2)}, u32[]{:S(2)}) %all-to-all-start.3) | async-done | bytes 1310752 | tf_op jit(solution)/shard_map/all_to_all | solution.py:510
  156.2 1.3 collective-permute-start.1
  157.5 2.6 %finish0.1 = (f32[512,2048]{1,0:T(8,128)}, f32[512,512]{1,0:T(8,128)}) custom-call(s32[1]{0:T(128)} %bitcast.half_ref, bf16[4,256,640]{2,1,0:T(8,128)(2,1)} %bitcast.13.in_ref), custom_call_target="tpu_custom_call" | custom-call | flops 1000000 | bytes 4194304 | tf_op jit(solution)/shard_map/finish0/pallas_call | solution.py:489
  160.1 0.2 collective-permute-done.1
  160.3 1.7 %finish2.1 = (f32[512,2048]{1,0:T(8,128)}, f32[512,512]{1,0:T(8,128)}) custom-call(s32[1]{0:T(128)S(6)} %sub.3.half_ref, bf16[4,256,640]{2,1,0:T(8,128)(2,1)S(1)} %bitcast.21, f32[512,2048]{1,0:T(8,128)} %get-tuple-element.24.rest_0_, f32[512,512]{1,0:T(8,128)} %get-tuple-element.25.rest_1_), custom_call_target="tpu_custom_call", output_to_operand_aliasing={{0}: (2, {}), {1}: (3, {})} | custom-call | flops 1000000 | bytes 4194304 | tf_op jit(solution)/shard_map/finish2/pallas_call | solution.py:489
Async XLA Ops:
  0.6 0.7 copy-start.1
  1.3 0.7 copy-start.2
  31.5 29.4 %copy-start.3 = (bf16[3,256,512]{2,1,0:T(8,128)(2,1)S(1)}, bf16[3,256,512]{2,1,0:T(8,128)(2,1)}, u32[]{:S(2)}) copy-start(bf16[3,256,512]{2,1,0:T(8,128)(2,1)} %cot_hbm.1) | copy-start | bytes 2359300
  31.5 29.4 %copy-start.4 = (bf16[512,512]{1,0:T(8,128)(2,1)S(1)}, bf16[512,512]{1,0:T(8,128)(2,1)}, u32[]{:S(2)}) copy-start(bf16[512,512]{1,0:T(8,128)(2,1)} %w_out_hbm.1) | copy-start | bytes 1572868
  31.5 29.4 %copy-start.5 = (s32[3,1,4]{2,1,0:T(1,128)S(1)}, s32[3,1,4]{2,1,0:T(1,128)}, u32[]{:S(2)}) copy-start(s32[3,1,4]{2,1,0:T(1,128)} %lengths_ref.1) | copy-start | bytes 148
  31.5 29.3 %all-to-all-start.1 = ((bf16[128,8,768]{2,1,0:T(8,128)(2,1)}), bf16[128,8,768]{2,1,0:T(8,128)(2,1)S(1)}, u32[]{:S(2)}, u32[]{:S(2)}) async-start(bf16[128,8,768]{2,1,0:T(8,128)(2,1)} %bitcast.25), calls=%async_computation.1 | async-start | bytes 3145728 | tf_op jit(solution)/shard_map/all_to_all | solution.py:510
  81.1 4.0 %collective-permute-start = (bf16[1024,640]{1,0:T(8,128)(2,1)S(1)}, bf16[1024,640]{1,0:T(8,128)(2,1)S(1)}, u32[]{:S(2)}, u32[]{:S(2)}) collective-permute-start(bf16[1024,640]{1,0:T(8,128)(2,1)S(1)} %bitcast.24), channel_id=1, source_target_pairs={{0,1},{1,0},{2,3},{3,2},{4,5},{5,4},{6,7},{7,6},{8,9},{9,8},{10,11... | collective-permute-start | bytes 3932168 | tf_op jit(solution)/shard_map/ppermute | solution.py:529
  128.1 1.1 copy-start
  129.2 5.5 %copy-start.6 = (s32[128,1,128]{2,1,0:T(1,128)S(1)}, s32[128,1,128]{2,1,0:T(1,128)}, u32[]{:S(2)}) copy-start(s32[128,1,128]{2,1,0:T(1,128)} %all_to_all.45) | copy-start | bytes 196612
  129.2 27.0 %all-to-all-start.3 = ((bf16[128,8,640]{2,1,0:T(8,128)(2,1)}), bf16[128,8,640]{2,1,0:T(8,128)(2,1)}, u32[]{:S(2)}, u32[]{:S(2)}) async-start(bf16[128,8,640]{2,1,0:T(8,128)(2,1)} %bitcast.19), calls=%async_computation.3 | async-start | bytes 2621440 | tf_op jit(solution)/shard_map/all_to_all | solution.py:510
  156.2 4.2 %collective-permute-start.1 = (bf16[1024,640]{1,0:T(8,128)(2,1)}, bf16[1024,640]{1,0:T(8,128)(2,1)S(1)}, u32[]{:S(2)}, u32[]{:S(2)}) collective-permute-start(bf16[1024,640]{1,0:T(8,128)(2,1)} %bitcast.11), channel_id=1, source_target_pairs={{0,1},{1,0},{2,3},{3,2},{4,5},{5,4},{6,7},{7,6},{8,9},{9,8},{10,11... | collective-permute-start | bytes 3932168 | tf_op jit(solution)/shard_map/ppermute | solution.py:535

commit v4 on v3

--- a/solution.py
+++ b/solution.py
@@ -5,12 +5,13 @@
 from jax import lax
 from jax.experimental import pallas as pl
 from jax.experimental.pallas import tpu as pltpu
+from jax.sharding import Mesh
 from jax.sharding import PartitionSpec as P
 
 HEADS = 8
 MB = 3
 CAP = 4
-AXES = ("dp", "table")
+AXES = ("dp", "y", "core")
 F32 = jnp.float32
 BF16 = jnp.bfloat16
 I32 = jnp.int32
@@ -470,54 +471,58 @@
     )(pair_row, last_row, arrived)
 
 
-def finish_kernel(half_ref, in_ref, *rest):
-    del half_ref
+def finish_kernel(core_ref, in_ref, *rest):
+    del core_ref
     win_ref, wout_ref = rest[-2:]
-    groups, _, columns = in_ref.shape
-    width4 = win_ref.shape[1]
+    groups, _, _, columns = in_ref.shape
+    width4 = win_ref.shape[-1]
     for group in range(groups):
         first = group * columns
         last = min(first + columns, width4)
-        win_ref[:, first:last] = in_ref[group, :, : last - first].astype(F32)
-    wout_ref[...] = in_ref[groups - 1, :, width4 - (groups - 1) * columns :].astype(F32)
-
-
-def finish(half_index, part, before, width, width4):
-    half = width // 2
-    shape = part.shape
+        part = in_ref[group].astype(F32)
+        for half in range(2):
+            rows = part[:, 8 * half : 8 * half + 8]
+            win_ref[half, :, 0, :, first:last] = rows[:, :, : last - first]
+            if group == groups - 1:
+                wout_ref[half, :, 0] = rows[:, :, last - first :]
+
+
+def finish(core, part, before, width, width4):
+    across = width // 32
+    part = part.reshape(4, across, 16, part.shape[1])
     steps = 2
+    block = across // steps
+    shapes = [(2, across, 2, 8, width4), (2, across, 2, 8, width)]
     return pl.pallas_call(
         finish_kernel,
-        out_shape=(jax.ShapeDtypeStruct((width, width4), F32), jax.ShapeDtypeStruct((width, width), F32)),
+        out_shape=[jax.ShapeDtypeStruct(shape, F32) for shape in shapes],
         grid_spec=pltpu.PrefetchScalarGridSpec(
             num_scalar_prefetch=1,
             grid=(steps,),
-            in_specs=[pl.BlockSpec((shape[0], shape[1] // steps, shape[2]), lambda i, which: (0, i, 0))]
+            in_specs=[pl.BlockSpec((4, block, 16, part.shape[3]), lambda i, which: (0, i, 0, 0))]
             + [pl.BlockSpec(memory_space=pl.ANY)] * len(before),
-            out_specs=(
-                pl.BlockSpec((half // steps, width4), lambda i, which: (which[0] * steps + i, 0)),
-                pl.BlockSpec((half // steps, width), lambda i, which: (which[0] * steps + i, 0)),
-            ),
+            out_specs=[
+                pl.BlockSpec((2, block, 1, 8, shape[4]), lambda i, which: (0, i, which[0], 0, 0)) for shape in shapes
+            ],
         ),
         input_output_aliases={2: 0, 3: 1} if before else {},
         compiler_params=params(16),
         cost_estimate=cost(1_000_000, 4 * 1024 * 1024),
         name=f"finish{len(before)}",
-    )(half_index, part, *before)
-
-
-def trade(payload):
-    return lax.all_to_all(payload, AXES, split_axis=0, concat_axis=0, tiled=True)
+    )(core, part, *before)
+
+
+def trade(payload, axes=AXES):
+    return lax.all_to_all(payload, axes, split_axis=0, concat_axis=0, tiled=True)
 
 
 def shards(table, w_in, w_out, item_owner, item_slot, seq_lengths, cotangent):
-    table_axis = lax.axis_size("table")
-    owners_n = lax.axis_size("dp") * table_axis
+    owners_n = lax.axis_size(AXES)
     length = item_slot.shape[1]
     own_rows, width = table.shape
     slots = owners_n * 8
-    core = (lax.axis_index("table") % 2).astype(I32).reshape(1)
-    swap = [(i, i ^ 1) for i in range(table_axis)]
+    core = lax.axis_index("core").astype(I32).reshape(1)
+    swap = [(0, 1), (1, 0)]
 
     wanted, flat = requests(item_owner.reshape(MB, 1, length), item_slot, owners_n)
     asked = trade(wanted)
@@ -526,20 +531,22 @@
     last_row = asked[:, 8:12].reshape(1, slots // 2)
     out, sent, back, kept = layers(core, seq_lengths, flat, rows, w_in, w_out, cotangent)
     columns = sent.shape[2]
-    other = lax.ppermute(sent.reshape(slots, columns), "table", swap)
+    other = lax.ppermute(sent.reshape(slots, columns), "core", swap)
     arrived = trade(message(back, kept, other))
     factor = (MB * length * owners_n) ** (-0.5)
-    mine_full = trade(shard_sum(arrived, rows.shape[1], factor))
+    mine_full = trade(shard_sum(arrived, rows.shape[1], factor), AXES[:2])
     table_grad = table_gradient(pair_row, last_row, arrived, own_rows, width)
     mine_full, table_grad = lax.optimization_barrier((mine_full, table_grad))
-    other_full = lax.ppermute(mine_full, "table", swap)
-    shape = (4, width // 2, columns)
-    partial = finish(core, mine_full.reshape(shape), (), width, w_in.shape[1])
-    win_grad, wout_grad = finish(1 - core, other_full.reshape(shape), partial, width, w_in.shape[1])
-    return out, table_grad, win_grad, wout_grad
+    other_full = lax.ppermute(mine_full, "core", swap)
+    width4 = w_in.shape[1]
+    partial = finish(core, mine_full, (), width, width4)
+    win_grad, wout_grad = finish(1 - core, other_full, partial, width, width4)
+    return out, table_grad, win_grad.reshape(width, width4), wout_grad.reshape(width, width)
 
 
 def solution(mesh):
+    dp, table_axis = mesh.devices.shape
+    mesh = Mesh(mesh.devices.reshape(dp, table_axis // 2, 2), AXES)
     in_specs = (
         P(AXES, None),
         P(),

time: 162 us -> 162 us (level)
  waiting for transfers between devices: 39.8 us -> 38 us
    all_to_all x2, waiting for transfers between devices: 36.9 us -> 35.1 us  [trade(): lax.all_to_all(payload, axes, split_axis=0, concat_axis=0, tiled=True)]
where the time goes in v4:
time: 162 us
  blocking collectives  63.5 us (39%)
  Pallas kernels  42.6 us (26%)
  waiting for transfers between devices  38 us (23%)
  starting transfers between devices  14.1 us (9%)
  local copies, waits for them, and re-layouts  2.72 us (2%)
    all_to_all x2, blocking collectives, trade(): lax.all_to_all(payload, axes, split_axis=0, concat_axis=0, tiled=True)  63.5 us
    all_to_all x2, waiting for transfers between devices, trade(): lax.all_to_all(payload, axes, split_axis=0, concat_axis=0, tiled=True)  35.1 us
    pallas_call x1, Pallas kernels, layers(): pl.pallas_call(layers_kernel, out_shape=[jax.ShapeDtypeStruct(shape, BF16...  20.2 us
    all_to_all x2, starting transfers between devices, trade(): lax.all_to_all(payload, axes, split_axis=0, concat_axis=0, tiled=True)  10.3 us
    pallas_call x1, Pallas kernels, table_gradient(): pl.pallas_call(table_grad_kernel, out_shape=jax.ShapeDtypeStruct((own_row...  9 us
    pallas_call x1, Pallas kernels, gather(): pl.pallas_call(gather_kernel, out_shape=jax.ShapeDtypeStruct((devices * 8...  7.59 us
    pallas_call x2, Pallas kernels, finish(): pl.pallas_call(finish_kernel, out_shape=[jax.ShapeDtypeStruct(shape, F32)...  4.37 us
  transfers between devices with their start and end apart: 4, of which 4 were waited for; matrix products, arithmetic and copies ran while one was open for 0% of the time, Pallas kernels for 7%

profile of v4, /device:TPU:1, one launch (start us, length us, event | category | flops | bytes accessed | tf_op | source)
XLA Modules:
  0.0 161.7 jit_solution(13133214894273875542)
XLA Ops:
  0.6 0.0 copy-start.1
  0.6 0.7 copy-done.1
  1.3 0.0 copy-start.2
  1.3 0.7 copy-done.2
  2.0 0.7 requests.1
  2.7 21.1 %all_to_all.45 = s32[128,1,128]{2,1,0:T(1,128)} all-to-all(s32[128,1,128]{2,1,0:T(1,128)S(1)} %bitcast.24), channel_id=1, replica_groups=mesh['dp'=16,'y'=4,'core'=2] {'dp','y','core'}, dimensions={0} | all-to-all | bytes 131072 | tf_op jit(solution)/shard_map/all_to_all | solution.py:516
  23.9 7.6 %gather.1 = bf16[1024,768]{1,0:T(8,128)(2,1)} custom-call(s32[128,128]{1,0:T(8,128)} %bitcast.30, bf16[4096,512]{1,0:T(8,128)(2,1)} %table_hbm.1), custom_call_target="tpu_custom_call" | custom-call | flops 6000000000 | bytes 6291456 | tf_op jit(solution)/shard_map/gather/pallas_call | solution.py:146
  31.5 0.0 copy-start.3
  31.5 0.0 copy-start.4
  31.5 0.0 copy-start.5
  31.5 4.6 %all-to-all-start.1 = ((bf16[128,8,768]{2,1,0:T(8,128)(2,1)}), bf16[128,8,768]{2,1,0:T(8,128)(2,1)S(1)}, u32[]{:S(2)}, u32[]{:S(2)}) async-start(bf16[128,8,768]{2,1,0:T(8,128)(2,1)} %bitcast.28), calls=%async_computation.1 | async-start | bytes 3145728 | tf_op jit(solution)/shard_map/all_to_all | solution.py:516
  36.2 24.7 %all-to-all-done.1 = bf16[128,8,768]{2,1,0:T(8,128)(2,1)S(1)} async-done(((bf16[128,8,768]{2,1,0:T(8,128)(2,1)}), bf16[128,8,768]{2,1,0:T(8,128)(2,1)S(1)}, u32[]{:S(2)}, u32[]{:S(2)}) %all-to-all-start.1) | async-done | bytes 1572896 | tf_op jit(solution)/shard_map/all_to_all | solution.py:516
  60.9 0.0 copy-done.3
  60.9 0.0 copy-done.4
  60.9 0.0 copy-done.5
  60.9 20.2 %layers.1 = (bf16[3,256,512]{2,1,0:T(8,128)(2,1)}, bf16[4,256,640]{2,1,0:T(8,128)(2,1)S(1)}, bf16[1024,768]{1,0:T(8,128)(2,1)S(1)}, bf16[1024,640]{1,0:T(8,128)(2,1)S(1)}) custom-call(s32[1]{0:T(128)} %bitcast.half_ref.core_ref, s32[3,1,4]{2,1,0:T(1,128)S(1)} %copy-done.5, s32[8,256]{1,0:T(8,128)S(1)} %get-tuple-element.16.flat_ref, ...), custom_call_target="tpu_custom_call" | custom-call | flops 28000000000 | bytes 10485760 | tf_op jit(solution)/shard_map/layers/pallas_call | solution.py:357
  81.1 1.3 collective-permute-start
  82.4 2.7 %collective-permute-done.other_ref = bf16[1024,640]{1,0:T(8,128)(2,1)S(1)} collective-permute-done((bf16[1024,640]{1,0:T(8,128)(2,1)S(1)}, bf16[1024,640]{1,0:T(8,128)(2,1)S(1)}, u32[]{:S(2)}, u32[]{:S(2)}) %collective-permute-start) | collective-permute-done | bytes 1310752 | tf_op jit(solution)/shard_map/ppermute | solution.py:534
  85.1 0.4 message.1
  85.5 42.3 %all_to_all.46 = bf16[128,8,1408]{2,1,0:T(8,128)(2,1)S(1)} all-to-all(bf16[128,8,1408]{2,1,0:T(8,128)(2,1)S(1)} %bitcast.18), channel_id=1, replica_groups=mesh['dp'=16,'y'=4,'core'=2] {'dp','y','core'}, dimensions={0} | all-to-all | bytes 5767168 | tf_op jit(solution)/shard_map/all_to_all | solution.py:516
  127.9 0.3 shard_sum.1
  128.1 0.0 copy-start
  128.1 1.0 copy-done
  129.2 0.0 copy-start.6
  129.2 5.6 %all-to-all-start.3 = ((bf16[64,16,640]{2,1,0:T(8,128)(2,1)}), bf16[64,16,640]{2,1,0:T(8,128)(2,1)}, u32[]{:S(2)}, u32[]{:S(2)}) async-start(bf16[64,16,640]{2,1,0:T(8,128)(2,1)} %bitcast.21), calls=%async_computation.3 | async-start | bytes 2621440 | tf_op jit(solution)/shard_map/all_to_all | solution.py:516
  134.8 0.0 copy-done.6
  134.8 0.1 slice.9
  134.9 0.1 reshape.46.pair_row_ref
  135.0 0.1 reshape.47.last_row_ref
  135.1 9.0 %table_grad.1 = f32[4096,512]{1,0:T(8,128)} custom-call(s32[1,1024]{1,0:T(1,128)S(1)} %reshape.46.pair_row_ref, s32[1,512]{1,0:T(1,128)S(1)} %reshape.47.last_row_ref, bf16[1024,1408]{1,0:T(8,128)(2,1)S(1)} %bitcast.20), custom_call_target="tpu_custom_call" | custom-call | flops 6442450944 | bytes 12582912 | tf_op jit(solution)/shard_map/table_grad/pallas_call | solution.py:461
  144.1 10.4 %all-to-all-done.3 = bf16[64,16,640]{2,1,0:T(8,128)(2,1)} async-done(((bf16[64,16,640]{2,1,0:T(8,128)(2,1)}), bf16[64,16,640]{2,1,0:T(8,128)(2,1)}, u32[]{:S(2)}, u32[]{:S(2)}) %all-to-all-start.3) | async-done | bytes 1310752 | tf_op jit(solution)/shard_map/all_to_all | solution.py:516
  154.5 2.5 %collective-permute-start.1 = (bf16[1024,640]{1,0:T(8,128)(2,1)}, bf16[1024,640]{1,0:T(8,128)(2,1)S(1)}, u32[]{:S(2)}, u32[]{:S(2)}) collective-permute-start(bf16[1024,640]{1,0:T(8,128)(2,1)} %bitcast.11), channel_id=1, source_target_pairs={{0,1},{1,0},{2,3},{3,2},{4,5},{5,4},{6,7},{7,6},{8,9},{9,8},{10,11... | collective-permute-start | bytes 3932168 | tf_op jit(solution)/shard_map/ppermute | solution.py:540
  157.1 2.7 %finish0.1 = (f32[2,16,2,8,2048]{4,3,2,1,0:T(8,128)}, f32[2,16,2,8,512]{4,3,2,1,0:T(8,128)}) custom-call(s32[1]{0:T(128)} %bitcast.half_ref.core_ref, bf16[4,16,16,640]{3,2,1,0:T(8,128)(2,1)} %bitcast.13.in_ref), custom_call_target="tpu_custom_call" | custom-call | flops 1000000 | bytes 4194304 | tf_op jit(solution)/shard_map/finish0/pallas_call | solution.py:496
  159.7 0.2 collective-permute-done.1
  159.9 1.7 %finish2.1 = (f32[2,16,2,8,2048]{4,3,2,1,0:T(8,128)}, f32[2,16,2,8,512]{4,3,2,1,0:T(8,128)}) custom-call(s32[1]{0:T(128)S(6)} %sub.3.core_ref, bf16[4,16,16,640]{3,2,1,0:T(8,128)(2,1)S(1)} %bitcast.23, f32[2,16,2,8,2048]{4,3,2,1,0:T(8,128)} %get-tuple-element.24.rest_0_, ...), custom_call_target="tpu_custom_call", output_to_operand_aliasing={{0}: (2, {}), {1}: (3, {})} | custom-call | flops 1000000 | bytes 4194304 | tf_op jit(solution)/shard_map/finish2/pallas_call | solution.py:496
Async XLA Ops:
  0.6 0.7 copy-start.1
  1.3 0.7 copy-start.2
  31.5 29.4 %copy-start.3 = (bf16[3,256,512]{2,1,0:T(8,128)(2,1)S(1)}, bf16[3,256,512]{2,1,0:T(8,128)(2,1)}, u32[]{:S(2)}) copy-start(bf16[3,256,512]{2,1,0:T(8,128)(2,1)} %cot_hbm.1) | copy-start | bytes 2359300
  31.5 29.4 %copy-start.4 = (bf16[512,512]{1,0:T(8,128)(2,1)S(1)}, bf16[512,512]{1,0:T(8,128)(2,1)}, u32[]{:S(2)}) copy-start(bf16[512,512]{1,0:T(8,128)(2,1)} %w_out_hbm.1) | copy-start | bytes 1572868
  31.5 29.4 %copy-start.5 = (s32[3,1,4]{2,1,0:T(1,128)S(1)}, s32[3,1,4]{2,1,0:T(1,128)}, u32[]{:S(2)}) copy-start(s32[3,1,4]{2,1,0:T(1,128)} %lengths_ref.1) | copy-start | bytes 148
  31.5 29.3 %all-to-all-start.1 = ((bf16[128,8,768]{2,1,0:T(8,128)(2,1)}), bf16[128,8,768]{2,1,0:T(8,128)(2,1)S(1)}, u32[]{:S(2)}, u32[]{:S(2)}) async-start(bf16[128,8,768]{2,1,0:T(8,128)(2,1)} %bitcast.28), calls=%async_computation.1 | async-start | bytes 3145728 | tf_op jit(solution)/shard_map/all_to_all | solution.py:516
  81.1 4.0 %collective-permute-start = (bf16[1024,640]{1,0:T(8,128)(2,1)S(1)}, bf16[1024,640]{1,0:T(8,128)(2,1)S(1)}, u32[]{:S(2)}, u32[]{:S(2)}) collective-permute-start(bf16[1024,640]{1,0:T(8,128)(2,1)S(1)} %bitcast.26), channel_id=1, source_target_pairs={{0,1},{1,0},{2,3},{3,2},{4,5},{5,4},{6,7},{7,6},{8,9},{9,8},{10,11... | collective-permute-start | bytes 3932168 | tf_op jit(solution)/shard_map/ppermute | solution.py:534
  128.1 1.1 copy-start
  129.2 5.6 %copy-start.6 = (s32[128,1,128]{2,1,0:T(1,128)S(1)}, s32[128,1,128]{2,1,0:T(1,128)}, u32[]{:S(2)}) copy-start(s32[128,1,128]{2,1,0:T(1,128)} %all_to_all.45) | copy-start | bytes 196612
  129.2 25.4 %all-to-all-start.3 = ((bf16[64,16,640]{2,1,0:T(8,128)(2,1)}), bf16[64,16,640]{2,1,0:T(8,128)(2,1)}, u32[]{:S(2)}, u32[]{:S(2)}) async-start(bf16[64,16,640]{2,1,0:T(8,128)(2,1)} %bitcast.21), calls=%async_computation.3 | async-start | bytes 2621440 | tf_op jit(solution)/shard_map/all_to_all | solution.py:516
  154.5 5.4 %collective-permute-start.1 = (bf16[1024,640]{1,0:T(8,128)(2,1)}, bf16[1024,640]{1,0:T(8,128)(2,1)S(1)}, u32[]{:S(2)}, u32[]{:S(2)}) collective-permute-start(bf16[1024,640]{1,0:T(8,128)(2,1)} %bitcast.11), channel_id=1, source_target_pairs={{0,1},{1,0},{2,3},{3,2},{4,5},{5,4},{6,7},{7,6},{8,9},{9,8},{10,11... | collective-permute-start | bytes 3932168 | tf_op jit(solution)/shard_map/ppermute | solution.py:540

commit v5 on v4

--- a/solution.py
+++ b/solution.py
@@ -317,8 +317,10 @@
     theirs = pl.ds(pl.multiple_of((1 - half_ref[0]) * half, half), half)
     mine = pl.ds(pl.multiple_of(half_ref[0] * half, half), half)
 
-    def weights(left_ref, right, first):
-        left = jnp.concatenate([left_ref[theirs, :], left_ref[mine, :]], axis=0)
+    def split_rows(ref):
+        return jnp.concatenate([ref[theirs, :], ref[mine, :]], axis=0)
+
+    def weights(left, right, first):
         part = mm(left, right).astype(BF16)
         start = first
         while start < first + right.shape[1]:
@@ -329,9 +331,10 @@
             kept_ref[group * half : (group + 1) * half, inside : inside + count] = here[half:]
             start += count
 
+    left = split_rows(emb_t_ref)
     for first in range(0, width4, 512):
-        weights(emb_t_ref, dpre_ref[:, first : first + 512], first)
-    weights(gated_t_ref, cot, width4)
+        weights(left, dpre_ref[:, first : first + 512], first)
+    weights(split_rows(gated_t_ref), cot, width4)
     send(sent_ref, sent_hbm)
     places = iota((slots, length), 0)
 

time: 162 us -> 162 us (level)
  no operation moved by 1% of the time
where the time goes in v5:
time: 162 us
  blocking collectives  63.5 us (39%)
  Pallas kernels  42.6 us (26%)
  waiting for transfers between devices  38 us (23%)
  starting transfers between devices  14.1 us (9%)
  local copies, waits for them, and re-layouts  2.72 us (2%)
    all_to_all x2, blocking collectives, trade(): lax.all_to_all(payload, axes, split_axis=0, concat_axis=0, tiled=True)  63.5 us
    all_to_all x2, waiting for transfers between devices, trade(): lax.all_to_all(payload, axes, split_axis=0, concat_axis=0, tiled=True)  35.1 us
    pallas_call x1, Pallas kernels, layers(): pl.pallas_call(layers_kernel, out_shape=[jax.ShapeDtypeStruct(shape, BF16...  20.2 us
    all_to_all x2, starting transfers between devices, trade(): lax.all_to_all(payload, axes, split_axis=0, concat_axis=0, tiled=True)  10.3 us
    pallas_call x1, Pallas kernels, table_gradient(): pl.pallas_call(table_grad_kernel, out_shape=jax.ShapeDtypeStruct((own_row...  9 us
    pallas_call x1, Pallas kernels, gather(): pl.pallas_call(gather_kernel, out_shape=jax.ShapeDtypeStruct((devices * 8...  7.59 us
    pallas_call x2, Pallas kernels, finish(): pl.pallas_call(finish_kernel, out_shape=[jax.ShapeDtypeStruct(shape, F32)...  4.37 us
  transfers between devices with their start and end apart: 4, of which 4 were waited for; matrix products, arithmetic and copies ran while one was open for 0% of the time, Pallas kernels for 7%

profile of v5, /device:TPU:1, one launch (start us, length us, event | category | flops | bytes accessed | tf_op | source)
XLA Modules:
  0.0 161.7 jit_solution(13850310756969501464)
XLA Ops:
  0.6 0.0 copy-start.1
  0.6 0.7 copy-done.1
  1.3 0.0 copy-start.2
  1.3 0.7 copy-done.2
  2.0 0.7 requests.1
  2.7 21.1 %all_to_all.45 = s32[128,1,128]{2,1,0:T(1,128)} all-to-all(s32[128,1,128]{2,1,0:T(1,128)S(1)} %bitcast.24), channel_id=1, replica_groups=mesh['dp'=16,'y'=4,'core'=2] {'dp','y','core'}, dimensions={0} | all-to-all | bytes 131072 | tf_op jit(solution)/shard_map/all_to_all | solution.py:519
  23.9 7.6 %gather.1 = bf16[1024,768]{1,0:T(8,128)(2,1)} custom-call(s32[128,128]{1,0:T(8,128)} %bitcast.30, bf16[4096,512]{1,0:T(8,128)(2,1)} %table_hbm.1), custom_call_target="tpu_custom_call" | custom-call | flops 6000000000 | bytes 6291456 | tf_op jit(solution)/shard_map/gather/pallas_call | solution.py:146
  31.5 0.0 copy-start.3
  31.5 0.0 copy-start.4
  31.5 0.0 copy-start.5
  31.5 4.6 %all-to-all-start.1 = ((bf16[128,8,768]{2,1,0:T(8,128)(2,1)}), bf16[128,8,768]{2,1,0:T(8,128)(2,1)S(1)}, u32[]{:S(2)}, u32[]{:S(2)}) async-start(bf16[128,8,768]{2,1,0:T(8,128)(2,1)} %bitcast.28), calls=%async_computation.1 | async-start | bytes 3145728 | tf_op jit(solution)/shard_map/all_to_all | solution.py:519
  36.2 24.7 %all-to-all-done.1 = bf16[128,8,768]{2,1,0:T(8,128)(2,1)S(1)} async-done(((bf16[128,8,768]{2,1,0:T(8,128)(2,1)}), bf16[128,8,768]{2,1,0:T(8,128)(2,1)S(1)}, u32[]{:S(2)}, u32[]{:S(2)}) %all-to-all-start.1) | async-done | bytes 1572896 | tf_op jit(solution)/shard_map/all_to_all | solution.py:519
  60.9 0.0 copy-done.3
  60.9 0.0 copy-done.4
  60.9 0.0 copy-done.5
  60.9 20.2 %layers.1 = (bf16[3,256,512]{2,1,0:T(8,128)(2,1)}, bf16[4,256,640]{2,1,0:T(8,128)(2,1)S(1)}, bf16[1024,768]{1,0:T(8,128)(2,1)S(1)}, bf16[1024,640]{1,0:T(8,128)(2,1)S(1)}) custom-call(s32[1]{0:T(128)} %bitcast.half_ref.core_ref, s32[3,1,4]{2,1,0:T(1,128)S(1)} %copy-done.5, s32[8,256]{1,0:T(8,128)S(1)} %get-tuple-element.16.flat_ref, ...), custom_call_target="tpu_custom_call" | custom-call | flops 28000000000 | bytes 10485760 | tf_op jit(solution)/shard_map/layers/pallas_call | solution.py:360
  81.1 1.3 collective-permute-start
  82.4 2.7 %collective-permute-done.other_ref = bf16[1024,640]{1,0:T(8,128)(2,1)S(1)} collective-permute-done((bf16[1024,640]{1,0:T(8,128)(2,1)S(1)}, bf16[1024,640]{1,0:T(8,128)(2,1)S(1)}, u32[]{:S(2)}, u32[]{:S(2)}) %collective-permute-start) | collective-permute-done | bytes 1310752 | tf_op jit(solution)/shard_map/ppermute | solution.py:537
  85.1 0.4 message.1
  85.5 42.3 %all_to_all.46 = bf16[128,8,1408]{2,1,0:T(8,128)(2,1)S(1)} all-to-all(bf16[128,8,1408]{2,1,0:T(8,128)(2,1)S(1)} %bitcast.18), channel_id=1, replica_groups=mesh['dp'=16,'y'=4,'core'=2] {'dp','y','core'}, dimensions={0} | all-to-all | bytes 5767168 | tf_op jit(solution)/shard_map/all_to_all | solution.py:519
  127.9 0.3 shard_sum.1
  128.1 0.0 copy-start
  128.1 1.0 copy-done
  129.2 0.0 copy-start.6
  129.2 5.6 %all-to-all-start.3 = ((bf16[64,16,640]{2,1,0:T(8,128)(2,1)}), bf16[64,16,640]{2,1,0:T(8,128)(2,1)}, u32[]{:S(2)}, u32[]{:S(2)}) async-start(bf16[64,16,640]{2,1,0:T(8,128)(2,1)} %bitcast.21), calls=%async_computation.3 | async-start | bytes 2621440 | tf_op jit(solution)/shard_map/all_to_all | solution.py:519
  134.8 0.0 copy-done.6
  134.8 0.1 slice.9
  134.9 0.1 reshape.46.pair_row_ref
  135.0 0.1 reshape.47.last_row_ref
  135.1 9.0 %table_grad.1 = f32[4096,512]{1,0:T(8,128)} custom-call(s32[1,1024]{1,0:T(1,128)S(1)} %reshape.46.pair_row_ref, s32[1,512]{1,0:T(1,128)S(1)} %reshape.47.last_row_ref, bf16[1024,1408]{1,0:T(8,128)(2,1)S(1)} %bitcast.20), custom_call_target="tpu_custom_call" | custom-call | flops 6442450944 | bytes 12582912 | tf_op jit(solution)/shard_map/table_grad/pallas_call | solution.py:464
  144.1 10.4 %all-to-all-done.3 = bf16[64,16,640]{2,1,0:T(8,128)(2,1)} async-done(((bf16[64,16,640]{2,1,0:T(8,128)(2,1)}), bf16[64,16,640]{2,1,0:T(8,128)(2,1)}, u32[]{:S(2)}, u32[]{:S(2)}) %all-to-all-start.3) | async-done | bytes 1310752 | tf_op jit(solution)/shard_map/all_to_all | solution.py:519
  154.5 2.5 %collective-permute-start.1 = (bf16[1024,640]{1,0:T(8,128)(2,1)}, bf16[1024,640]{1,0:T(8,128)(2,1)S(1)}, u32[]{:S(2)}, u32[]{:S(2)}) collective-permute-start(bf16[1024,640]{1,0:T(8,128)(2,1)} %bitcast.11), channel_id=1, source_target_pairs={{0,1},{1,0},{2,3},{3,2},{4,5},{5,4},{6,7},{7,6},{8,9},{9,8},{10,11... | collective-permute-start | bytes 3932168 | tf_op jit(solution)/shard_map/ppermute | solution.py:543
  157.1 2.7 %finish0.1 = (f32[2,16,2,8,2048]{4,3,2,1,0:T(8,128)}, f32[2,16,2,8,512]{4,3,2,1,0:T(8,128)}) custom-call(s32[1]{0:T(128)} %bitcast.half_ref.core_ref, bf16[4,16,16,640]{3,2,1,0:T(8,128)(2,1)} %bitcast.13.in_ref), custom_call_target="tpu_custom_call" | custom-call | flops 1000000 | bytes 4194304 | tf_op jit(solution)/shard_map/finish0/pallas_call | solution.py:499
  159.7 0.2 collective-permute-done.1
  159.9 1.7 %finish2.1 = (f32[2,16,2,8,2048]{4,3,2,1,0:T(8,128)}, f32[2,16,2,8,512]{4,3,2,1,0:T(8,128)}) custom-call(s32[1]{0:T(128)S(6)} %sub.3.core_ref, bf16[4,16,16,640]{3,2,1,0:T(8,128)(2,1)S(1)} %bitcast.23, f32[2,16,2,8,2048]{4,3,2,1,0:T(8,128)} %get-tuple-element.24.rest_0_, ...), custom_call_target="tpu_custom_call", output_to_operand_aliasing={{0}: (2, {}), {1}: (3, {})} | custom-call | flops 1000000 | bytes 4194304 | tf_op jit(solution)/shard_map/finish2/pallas_call | solution.py:499
Async XLA Ops:
  0.6 0.7 copy-start.1
  1.3 0.7 copy-start.2
  31.5 29.4 %copy-start.3 = (bf16[3,256,512]{2,1,0:T(8,128)(2,1)S(1)}, bf16[3,256,512]{2,1,0:T(8,128)(2,1)}, u32[]{:S(2)}) copy-start(bf16[3,256,512]{2,1,0:T(8,128)(2,1)} %cot_hbm.1) | copy-start | bytes 2359300
  31.5 29.4 %copy-start.4 = (bf16[512,512]{1,0:T(8,128)(2,1)S(1)}, bf16[512,512]{1,0:T(8,128)(2,1)}, u32[]{:S(2)}) copy-start(bf16[512,512]{1,0:T(8,128)(2,1)} %w_out_hbm.1) | copy-start | bytes 1572868
  31.5 29.4 %copy-start.5 = (s32[3,1,4]{2,1,0:T(1,128)S(1)}, s32[3,1,4]{2,1,0:T(1,128)}, u32[]{:S(2)}) copy-start(s32[3,1,4]{2,1,0:T(1,128)} %lengths_ref.1) | copy-start | bytes 148
  31.5 29.3 %all-to-all-start.1 = ((bf16[128,8,768]{2,1,0:T(8,128)(2,1)}), bf16[128,8,768]{2,1,0:T(8,128)(2,1)S(1)}, u32[]{:S(2)}, u32[]{:S(2)}) async-start(bf16[128,8,768]{2,1,0:T(8,128)(2,1)} %bitcast.28), calls=%async_computation.1 | async-start | bytes 3145728 | tf_op jit(solution)/shard_map/all_to_all | solution.py:519
  81.1 4.0 %collective-permute-start = (bf16[1024,640]{1,0:T(8,128)(2,1)S(1)}, bf16[1024,640]{1,0:T(8,128)(2,1)S(1)}, u32[]{:S(2)}, u32[]{:S(2)}) collective-permute-start(bf16[1024,640]{1,0:T(8,128)(2,1)S(1)} %bitcast.26), channel_id=1, source_target_pairs={{0,1},{1,0},{2,3},{3,2},{4,5},{5,4},{6,7},{7,6},{8,9},{9,8},{10,11... | collective-permute-start | bytes 3932168 | tf_op jit(solution)/shard_map/ppermute | solution.py:537
  128.1 1.1 copy-start
  129.2 5.6 %copy-start.6 = (s32[128,1,128]{2,1,0:T(1,128)S(1)}, s32[128,1,128]{2,1,0:T(1,128)}, u32[]{:S(2)}) copy-start(s32[128,1,128]{2,1,0:T(1,128)} %all_to_all.45) | copy-start | bytes 196612
  129.2 25.4 %all-to-all-start.3 = ((bf16[64,16,640]{2,1,0:T(8,128)(2,1)}), bf16[64,16,640]{2,1,0:T(8,128)(2,1)}, u32[]{:S(2)}, u32[]{:S(2)}) async-start(bf16[64,16,640]{2,1,0:T(8,128)(2,1)} %bitcast.21), calls=%async_computation.3 | async-start | bytes 2621440 | tf_op jit(solution)/shard_map/all_to_all | solution.py:519
  154.5 5.4 %collective-permute-start.1 = (bf16[1024,640]{1,0:T(8,128)(2,1)}, bf16[1024,640]{1,0:T(8,128)(2,1)S(1)}, u32[]{:S(2)}, u32[]{:S(2)}) collective-permute-start(bf16[1024,640]{1,0:T(8,128)(2,1)} %bitcast.11), channel_id=1, source_target_pairs={{0,1},{1,0},{2,3},{3,2},{4,5},{5,4},{6,7},{7,6},{8,9},{9,8},{10,11... | collective-permute-start | bytes 3932168 | tf_op jit(solution)/shard_map/ppermute | solution.py:543
